TPU v7x, 256 devices: a whole 4x4x8 slice. The times are simulated.
256 devices in a mesh: chan: 8 (over x, y_lo), row: 32 (over z, y_hi, core).
Axes of the slice: x: 4, y: 4 (y_hi: 2, y_lo: 2; y = y_hi * 2 + y_lo), z: 8, core: 2. Of those that a mesh axis runs over, the one named last changes fastest.
Arguments:
- pair: bfloat16 [2048, 2048, 128], P(('row', 'chan')), may hold values from -6 to 6
- pair_mask: int32 [2048, 2048], P(('row', 'chan')), may hold values 0 or 1
- in_gain: float32 [128], replicated, may hold values from 0.1 to 1.9
- in_bias: float32 [128], replicated, may hold values from -3 to 3
- w_value: bfloat16 [128, 256], replicated, may hold values from -0.5 to 0.5
- w_gate: bfloat16 [128, 256], replicated, may hold values from -0.5 to 0.5
- out_gate_w: bfloat16 [128, 128], replicated, may hold values from -0.5 to 0.5
- out_gain: float32 [128], replicated, may hold values from 0.1 to 1.9
- out_bias: float32 [128], replicated, may hold values from -3 to 3
- w_out: bfloat16 [128, 128], replicated, may hold values from -0.5 to 0.5
Outputs:
- update: bfloat16 [2048, 256, 128], P(('row', 'chan'))
All inputs are finite; a program needn't handle non-finite values. No bound on the sum of `pair_mask` on one device may be relied on, other than what follows from the above.
Results may differ from a plain program's by a relative error of at most 0.017.
Values may be sent and summed in bfloat16 or wider, within the bound.
No kernel may reach another device: no remote copies, remote signals or barrier semaphores. Data moves between devices by JAX's collectives and lax.ppermute only.
A program may use at most 128 MiB of HBM per device.

v0:
```python
import jax
import jax.numpy as jnp
from jax import lax
from jax.sharding import PartitionSpec as P

STEPS = 4


eps_norm = 1e-05


def passed_along(value, axis, by):
    count = lax.axis_size(axis)
    return lax.ppermute(value, axis, [(i, (i + by) % count) for i in range(count)])


def normalize(values, gain, bias, axis):
    average = jnp.mean(values, axis=axis, keepdims=True)
    centred = values - average
    variance = jnp.mean(centred * centred, axis=axis, keepdims=True)
    return centred * lax.rsqrt(variance + eps_norm) * gain + bias


def on_device(
    pair, pair_mask, in_gain, in_bias, w_value, w_gate, out_gate_w, out_gain, out_bias, w_out
):
    rows_here = pair.shape[0]
    token_count = pair.shape[1]
    groups = lax.axis_size("chan")
    channel_count = w_out.shape[0]
    block_rows = rows_here * groups
    window = STEPS * block_rows
    normed = normalize(pair.astype(jnp.float32), in_gain, in_bias, -1).astype(jnp.bfloat16)
    values = jnp.einsum("rlc,cd->rdl", normed, w_value, preferred_element_type=jnp.float32)
    gate_pre = jnp.einsum("rlc,cd->rdl", normed, w_gate, preferred_element_type=jnp.float32)
    mask_rows = pair_mask.astype(jnp.float32)[:, None, :]
    mixed_ab = (jax.nn.sigmoid(gate_pre) * values * mask_rows).astype(jnp.bfloat16)
    mixed_ab = mixed_ab.reshape(rows_here, 2, channel_count, token_count)
    pieces = lax.all_to_all(mixed_ab, "chan", split_axis=2, concat_axis=0, tiled=True)
    left_rows = pieces[:, 0]
    right_rows = pieces[:, 1]

    def contract(panel_rows):
        return lax.dot_general(
            left_rows, panel_rows, (((2,), (2,)), ((1,), (1,))), preferred_element_type=jnp.float32
        )

    products = [contract(right_rows)]
    current = right_rows
    for offset in range(1, STEPS):
        current = passed_along(current, "row", -1)
        products.append(contract(current))
    triangle = jnp.concatenate(products, axis=2)
    row_index = lax.axis_index("row")
    extended = jnp.concatenate([normed, normed[:, :window]], 1)
    window_rows = lax.dynamic_slice_in_dim(extended, row_index * block_rows, window, 1)
    out_gate = jax.nn.sigmoid(
        jnp.einsum("rjc,co->rjo", window_rows, out_gate_w, preferred_element_type=jnp.float32)
    )
    gathered = lax.all_to_all(triangle, "chan", split_axis=1, concat_axis=0, tiled=True)
    scaled = normalize(gathered, out_gain[:, None, None], out_bias[:, None, None], 0).astype(
        jnp.bfloat16
    )
    projected = jnp.einsum("krm,ko->rmo", scaled, w_out, preferred_element_type=jnp.float32)
    return (projected * out_gate).astype(jnp.bfloat16)


def solution(mesh):
    placed = (
        P(("row", "chan"), None, None),
        P(("row", "chan"), None),
        P(),
        P(),
        P(),
        P(),
        P(),
        P(),
        P(),
        P(),
    )
    return jax.shard_map(
        on_device,
        mesh=mesh,
        in_specs=placed,
        out_specs=P(("row", "chan"), None, None),
        check_vma=False,
    )
```

profile of v0, /device:TPU:8, one launch (start us, length us, event | category | flops | bytes accessed | tf_op | source)
XLA Modules:
  0.0 339.6 jit_solution(12224154154090453892)
XLA Ops:
  0.0 0.0 copy-start
  0.0 0.0 copy-start.9
  0.0 0.0 copy-start.8
  0.0 3.5 %convert_reduce_fusion = f32[8,2048]{1,0:T(8,128)S(1)} fusion(bf16[8,2048,128]{2,1,0:T(8,128)(2,1)} %param.10), kind=kLoop, calls=%fused_computation.2 | loop fusion | flops 4177920 | bytes 4259840 | tf_op jit(solution)/shard_map/reduce_sum | solution.py:18
  3.6 6.0 %fusion.2 = f32[8,2048]{1,0:T(8,128)S(1)} fusion(bf16[8,2048,128]{2,1,0:T(8,128)(2,1)} %param.10, f32[8,2048]{1,0:T(8,128)S(1)} %broadcast_multiply_fusion), kind=kLoop, calls=%fused_computation.5 | loop fusion | flops 8372224 | bytes 4325376 | tf_op jit(solution)/shard_map/reduce_sum | solution.py:20
  9.6 0.0 copy-done.5
  9.6 0.0 copy-done.3
  9.6 0.0 copy-done.9
  9.6 0.0 copy-done.8
  9.7 5.0 %fusion.5 = bf16[8,2048,128]{2,1,0:T(8,128)(2,1)S(1)} fusion(bf16[8,2048,128]{2,1,0:T(8,128)(2,1)S(1)} %copy-done.3, f32[128]{0:T(128)S(1)} %copy-done.8, f32[128]{0:T(128)S(1)} %copy-done.9, f32[8,2048]{1,0:T(8,128)S(1)} %add_rsqrt_fusion, f32[8,2048]{1,0:T(8,128)S(1)} %broadcast_multiply_fusion), kind=kLoop, calls=%fused_computation.8 | loop fusion | flops 12582912 | bytes 8520704 | tf_op jit(solution)/shard_map/convert_element_type | solution.py:33
  14.6 0.0 copy-done
  14.6 0.0 copy-start.2
  14.7 0.0 copy-start.12
  14.7 8.1 %fusion.26 = f32[8,2048,256]{1,2,0:T(8,128)} fusion(bf16[8,2048,128]{2,1,0:T(8,128)(2,1)S(1)} %fusion.5, bf16[128,256]{1,0:T(8,128)(2,1)S(1)} %copy-done), kind=kOutput, calls=%fused_computation.38 | convolution fusion | flops 1073741824 | bytes 21037056 | tf_op jit(solution)/shard_map/rlc,cd->rdl/dot_general | solution.py:35
  22.8 0.0 copy-done.2
  22.8 0.0 copy-done.12
  22.8 8.7 %multiply_convert_fusion = bf16[8,2048,256]{1,2,0:T(8,128)(2,1)S(1)} fusion(f32[8,2048,256]{1,2,0:T(8,128)} %fusion.26, f32[8,2048]{1,0:T(8,128)S(1)} %convert_element_type.20, bf16[8,2048,128]{2,1,0:T(8,128)(2,1)S(1)} %fusion.5, bf16[128,256]{1,0:T(8,128)(2,1)S(1)} %copy-done.12), kind=kOutput, calls=%fused_computation | convolution fusion | flops 1098907648 | bytes 29491200 | tf_op jit(solution)/shard_map/rlc,cd->rdl/dot_general | solution.py:34
  31.4 15.7 %copy.28 = bf16[8,2,128,2048]{3,1,0,2:T(2,128)(2,1)S(1)} copy(bf16[8,2,128,2048]{3,2,1,0:T(8,128)(2,1)S(1)} %bitcast.62) | data formatting | bytes 16777216 | tf_op jit(solution)/shard_map/reshape | solution.py:38
  47.1 100.2 %all_to_all.36 = bf16[8,2,128,2048]{3,1,0,2:T(2,128)(2,1)} all-to-all(bf16[8,2,128,2048]{3,1,0,2:T(2,128)(2,1)S(1)} %copy.28), channel_id=1, replica_groups=mesh['chan'=8,'row'=32] {'chan'}, dimensions={2} | all-to-all | bytes 16777216 | tf_op jit(solution)/shard_map/all_to_all | solution.py:39
  147.3 10.5 %copy.44 = bf16[8,2,8,16,2048]{4,0,2,3,1:T(8,128)(2,1)} copy(bf16[8,2,8,16,2048]{4,1,0,3,2:T(2,128)(2,1)} %bitcast.55) | data formatting | bytes 16777216 | tf_op jit(solution)/shard_map/all_to_all | solution.py:39
  157.8 2.9 slice_bitcast_fusion
  160.7 5.9 %collective-permute-start = (bf16[64,16,2048]{2,0,1:T(8,128)(2,1)S(1)}, bf16[64,16,2048]{2,0,1:T(8,128)(2,1)S(1)}, u32[]{:S(2)}, u32[]{:S(2)}) collective-permute-start(bf16[64,16,2048]{2,0,1:T(8,128)(2,1)S(1)} %slice_bitcast_fusion), channel_id=1, source_target_pairs={{0,31},{1,0},{2,1},{3,2},{4,3},{5,4},{6,5},{7,6},{8,7},{9,8},{10,9... | collective-permute-start | bytes 12582920 | tf_op jit(solution)/shard_map/ppermute | solution.py:14
  166.6 46.0 %collective-permute-done = bf16[64,16,2048]{2,0,1:T(8,128)(2,1)S(1)} collective-permute-done((bf16[64,16,2048]{2,0,1:T(8,128)(2,1)S(1)}, bf16[64,16,2048]{2,0,1:T(8,128)(2,1)S(1)}, u32[]{:S(2)}, u32[]{:S(2)}) %collective-permute-start) | collective-permute-done | bytes 4194336 | tf_op jit(solution)/shard_map/ppermute | solution.py:14
  212.6 5.5 %collective-permute-start.1 = (bf16[64,16,2048]{2,0,1:T(8,128)(2,1)S(1)}, bf16[64,16,2048]{2,0,1:T(8,128)(2,1)S(1)}, u32[]{:S(2)}, u32[]{:S(2)}) collective-permute-start(bf16[64,16,2048]{2,0,1:T(8,128)(2,1)S(1)} %collective-permute-done), channel_id=1, source_target_pairs={{0,31},{1,0},{2,1},{3,2},{4,3},{5,4},{6,5},{7,6},{8,7},{9,8},{10,9... | collective-permute-start | bytes 12582920 | tf_op jit(solution)/shard_map/ppermute | solution.py:14
  218.1 46.0 %collective-permute-done.1 = bf16[64,16,2048]{2,0,1:T(8,128)(2,1)S(1)} collective-permute-done((bf16[64,16,2048]{2,0,1:T(8,128)(2,1)S(1)}, bf16[64,16,2048]{2,0,1:T(8,128)(2,1)S(1)}, u32[]{:S(2)}, u32[]{:S(2)}) %collective-permute-start.1) | collective-permute-done | bytes 4194336 | tf_op jit(solution)/shard_map/ppermute | solution.py:14
  264.2 5.5 %collective-permute-start.2 = (bf16[64,16,2048]{2,0,1:T(8,128)(2,1)S(1)}, bf16[64,16,2048]{2,0,1:T(8,128)(2,1)S(1)}, u32[]{:S(2)}, u32[]{:S(2)}) collective-permute-start(bf16[64,16,2048]{2,0,1:T(8,128)(2,1)S(1)} %collective-permute-done.1), channel_id=1, source_target_pairs={{0,31},{1,0},{2,1},{3,2},{4,3},{5,4},{6,5},{7,6},{8,7},{9,8},{10,9... | collective-permute-start | bytes 12582920 | tf_op jit(solution)/shard_map/ppermute | solution.py:14
  269.7 0.0 copy-done.4
  269.7 1.2 fusion.9
  270.9 1.2 fusion.8
  272.2 1.2 fusion.7
  273.4 42.3 %collective-permute-done.2 = bf16[64,16,2048]{2,0,1:T(8,128)(2,1)S(1)} collective-permute-done((bf16[64,16,2048]{2,0,1:T(8,128)(2,1)S(1)}, bf16[64,16,2048]{2,0,1:T(8,128)(2,1)S(1)}, u32[]{:S(2)}, u32[]{:S(2)}) %collective-permute-start.2) | collective-permute-done | bytes 4194336 | tf_op jit(solution)/shard_map/ppermute | solution.py:14
  315.7 1.2 fusion.6
  316.9 0.0 copy-start.10
  317.0 0.0 copy-start.11
  317.0 0.0 copy-start.7
  317.0 0.0 slice-start
  317.0 0.0 copy-start.6
  317.0 0.5 pad_maximum_fusion
  317.5 0.0 copy-start.1
  317.5 1.6 copy.30
  319.1 4.9 %all-to-all-start.1 = ((f32[16,64,256]{2,0,1:T(8,128)}), f32[16,64,256]{2,0,1:T(8,128)S(1)}, u32[]{:S(2)}, u32[]{:S(2)}) async-start(f32[16,64,256]{2,0,1:T(8,128)} %copy.30), calls=%async_computation.1 | async-start | bytes 2097152 | tf_op jit(solution)/shard_map/all_to_all | solution.py:60
  323.9 10.8 %all-to-all-done.1 = f32[16,64,256]{2,0,1:T(8,128)S(1)} async-done(((f32[16,64,256]{2,0,1:T(8,128)}), f32[16,64,256]{2,0,1:T(8,128)S(1)}, u32[]{:S(2)}, u32[]{:S(2)}) %all-to-all-start.1) | async-done | bytes 1048608 | tf_op jit(solution)/shard_map/all_to_all | solution.py:60
  334.8 0.5 bitcast_reduce_fusion
  335.3 0.6 fusion.16
  335.9 0.6 copy.32
  336.5 0.3 fusion.20
  336.9 0.3 fusion.23
  337.2 2.4 fusion.14
  (14 shorter events, 0.1 us)
Async XLA Ops:
  0.0 14.6 %copy-start = (bf16[128,256]{1,0:T(8,128)(2,1)S(1)}, bf16[128,256]{1,0:T(8,128)(2,1)}, u32[]{:S(2)}) copy-start(bf16[128,256]{1,0:T(8,128)(2,1)} %param.15) | copy-start | bytes 196612
  0.0 9.6 %copy-start.3 = (bf16[8,2048,128]{2,1,0:T(8,128)(2,1)S(1)}, bf16[8,2048,128]{2,1,0:T(8,128)(2,1)}, u32[]{:S(2)}) copy-start(bf16[8,2048,128]{2,1,0:T(8,128)(2,1)} %param.10) | copy-start | bytes 12582916
  0.0 9.6 %copy-start.5 = (s32[8,2048]{1,0:T(8,128)S(1)}, s32[8,2048]{1,0:T(8,128)}, u32[]{:S(2)}) copy-start(s32[8,2048]{1,0:T(8,128)} %param.11) | copy-start | bytes 196612
  0.0 9.6 %copy-start.9 = (f32[128]{0:T(128)S(1)}, f32[128]{0:T(128)}, u32[]{:S(2)}) copy-start(f32[128]{0:T(128)} %param.12) | copy-start | bytes 1540
  0.0 9.6 %copy-start.8 = (f32[128]{0:T(128)S(1)}, f32[128]{0:T(128)}, u32[]{:S(2)}) copy-start(f32[128]{0:T(128)} %param.13) | copy-start | bytes 1540
  14.6 8.1 %copy-start.2 = (bf16[8,2048,128]{2,1,0:T(8,128)(2,1)}, bf16[8,2048,128]{2,1,0:T(8,128)(2,1)S(1)}, u32[]{:S(2)}) copy-start(bf16[8,2048,128]{2,1,0:T(8,128)(2,1)S(1)} %fusion.5) | copy-start | bytes 12582916
  14.7 8.1 %copy-start.12 = (bf16[128,256]{1,0:T(8,128)(2,1)S(1)}, bf16[128,256]{1,0:T(8,128)(2,1)}, u32[]{:S(2)}) copy-start(bf16[128,256]{1,0:T(8,128)(2,1)} %param.14) | copy-start | bytes 196612
  157.8 111.9 %copy-start.4 = (bf16[8,2,8,16,2048]{4,0,2,3,1:T(8,128)(2,1)S(1)}, bf16[8,2,8,16,2048]{4,0,2,3,1:T(8,128)(2,1)}, u32[]{:S(2)}) copy-start(bf16[8,2,8,16,2048]{4,0,2,3,1:T(8,128)(2,1)} %copy.44) | copy-start | bytes 25165828
  160.7 51.9 %collective-permute-start = (bf16[64,16,2048]{2,0,1:T(8,128)(2,1)S(1)}, bf16[64,16,2048]{2,0,1:T(8,128)(2,1)S(1)}, u32[]{:S(2)}, u32[]{:S(2)}) collective-permute-start(bf16[64,16,2048]{2,0,1:T(8,128)(2,1)S(1)} %slice_bitcast_fusion), channel_id=1, source_target_pairs={{0,31},{1,0},{2,1},{3,2},{4,3},{5,4},{6,5},{7,6},{8,7},{9,8},{10,9... | collective-permute-start | bytes 12582920 | tf_op jit(solution)/shard_map/ppermute | solution.py:14
  212.6 51.5 %collective-permute-start.1 = (bf16[64,16,2048]{2,0,1:T(8,128)(2,1)S(1)}, bf16[64,16,2048]{2,0,1:T(8,128)(2,1)S(1)}, u32[]{:S(2)}, u32[]{:S(2)}) collective-permute-start(bf16[64,16,2048]{2,0,1:T(8,128)(2,1)S(1)} %collective-permute-done), channel_id=1, source_target_pairs={{0,31},{1,0},{2,1},{3,2},{4,3},{5,4},{6,5},{7,6},{8,7},{9,8},{10,9... | collective-permute-start | bytes 12582920 | tf_op jit(solution)/shard_map/ppermute | solution.py:14
  264.2 51.5 %collective-permute-start.2 = (bf16[64,16,2048]{2,0,1:T(8,128)(2,1)S(1)}, bf16[64,16,2048]{2,0,1:T(8,128)(2,1)S(1)}, u32[]{:S(2)}, u32[]{:S(2)}) collective-permute-start(bf16[64,16,2048]{2,0,1:T(8,128)(2,1)S(1)} %collective-permute-done.1), channel_id=1, source_target_pairs={{0,31},{1,0},{2,1},{3,2},{4,3},{5,4},{6,5},{7,6},{8,7},{9,8},{10,9... | collective-permute-start | bytes 12582920 | tf_op jit(solution)/shard_map/ppermute | solution.py:14
  316.9 19.6 %copy-start.10 = (f32[128]{0:T(128)S(1)}, f32[128]{0:T(128)}, u32[]{:S(2)}) copy-start(f32[128]{0:T(128)} %param.18) | copy-start | bytes 1540
  317.0 19.6 %copy-start.11 = (f32[128]{0:T(128)S(1)}, f32[128]{0:T(128)}, u32[]{:S(2)}) copy-start(f32[128]{0:T(128)} %param.17) | copy-start | bytes 1540
  317.0 19.9 %copy-start.7 = (bf16[128,128]{1,0:T(8,128)(2,1)S(1)}, bf16[128,128]{1,0:T(8,128)(2,1)}, u32[]{:S(2)}) copy-start(bf16[128,128]{1,0:T(8,128)(2,1)} %param.19) | copy-start | bytes 98308
  317.0 20.2 %slice-start = ((bf16[8,2048,128]{2,1,0:T(8,128)(2,1)}), bf16[8,256,128]{2,1,0:T(8,128)(2,1)S(1)}, s32[]{:S(2)}) async-start(bf16[8,2048,128]{2,1,0:T(8,128)(2,1)} %copy-done.2), calls=%async_computation.2 | async-start | bytes 1048576 | tf_op jit(solution)/shard_map/slice | solution.py:55
  317.0 20.2 %copy-start.6 = (bf16[128,128]{1,0:T(8,128)(2,1)S(1)}, bf16[128,128]{1,0:T(8,128)(2,1)}, u32[]{:S(2)}) copy-start(bf16[128,128]{1,0:T(8,128)(2,1)} %param.16) | copy-start | bytes 98308
  317.5 22.2 %copy-start.1 = (bf16[128,256]{1,0:T(8,128)(2,1)S(1)}, bf16[128,256]{1,0:T(8,128)(2,1)}, u32[]{:S(2)}) copy-start(bf16[128,256]{1,0:T(8,128)(2,1)} %param.15) | copy-start | bytes 196612
  319.1 15.7 %all-to-all-start.1 = ((f32[16,64,256]{2,0,1:T(8,128)}), f32[16,64,256]{2,0,1:T(8,128)S(1)}, u32[]{:S(2)}, u32[]{:S(2)}) async-start(f32[16,64,256]{2,0,1:T(8,128)} %copy.30), calls=%async_computation.1 | async-start | bytes 2097152 | tf_op jit(solution)/shard_map/all_to_all | solution.py:60
where the time goes:
time: 340 us
  waiting for transfers between devices  145 us (43%)
  blocking collectives  100 us (29%)
  local copies, waits for them, and re-layouts  31.3 us (9%)
  matrix products  24.4 us (7%)
  starting transfers between devices  21.8 us (6%)
  other arithmetic  16.4 us (5%)
    ppermute x3, waiting for transfers between devices, passed_along(): lax.ppermute(value, axis, [(i, (i + by) % count) for i in range(count)])  134 us
    all_to_all x1, blocking collectives, on_device(): lax.all_to_all(mixed_ab, 'chan', split_axis=2, concat_axis=0, tiled=True)  100 us
    ppermute x3, starting transfers between devices, passed_along(): lax.ppermute(value, axis, [(i, (i + by) % count) for i in range(count)])  16.9 us
    reshape x1, local copies, waits for them, and re-layouts, on_device(): mixed_ab = mixed_ab.reshape(rows_here, 2, channel_count, token_count)  15.7 us
    all_to_all x1, waiting for transfers between devices, on_device(): lax.all_to_all(triangle, 'chan', split_axis=1, concat_axis=0, tiled=True)  10.8 us
    all_to_all x1, local copies, waits for them, and re-layouts, on_device(): lax.all_to_all(mixed_ab, 'chan', split_axis=2, concat_axis=0, tiled=True)  10.5 us
    dot_general x1, matrix products, on_device(): jnp.einsum('rlc,cd->rdl', normed, w_value, preferred_element_type=jnp.flo...  8.66 us
    dot_general x1, matrix products, on_device(): jnp.einsum('rlc,cd->rdl', normed, w_gate, preferred_element_type=jnp.floa...  8.11 us
  transfers between devices with their start and end apart: 4, of which 4 were waited for; matrix products, arithmetic and copies ran while one was open for 1% of the time, Pallas kernels for 0%

commit v1 on v0

v1 whole, which is shorter than its diff:
```python
import functools

import jax
import jax.numpy as jnp
from jax import lax
from jax.experimental import pallas as pl
from jax.experimental.pallas import tpu as pltpu
from jax.sharding import Mesh, PartitionSpec as P

EPS = 1e-05
BLOCK = 64
STEPS = 4
SUB = 8
PLANE = ("yhi", "core", "x", "ylo")
PARTS = 32
OWN = 4
HALVES = ((0, 1024), (1024, 1024))
F32 = jnp.float32
BF16 = jnp.bfloat16
VMEM_LIMIT = 56 * 1024 * 1024


def dot(a, b, dims):
    return lax.dot_general(a, b, (dims, ((), ())), preferred_element_type=F32)


def columns(row):
    return jnp.transpose(jnp.broadcast_to(row, (128, 128)))


def across(block, width):
    return jnp.concatenate([block] * (width // 128), axis=1)


def project_kernel(pair_ref, mask_ref, gain_ref, bias_ref, value_ref, gate_ref, out_ref, mixed):
    width = pair_ref.shape[1]
    lane = lax.broadcasted_iota(jnp.int32, (128, 128), 0)
    sub = lax.broadcasted_iota(jnp.int32, (128, 128), 1)
    eye = jnp.where(lane == sub, 1.0, 0.0).astype(BF16)
    gain = across(columns(gain_ref[...]), width)
    bias = across(columns(bias_ref[...]), width)
    value_t = jnp.transpose(value_ref[...].astype(F32)).astype(BF16)
    gate_t = jnp.transpose(gate_ref[...].astype(F32) * 0.5).astype(BF16)
    weight = jnp.concatenate([value_t, gate_t], axis=0)
    half_mask = mask_ref[...].astype(F32) * 0.5
    for row in range(SUB):
        turned = dot(eye, pair_ref[row], ((1,), (1,)))
        centred = turned - jnp.sum(turned, axis=0, keepdims=True) * (1.0 / 128)
        variance = jnp.sum(centred * centred, axis=0, keepdims=True) * (1.0 / 128)
        normed = (centred * lax.rsqrt(variance + EPS) * gain + bias).astype(BF16)
        both = dot(weight, normed, ((1,), (0,)))
        half = both[:128] * half_mask[row : row + 1]
        result = half + half * jnp.tanh(both[128:])
        for tile in range(width // 128):
            first = (tile * SUB + row) * 128
            mixed[first : first + 128, :] = result[:, tile * 128 : (tile + 1) * 128]
    for tile in range(width // 128):
        for part in range(PARTS):
            first = tile * SUB * 128 + part * OWN
            pieces = [mixed[pl.ds(first + k, SUB, stride=128), :] for k in range(OWN)]
            out_ref[part, :, tile * 128 : (tile + 1) * 128] = jnp.concatenate(
                pieces, axis=0
            ).astype(BF16)


def project(pair, mask, gain, bias, w_value, w_gate, side, start, length):
    width = min(512, length)
    first = start // width
    whole = lambda i: (0, 0)
    column = lambda i: (0, side)
    tokens = SUB * length
    return pl.pallas_call(
        project_kernel,
        grid=(length // width,),
        in_specs=[
            pl.BlockSpec((SUB, width, 128), lambda i: (0, first + i, 0)),
            pl.BlockSpec((SUB, width), lambda i: (0, first + i)),
            pl.BlockSpec((1, 128), whole),
            pl.BlockSpec((1, 128), whole),
            pl.BlockSpec((128, 128), column),
            pl.BlockSpec((128, 128), column),
        ],
        out_specs=pl.BlockSpec((PARTS, OWN * SUB, width), lambda i: (0, 0, i)),
        out_shape=jax.ShapeDtypeStruct((PARTS, OWN * SUB, length), BF16),
        scratch_shapes=[pltpu.VMEM((SUB * width, 128), F32)],
        compiler_params=pltpu.CompilerParams(vmem_limit_bytes=VMEM_LIMIT),
        cost_estimate=pl.CostEstimate(
            flops=tokens * 128 * 384 * 2, bytes_accessed=tokens * 512, transcendentals=tokens * 128
        ),
        name="project",
    )(pair, mask, gain, bias, w_value, w_gate)


def rows_of(ref, pair_of_channels):
    parts, _, width = ref.shape
    both = ref[:, pair_of_channels * 16 : (pair_of_channels + 1) * 16, :].astype(F32)
    return [
        both[:, k * SUB : (k + 1) * SUB, :].reshape(parts * SUB, width).astype(BF16)
        for k in range(2)
    ]


def contract_kernel(last, left_ref, right_ref, next_ref, *rest):
    if last:
        before_ref, out_ref, total = rest
    else:
        out_ref, total = rest
    step = pl.program_id(0)

    @pl.when(step == 0)
    def _():
        total[...] = before_ref[...] if last else jnp.zeros_like(total)

    for pair_of_channels in range(OWN // 2):
        left = rows_of(left_ref, pair_of_channels)
        right = rows_of(right_ref, pair_of_channels)
        after = rows_of(next_ref, pair_of_channels)
        for k in range(2):
            window = jnp.concatenate([right[k], after[k]], axis=0)
            total[pair_of_channels * 2 + k] += dot(left[k], window, ((1,), (1,)))

    @pl.when(step == pl.num_programs(0) - 1)
    def _():
        if not last:
            out_ref[...] = total[...]
        else:
            groups = BLOCK // SUB
            for block in range(STEPS):
                for pair_of_channels in range(OWN // 2):
                    band = [
                        total[
                            pair_of_channels * 2 + k,
                            block * BLOCK : (block + 1) * BLOCK,
                            block * BLOCK : (block + STEPS) * BLOCK,
                        ].reshape(groups, SUB, STEPS * BLOCK)
                        for k in range(2)
                    ]
                    out_ref[
                        block * groups : (block + 1) * groups,
                        pair_of_channels * 16 : (pair_of_channels + 1) * 16,
                        :,
                    ] = jnp.concatenate(band, axis=1).astype(BF16)


def contract(left, right, after, before):
    length = left.shape[2]
    width = 256
    last = before is not None
    shape = (OWN, BLOCK * STEPS, BLOCK * (2 * STEPS - 1))
    part = lambda i: (0, 0, i)
    whole = lambda i: (0, 0, 0)
    in_specs = [pl.BlockSpec(v.shape[:2] + (width,), part) for v in (left, right, after)]
    operands = [left, right, after]
    if last:
        in_specs.append(pl.BlockSpec(shape, whole))
        operands.append(before)
        out_shape = jax.ShapeDtypeStruct((PARTS, OWN * SUB, STEPS * BLOCK), BF16)
    else:
        out_shape = jax.ShapeDtypeStruct(shape, F32)
    return pl.pallas_call(
        functools.partial(contract_kernel, last),
        grid=(length // width,),
        in_specs=in_specs,
        out_specs=pl.BlockSpec(out_shape.shape, whole),
        out_shape=out_shape,
        scratch_shapes=[pltpu.VMEM(shape, F32)],
        compiler_params=pltpu.CompilerParams(vmem_limit_bytes=VMEM_LIMIT),
        cost_estimate=pl.CostEstimate(
            flops=2 * 4 * 256 * 448 * length, bytes_accessed=6 * 1024 * length, transcendentals=0
        ),
        name="contract",
    )(*operands)


def finish_kernel(triangle_ref, gate_ref, gain_ref, bias_ref, w_ref, out_ref, scaled):
    width = triangle_ref.shape[2]
    values = triangle_ref[...].astype(F32).reshape(128, SUB, width)
    centred = values - jnp.sum(values, axis=0, keepdims=True) * (1.0 / 128)
    variance = jnp.sum(centred * centred, axis=0, keepdims=True) * (1.0 / 128)
    even = (centred * lax.rsqrt(variance + EPS)).reshape(128 * SUB, width)
    tiles = width // 128
    for tile in range(tiles):
        scaled[tile * SUB * 128 : (tile + 1) * SUB * 128, :] = even[:, tile * 128 : (tile + 1) * 128]
    gain = across(columns(gain_ref[...]), width)
    bias = across(columns(bias_ref[...]), width)
    for row in range(SUB):
        mine = [scaled[pl.ds(tile * SUB * 128 + row, 128, stride=SUB), :] for tile in range(tiles)]
        held = (jnp.concatenate(mine, axis=1) * gain + bias).astype(BF16)
        projected = dot(held, w_ref[...], ((0,), (0,)))
        out_ref[row] = (projected * gate_ref[row]).astype(BF16)


def finish(triangle, gate, gain, bias, w_out):
    width = 256
    whole = lambda i: (0, 0)
    return pl.pallas_call(
        finish_kernel,
        grid=(STEPS * BLOCK // width,),
        in_specs=[
            pl.BlockSpec((PARTS, OWN * SUB, width), lambda i: (0, 0, i)),
            pl.BlockSpec((SUB, width, 128), lambda i: (0, i, 0)),
            pl.BlockSpec((1, 128), whole),
            pl.BlockSpec((1, 128), whole),
            pl.BlockSpec((128, 128), whole),
        ],
        out_specs=pl.BlockSpec((SUB, width, 128), lambda i: (0, i, 0)),
        out_shape=jax.ShapeDtypeStruct((SUB, STEPS * BLOCK, 128), BF16),
        scratch_shapes=[pltpu.VMEM((SUB * width, 128), F32)],
        compiler_params=pltpu.CompilerParams(vmem_limit_bytes=VMEM_LIMIT),
        cost_estimate=pl.CostEstimate(
            flops=SUB * 256 * 128 * 256, bytes_accessed=2 * 1024 * 1024, transcendentals=2048
        ),
        name="finish",
    )(triangle, gate, gain, bias, w_out)


def output_gate(pair, in_gain, in_bias, out_gate_w, block):
    blocks = pair.shape[1] // BLOCK
    window = jnp.concatenate(
        [
            lax.dynamic_slice_in_dim(pair, lax.rem(block + k, blocks) * BLOCK, BLOCK, 1)
            for k in range(STEPS)
        ],
        axis=1,
    ).astype(F32)
    centred = window - jnp.mean(window, axis=-1, keepdims=True)
    variance = jnp.mean(centred * centred, axis=-1, keepdims=True)
    normed = (centred * lax.rsqrt(variance + EPS) * in_gain + in_bias).astype(BF16)
    return jax.nn.sigmoid(dot(normed, out_gate_w, ((2,), (0,))))


def on_device(
    pair, pair_mask, in_gain, in_bias, w_value, w_gate, out_gate_w, out_gain, out_bias, w_out
):
    gain, bias = in_gain.reshape(1, 128), in_bias.reshape(1, 128)
    planes = lax.axis_size("z")
    to_before = [(i, (i - 1) % planes) for i in range(planes)]

    def operand(side, chunk):
        return project(pair, pair_mask, gain, bias, w_value, w_gate, side, *chunk)

    def spread(value):
        return lax.all_to_all(value, PLANE, 0, 0, tiled=True)

    rights = [spread(operand(1, chunk)) for chunk in HALVES]
    afters = [
        lax.ppermute(right[: (STEPS - 1) * BLOCK // SUB], "z", to_before) for right in rights
    ]
    lefts = [spread(operand(0, chunk)) for chunk in HALVES]
    block = lax.axis_index("z") * 4 + lax.axis_index("yhi") * 2 + lax.axis_index("core")
    gate = output_gate(pair, in_gain, in_bias, out_gate_w, block)
    total = contract(lefts[0], rights[0], afters[0], None)
    band = contract(lefts[1], rights[1], afters[1], total)
    triangle = spread(band)
    return finish(triangle, gate, out_gain.reshape(1, 128), out_bias.reshape(1, 128), w_out)


def solution(mesh):
    fine = Mesh(mesh.devices.reshape(4, 2, 8, 2, 2), ("x", "ylo", "z", "yhi", "core"))
    rows = ("z", "yhi", "core", "x", "ylo")
    placed = (P(rows, None, None), P(rows, None)) + (P(),) * 8
    return jax.shard_map(
        on_device,
        mesh=fine,
        in_specs=placed,
        out_specs=P(rows, None, None),
        check_vma=False,
    )
```

time: 340 us -> 225 us (0.66)
  blocking collectives: 100 us -> 0 us
  Pallas kernels: 0 us -> 57 us
  waiting for transfers between devices: 145 us -> 117 us
  local copies, waits for them, and re-layouts: 31.3 us -> 6.47 us
  matrix products: 24.4 us -> 1.79 us
  starting transfers between devices: 21.8 us -> 39.8 us
  other arithmetic: 16.4 us -> 0.86 us
    all_to_all x1 -> x0, blocking collectives: 100 us -> none  [on_device(): lax.all_to_all(mixed_ab, 'chan', split_axis=2, concat_axis=0, tiled=True)]
    ppermute x3 -> x2, waiting for transfers between devices: 134 us -> 56.8 us  [on_device(): lax.ppermute(right[:(STEPS - 1) * BLOCK // SUB], 'z', to_before)]
    pallas_call x0 -> x7, Pallas kernels: none -> 57 us  [the longest x4 42 us: project(): pl.pallas_call(project_kernel, grid=(length // width,), in_specs=[pl.Bloc...]
    all_to_all x1 -> x5, waiting for transfers between devices: 10.8 us -> 60.1 us  [spread(): return lax.all_to_all(value, PLANE, 0, 0, tiled=True)]
    all_to_all x1 -> x5, starting transfers between devices: 4.85 us -> 32.7 us  [spread(): return lax.all_to_all(value, PLANE, 0, 0, tiled=True)]
    dot_general x8 -> x1, matrix products: 24.4 us -> 1.79 us  [dot(): return lax.dot_general(a, b, (dims, ((), ())), preferred_element_type=F32)]
    reshape x1 -> x0, local copies, waits for them, and re-layouts: 15.7 us -> none  [on_device(): mixed_ab = mixed_ab.reshape(rows_here, 2, channel_count, token_count)]
    all_to_all x2 -> x0, local copies, waits for them, and re-layouts: 11.1 us -> none  [the longest x1 10.5 us: on_device(): lax.all_to_all(mixed_ab, 'chan', split_axis=2, concat_axis=0, tiled=True)]
  transfers between devices with their start and end apart: 4 -> 7, of which waited for: 4 -> 6; matrix products, arithmetic and copies ran while one was open for 1% -> 3% of each run, Pallas kernels for 0% -> 17%
where the time goes in v1:
time: 225 us; the launch traced here: 223 us
  waiting for transfers between devices  117 us (52%)
  Pallas kernels  57 us (25%)
  starting transfers between devices  39.8 us (18%)
  local copies, waits for them, and re-layouts  6.47 us (3%)
    all_to_all x5, waiting for transfers between devices, spread(): return lax.all_to_all(value, PLANE, 0, 0, tiled=True)  60.1 us
    ppermute x2, waiting for transfers between devices, on_device(): lax.ppermute(right[:(STEPS - 1) * BLOCK // SUB], 'z', to_before)  56.8 us
    pallas_call x4, Pallas kernels, project(): pl.pallas_call(project_kernel, grid=(length // width,), in_specs=[pl.Bloc...  42 us
    all_to_all x5, starting transfers between devices, spread(): return lax.all_to_all(value, PLANE, 0, 0, tiled=True)  32.7 us
    pallas_call x2, Pallas kernels, contract(): pl.pallas_call(functools.partial(contract_kernel, last), grid=(length //...  12 us
    ppermute x2, starting transfers between devices, on_device(): lax.ppermute(right[:(STEPS - 1) * BLOCK // SUB], 'z', to_before)  7.16 us
  transfers between devices with their start and end apart: 7, of which 6 were waited for; matrix products, arithmetic and copies ran while one was open for 3% of the time, Pallas kernels for 17%

profile of v1, /device:TPU:8, one launch (start us, length us, event | category | flops | bytes accessed | tf_op | source)
XLA Modules:
  0.0 223.0 jit_solution(17075103506226180965)
XLA Ops:
  0.0 0.0 copy-start
  0.0 10.4 %project.7 = bf16[32,32,1024]{2,1,0:T(8,128)(2,1)} custom-call(bf16[8,2048,128]{2,1,0:T(8,128)(2,1)} %pair_ref.7, s32[8,2048]{1,0:T(8,128)} %mask_ref.7, f32[1,128]{1,0:T(1,128)} %bitcast.7, f32[1,128]{1,0:T(1,128)} %bitcast.11, bf16[128,256]{1,0:T(8,128)(2,1)} %value_ref.7, bf16[128,256]{1,0:T(8,128)(2,1)} %gate_ref.7), custom_call_target="tpu_custom_call" | custom-call | flops 805306368 | bytes 4194304 | tf_op jit(solution)/shard_map/project/pallas_call | solution.py:72
  10.4 7.5 %all-to-all-start.3 = ((bf16[32,32,1024]{2,1,0:T(8,128)(2,1)}), bf16[32,32,1024]{2,1,0:T(8,128)(2,1)S(1)}, u32[]{:S(2)}, u32[]{:S(2)}) async-start(bf16[32,32,1024]{2,1,0:T(8,128)(2,1)} %project.7), calls=%async_computation.3 | async-start | bytes 4194304 | tf_op jit(solution)/shard_map/all_to_all | solution.py:243
  18.0 10.5 %project.6 = bf16[32,32,1024]{2,1,0:T(8,128)(2,1)} custom-call(bf16[8,2048,128]{2,1,0:T(8,128)(2,1)} %pair_ref.7, s32[8,2048]{1,0:T(8,128)} %mask_ref.7, f32[1,128]{1,0:T(1,128)} %bitcast.8, f32[1,128]{1,0:T(1,128)} %bitcast.12, bf16[128,256]{1,0:T(8,128)(2,1)} %value_ref.7, bf16[128,256]{1,0:T(8,128)(2,1)} %gate_ref.7), custom_call_target="tpu_custom_call" | custom-call | flops 805306368 | bytes 4194304 | tf_op jit(solution)/shard_map/project/pallas_call | solution.py:72
  28.5 17.1 %all-to-all-done.3.right_ref = bf16[32,32,1024]{2,1,0:T(8,128)(2,1)S(1)} async-done(((bf16[32,32,1024]{2,1,0:T(8,128)(2,1)}), bf16[32,32,1024]{2,1,0:T(8,128)(2,1)S(1)}, u32[]{:S(2)}, u32[]{:S(2)}) %all-to-all-start.3) | async-done | bytes 2097184 | tf_op jit(solution)/shard_map/all_to_all | solution.py:243
  45.6 0.0 copy-start.1
  45.6 5.9 %all-to-all-start.2 = ((bf16[32,32,1024]{2,1,0:T(8,128)(2,1)}), bf16[32,32,1024]{2,1,0:T(8,128)(2,1)}, u32[]{:S(2)}, u32[]{:S(2)}) async-start(bf16[32,32,1024]{2,1,0:T(8,128)(2,1)} %project.6), calls=%async_computation.2 | async-start | bytes 4194304 | tf_op jit(solution)/shard_map/all_to_all | solution.py:243
  51.6 10.5 %project.5 = bf16[32,32,1024]{2,1,0:T(8,128)(2,1)} custom-call(bf16[8,2048,128]{2,1,0:T(8,128)(2,1)} %pair_ref.7, s32[8,2048]{1,0:T(8,128)} %mask_ref.7, f32[1,128]{1,0:T(1,128)} %bitcast.9, f32[1,128]{1,0:T(1,128)} %bitcast.13, bf16[128,256]{1,0:T(8,128)(2,1)} %value_ref.7, bf16[128,256]{1,0:T(8,128)(2,1)} %gate_ref.7), custom_call_target="tpu_custom_call" | custom-call | flops 805306368 | bytes 4194304 | tf_op jit(solution)/shard_map/project/pallas_call | solution.py:72
  62.1 17.3 %all-to-all-done.2.left_ref = bf16[32,32,1024]{2,1,0:T(8,128)(2,1)} async-done(((bf16[32,32,1024]{2,1,0:T(8,128)(2,1)}), bf16[32,32,1024]{2,1,0:T(8,128)(2,1)}, u32[]{:S(2)}, u32[]{:S(2)}) %all-to-all-start.2) | async-done | bytes 2097184 | tf_op jit(solution)/shard_map/all_to_all | solution.py:243
  79.4 5.9 %all-to-all-start.1 = ((bf16[32,32,1024]{2,1,0:T(8,128)(2,1)}), bf16[32,32,1024]{2,1,0:T(8,128)(2,1)}, u32[]{:S(2)}, u32[]{:S(2)}) async-start(bf16[32,32,1024]{2,1,0:T(8,128)(2,1)} %project.5), calls=%async_computation.1 | async-start | bytes 4194304 | tf_op jit(solution)/shard_map/all_to_all | solution.py:243
  85.3 10.5 %project.4 = bf16[32,32,1024]{2,1,0:T(8,128)(2,1)} custom-call(bf16[8,2048,128]{2,1,0:T(8,128)(2,1)} %pair_ref.7, s32[8,2048]{1,0:T(8,128)} %mask_ref.7, f32[1,128]{1,0:T(1,128)} %bitcast.10, f32[1,128]{1,0:T(1,128)} %bitcast.14, bf16[128,256]{1,0:T(8,128)(2,1)} %value_ref.7, bf16[128,256]{1,0:T(8,128)(2,1)} %gate_ref.7), custom_call_target="tpu_custom_call" | custom-call | flops 805306368 | bytes 4194304 | tf_op jit(solution)/shard_map/project/pallas_call | solution.py:72
  95.7 17.4 %all-to-all-done.1.right_ref = bf16[32,32,1024]{2,1,0:T(8,128)(2,1)} async-done(((bf16[32,32,1024]{2,1,0:T(8,128)(2,1)}), bf16[32,32,1024]{2,1,0:T(8,128)(2,1)}, u32[]{:S(2)}, u32[]{:S(2)}) %all-to-all-start.1) | async-done | bytes 2097184 | tf_op jit(solution)/shard_map/all_to_all | solution.py:243
  113.1 5.9 %all-to-all-start = ((bf16[32,32,1024]{2,1,0:T(8,128)(2,1)}), bf16[32,32,1024]{2,1,0:T(8,128)(2,1)}, u32[]{:S(2)}, u32[]{:S(2)}) async-start(bf16[32,32,1024]{2,1,0:T(8,128)(2,1)} %project.4), calls=%async_computation | async-start | bytes 4194304 | tf_op jit(solution)/shard_map/all_to_all | solution.py:243
  119.0 0.0 copy-done.1
  119.0 1.3 slice.9
  120.3 5.9 %collective-permute-start.1 = (bf16[24,32,1024]{2,1,0:T(8,128)(2,1)}, bf16[24,32,1024]{2,1,0:T(8,128)(2,1)}, u32[]{:S(2)}, u32[]{:S(2)}) collective-permute-start(bf16[24,32,1024]{2,1,0:T(8,128)(2,1)} %slice.9), channel_id=1, source_target_pairs={{0,28},{4,0},{8,4},{12,8},{16,12},{20,16},{24,20},{28,24},{1,29},{... | collective-permute-start | bytes 4718600 | tf_op jit(solution)/shard_map/ppermute | solution.py:247
  126.2 1.6 slice.8
  127.7 1.3 collective-permute-start
  129.0 1.1 constant_dynamic-slice_fusion.3
  130.2 0.0 copy-start.4
  130.2 0.0 copy-start.6
  130.2 0.2 convert_reduce_fusion
  130.4 0.4 copy-done.4
  130.8 0.6 fusion.5
  131.5 0.0 copy-done.6
  131.5 29.8 %collective-permute-done.1.next_ref = bf16[24,32,1024]{2,1,0:T(8,128)(2,1)} collective-permute-done((bf16[24,32,1024]{2,1,0:T(8,128)(2,1)}, bf16[24,32,1024]{2,1,0:T(8,128)(2,1)}, u32[]{:S(2)}, u32[]{:S(2)}) %collective-permute-start.1) | collective-permute-done | bytes 1572896 | tf_op jit(solution)/shard_map/ppermute | solution.py:247
  161.2 5.8 %contract.2.rest_0_ = f32[4,256,448]{2,1,0:T(8,128)} custom-call(bf16[32,32,1024]{2,1,0:T(8,128)(2,1)} %all-to-all-done.2.left_ref, bf16[32,32,1024]{2,1,0:T(8,128)(2,1)} %copy-done.1, bf16[24,32,1024]{2,1,0:T(8,128)(2,1)} %collective-permute-done.1.next_ref), custom_call_target="tpu_custom_call" | custom-call | flops 939524096 | bytes 6291456 | tf_op jit(solution)/shard_map/contract/pallas_call | solution.py:160
  167.0 0.0 copy-start.8
  167.0 0.0 copy-start.9
  167.0 0.0 all-to-all-done.left_ref
  167.0 27.0 %collective-permute-done.next_ref = bf16[24,32,1024]{2,1,0:T(8,128)(2,1)S(1)} collective-permute-done((bf16[24,32,1024]{2,1,0:T(8,128)(2,1)S(1)}, bf16[24,32,1024]{2,1,0:T(8,128)(2,1)S(1)}, u32[]{:S(2)}, u32[]{:S(2)}) %collective-permute-start) | collective-permute-done | bytes 1572896 | tf_op jit(solution)/shard_map/ppermute | solution.py:247
  194.1 0.0 copy-start.3
  194.1 1.2 copy-done.3
  195.3 0.0 copy-start.5
  195.3 0.0 copy-start.7
  195.3 6.2 %contract.3 = bf16[32,32,256]{2,1,0:T(8,128)(2,1)} custom-call(bf16[32,32,1024]{2,1,0:T(8,128)(2,1)} %all-to-all-done.left_ref, bf16[32,32,1024]{2,1,0:T(8,128)(2,1)} %all-to-all-done.1.right_ref, bf16[24,32,1024]{2,1,0:T(8,128)(2,1)} %copy-done.3, f32[4,256,448]{2,1,0:T(8,128)} %contract.2.rest_0_), custom_call_target="tpu_custom_call" | custom-call | flops 939524096 | bytes 6291456 | tf_op jit(solution)/shard_map/contract/pallas_call | solution.py:160
  201.5 7.5 %all-to-all-start.4 = ((bf16[32,32,256]{2,1,0:T(8,128)(2,1)}), bf16[32,32,256]{2,1,0:T(8,128)(2,1)S(1)}, u32[]{:S(2)}, u32[]{:S(2)}) async-start(bf16[32,32,256]{2,1,0:T(8,128)(2,1)} %contract.3), calls=%async_computation.4 | async-start | bytes 1048576 | tf_op jit(solution)/shard_map/all_to_all | solution.py:243
  209.1 0.0 copy-done
  209.1 0.0 copy-done.8
  209.1 0.0 copy-done.9
  209.1 0.0 copy-done.5
  209.1 0.0 copy-done.7
  209.1 1.8 fusion.2.gate_ref
  210.9 8.3 %all-to-all-done.4.triangle_ref = bf16[32,32,256]{2,1,0:T(8,128)(2,1)S(1)} async-done(((bf16[32,32,256]{2,1,0:T(8,128)(2,1)}), bf16[32,32,256]{2,1,0:T(8,128)(2,1)S(1)}, u32[]{:S(2)}, u32[]{:S(2)}) %all-to-all-start.4) | async-done | bytes 524320 | tf_op jit(solution)/shard_map/all_to_all | solution.py:243
  219.2 0.0 copy-start.2
  219.2 0.8 copy-done.2
  220.0 3.0 %finish.1 = bf16[8,256,128]{2,1,0:T(8,128)(2,1)} custom-call(bf16[32,32,256]{2,1,0:T(8,128)(2,1)} %copy-done.2, f32[8,256,128]{2,1,0:T(8,128)} %fusion.2.gate_ref, f32[1,128]{1,0:T(1,128)} %bitcast.15, f32[1,128]{1,0:T(1,128)} %bitcast.16, bf16[128,128]{1,0:T(8,128)(2,1)} %w_ref.1), custom_call_target="tpu_custom_call" | custom-call | flops 67108864 | bytes 2097152 | tf_op jit(solution)/shard_map/finish/pallas_call | solution.py:196
  (2 shorter events, 0.0 us)
Async XLA Ops:
  0.0 209.1 %copy-start = (bf16[128,128]{1,0:T(8,128)(2,1)S(1)}, bf16[128,128]{1,0:T(8,128)(2,1)}, u32[]{:S(2)}) copy-start(bf16[128,128]{1,0:T(8,128)(2,1)} %param.16) | copy-start | bytes 98308
  10.4 35.2 %all-to-all-start.3 = ((bf16[32,32,1024]{2,1,0:T(8,128)(2,1)}), bf16[32,32,1024]{2,1,0:T(8,128)(2,1)S(1)}, u32[]{:S(2)}, u32[]{:S(2)}) async-start(bf16[32,32,1024]{2,1,0:T(8,128)(2,1)} %project.7), calls=%async_computation.3 | async-start | bytes 4194304 | tf_op jit(solution)/shard_map/all_to_all | solution.py:243
  45.6 73.4 %copy-start.1 = (bf16[32,32,1024]{2,1,0:T(8,128)(2,1)}, bf16[32,32,1024]{2,1,0:T(8,128)(2,1)S(1)}, u32[]{:S(2)}) copy-start(bf16[32,32,1024]{2,1,0:T(8,128)(2,1)S(1)} %all-to-all-done.3.right_ref) | copy-start | bytes 6291460
  45.6 33.8 %all-to-all-start.2 = ((bf16[32,32,1024]{2,1,0:T(8,128)(2,1)}), bf16[32,32,1024]{2,1,0:T(8,128)(2,1)}, u32[]{:S(2)}, u32[]{:S(2)}) async-start(bf16[32,32,1024]{2,1,0:T(8,128)(2,1)} %project.6), calls=%async_computation.2 | async-start | bytes 4194304 | tf_op jit(solution)/shard_map/all_to_all | solution.py:243
  79.4 33.7 %all-to-all-start.1 = ((bf16[32,32,1024]{2,1,0:T(8,128)(2,1)}), bf16[32,32,1024]{2,1,0:T(8,128)(2,1)}, u32[]{:S(2)}, u32[]{:S(2)}) async-start(bf16[32,32,1024]{2,1,0:T(8,128)(2,1)} %project.5), calls=%async_computation.1 | async-start | bytes 4194304 | tf_op jit(solution)/shard_map/all_to_all | solution.py:243
  113.1 53.9 %all-to-all-start = ((bf16[32,32,1024]{2,1,0:T(8,128)(2,1)}), bf16[32,32,1024]{2,1,0:T(8,128)(2,1)}, u32[]{:S(2)}, u32[]{:S(2)}) async-start(bf16[32,32,1024]{2,1,0:T(8,128)(2,1)} %project.4), calls=%async_computation | async-start | bytes 4194304 | tf_op jit(solution)/shard_map/all_to_all | solution.py:243
  120.3 40.9 %collective-permute-start.1 = (bf16[24,32,1024]{2,1,0:T(8,128)(2,1)}, bf16[24,32,1024]{2,1,0:T(8,128)(2,1)}, u32[]{:S(2)}, u32[]{:S(2)}) collective-permute-start(bf16[24,32,1024]{2,1,0:T(8,128)(2,1)} %slice.9), channel_id=1, source_target_pairs={{0,28},{4,0},{8,4},{12,8},{16,12},{20,16},{24,20},{28,24},{1,29},{... | collective-permute-start | bytes 4718600 | tf_op jit(solution)/shard_map/ppermute | solution.py:247
  127.7 66.3 %collective-permute-start = (bf16[24,32,1024]{2,1,0:T(8,128)(2,1)S(1)}, bf16[24,32,1024]{2,1,0:T(8,128)(2,1)S(1)}, u32[]{:S(2)}, u32[]{:S(2)}) collective-permute-start(bf16[24,32,1024]{2,1,0:T(8,128)(2,1)S(1)} %slice.8), channel_id=1, source_target_pairs={{0,28},{4,0},{8,4},{12,8},{16,12},{20,16},{24,20},{28,24},{1,29},{... | collective-permute-start | bytes 4718600 | tf_op jit(solution)/shard_map/ppermute | solution.py:247
  130.2 0.6 copy-start.4
  130.2 1.3 copy-start.6
  167.0 42.0 %copy-start.8 = (f32[128]{0:T(128)S(1)}, f32[128]{0:T(128)}, u32[]{:S(2)}) copy-start(f32[128]{0:T(128)} %param.12) | copy-start | bytes 1540
  167.0 42.0 %copy-start.9 = (f32[128]{0:T(128)S(1)}, f32[128]{0:T(128)}, u32[]{:S(2)}) copy-start(f32[128]{0:T(128)} %param.13) | copy-start | bytes 1540
  194.1 1.2 copy-start.3
  195.3 13.8 %copy-start.5 = (bf16[8,64,128]{2,1,0:T(8,128)(2,1)S(1)}, bf16[8,64,128]{2,1,0:T(8,128)(2,1)}, u32[]{:S(2)}) copy-start(bf16[8,64,128]{2,1,0:T(8,128)(2,1)} %copy-done.4) | copy-start | bytes 393220
  195.3 13.8 %copy-start.7 = (bf16[8,64,128]{2,1,0:T(8,128)(2,1)S(1)}, bf16[8,64,128]{2,1,0:T(8,128)(2,1)}, u32[]{:S(2)}) copy-start(bf16[8,64,128]{2,1,0:T(8,128)(2,1)} %copy-done.6) | copy-start | bytes 393220
  201.5 17.6 %all-to-all-start.4 = ((bf16[32,32,256]{2,1,0:T(8,128)(2,1)}), bf16[32,32,256]{2,1,0:T(8,128)(2,1)S(1)}, u32[]{:S(2)}, u32[]{:S(2)}) async-start(bf16[32,32,256]{2,1,0:T(8,128)(2,1)} %contract.3), calls=%async_computation.4 | async-start | bytes 1048576 | tf_op jit(solution)/shard_map/all_to_all | solution.py:243
  219.2 0.8 copy-start.2

commit v2 on v1

--- a/solution.py
+++ b/solution.py
@@ -14,7 +14,9 @@
 PLANE = ("yhi", "core", "x", "ylo")
 PARTS = 32
 OWN = 4
-HALVES = ((0, 1024), (1024, 1024))
+RIGHTS = ((0, 768), (768, 1280))
+CHUNK = 256
+STRIDE = 136
 F32 = jnp.float32
 BF16 = jnp.bfloat16
 VMEM_LIMIT = 56 * 1024 * 1024
@@ -34,37 +36,35 @@
 
 def project_kernel(pair_ref, mask_ref, gain_ref, bias_ref, value_ref, gate_ref, out_ref, mixed):
     width = pair_ref.shape[1]
-    lane = lax.broadcasted_iota(jnp.int32, (128, 128), 0)
-    sub = lax.broadcasted_iota(jnp.int32, (128, 128), 1)
-    eye = jnp.where(lane == sub, 1.0, 0.0).astype(BF16)
-    gain = across(columns(gain_ref[...]), width)
-    bias = across(columns(bias_ref[...]), width)
+    gain = across(columns(gain_ref[...]), CHUNK)
+    bias = across(columns(bias_ref[...]), CHUNK)
     value_t = jnp.transpose(value_ref[...].astype(F32)).astype(BF16)
     gate_t = jnp.transpose(gate_ref[...].astype(F32) * 0.5).astype(BF16)
     weight = jnp.concatenate([value_t, gate_t], axis=0)
-    half_mask = mask_ref[...].astype(F32) * 0.5
-    for row in range(SUB):
-        turned = dot(eye, pair_ref[row], ((1,), (1,)))
-        centred = turned - jnp.sum(turned, axis=0, keepdims=True) * (1.0 / 128)
-        variance = jnp.sum(centred * centred, axis=0, keepdims=True) * (1.0 / 128)
-        normed = (centred * lax.rsqrt(variance + EPS) * gain + bias).astype(BF16)
-        both = dot(weight, normed, ((1,), (0,)))
-        half = both[:128] * half_mask[row : row + 1]
-        result = half + half * jnp.tanh(both[128:])
-        for tile in range(width // 128):
-            first = (tile * SUB + row) * 128
-            mixed[first : first + 128, :] = result[:, tile * 128 : (tile + 1) * 128]
-    for tile in range(width // 128):
-        for part in range(PARTS):
-            first = tile * SUB * 128 + part * OWN
-            pieces = [mixed[pl.ds(first + k, SUB, stride=128), :] for k in range(OWN)]
-            out_ref[part, :, tile * 128 : (tile + 1) * 128] = jnp.concatenate(
-                pieces, axis=0
-            ).astype(BF16)
+    for start in range(0, width, CHUNK):
+        for row in range(SUB):
+            turned = jnp.transpose(pair_ref[row, start : start + CHUNK, :]).astype(F32)
+            half_mask = mask_ref[row : row + 1, start : start + CHUNK].astype(F32) * 0.5
+            centred = turned - jnp.sum(turned, axis=0, keepdims=True) * (1.0 / 128)
+            variance = jnp.sum(centred * centred, axis=0, keepdims=True) * (1.0 / 128)
+            normed = (centred * lax.rsqrt(variance + EPS) * gain + bias).astype(BF16)
+            both = dot(weight, normed, ((1,), (0,)))
+            half = both[:128] * half_mask
+            result = half + half * jnp.tanh(both[128:])
+            for tile in range(CHUNK // 128):
+                first = ((start // 128 + tile) * SUB + row) * STRIDE
+                mixed[first : first + 128, :] = result[:, tile * 128 : (tile + 1) * 128]
+        for tile in range(start // 128, (start + CHUNK) // 128):
+            for part in range(PARTS):
+                first = tile * SUB * STRIDE + part * OWN
+                pieces = [mixed[pl.ds(first + k, SUB, stride=STRIDE), :] for k in range(OWN)]
+                out_ref[part, :, tile * 128 : (tile + 1) * 128] = jnp.concatenate(
+                    pieces, axis=0
+                ).astype(BF16)
 
 
 def project(pair, mask, gain, bias, w_value, w_gate, side, start, length):
-    width = min(512, length)
+    width = 512 if start % 512 == 0 and length % 512 == 0 else 256
     first = start // width
     whole = lambda i: (0, 0)
     column = lambda i: (0, side)
@@ -82,7 +82,7 @@
         ],
         out_specs=pl.BlockSpec((PARTS, OWN * SUB, width), lambda i: (0, 0, i)),
         out_shape=jax.ShapeDtypeStruct((PARTS, OWN * SUB, length), BF16),
-        scratch_shapes=[pltpu.VMEM((SUB * width, 128), F32)],
+        scratch_shapes=[pltpu.VMEM((SUB * STRIDE * (width // 128), 128), F32)],
         compiler_params=pltpu.CompilerParams(vmem_limit_bytes=VMEM_LIMIT),
         cost_estimate=pl.CostEstimate(
             flops=tokens * 128 * 384 * 2, bytes_accessed=tokens * 512, transcendentals=tokens * 128
@@ -100,70 +100,66 @@
     ]
 
 
-def contract_kernel(last, left_ref, right_ref, next_ref, *rest):
-    if last:
-        before_ref, out_ref, total = rest
-    else:
-        out_ref, total = rest
+def contract_kernel(steps, left_ref, *rest):
+    pieces = rest[: 2 * len(steps)]
+    out_ref, total = rest[2 * len(steps) :]
     step = pl.program_id(0)
 
     @pl.when(step == 0)
     def _():
-        total[...] = before_ref[...] if last else jnp.zeros_like(total)
-
-    for pair_of_channels in range(OWN // 2):
-        left = rows_of(left_ref, pair_of_channels)
-        right = rows_of(right_ref, pair_of_channels)
-        after = rows_of(next_ref, pair_of_channels)
-        for k in range(2):
-            window = jnp.concatenate([right[k], after[k]], axis=0)
-            total[pair_of_channels * 2 + k] += dot(left[k], window, ((1,), (1,)))
+        total[...] = jnp.zeros_like(total)
+
+    for k, (begin, end) in enumerate(steps):
+
+        @pl.when((step >= begin) & (step < end))
+        def _(right_ref=pieces[2 * k], next_ref=pieces[2 * k + 1]):
+            for pair_of_channels in range(OWN // 2):
+                left = rows_of(left_ref, pair_of_channels)
+                right = rows_of(right_ref, pair_of_channels)
+                after = rows_of(next_ref, pair_of_channels)
+                for k in range(2):
+                    window = jnp.concatenate([right[k], after[k]], axis=0)
+                    total[pair_of_channels * 2 + k] += dot(left[k], window, ((1,), (1,)))
 
     @pl.when(step == pl.num_programs(0) - 1)
     def _():
-        if not last:
-            out_ref[...] = total[...]
-        else:
-            groups = BLOCK // SUB
-            for block in range(STEPS):
-                for pair_of_channels in range(OWN // 2):
-                    band = [
-                        total[
-                            pair_of_channels * 2 + k,
-                            block * BLOCK : (block + 1) * BLOCK,
-                            block * BLOCK : (block + STEPS) * BLOCK,
-                        ].reshape(groups, SUB, STEPS * BLOCK)
-                        for k in range(2)
-                    ]
-                    out_ref[
-                        block * groups : (block + 1) * groups,
-                        pair_of_channels * 16 : (pair_of_channels + 1) * 16,
-                        :,
-                    ] = jnp.concatenate(band, axis=1).astype(BF16)
-
-
-def contract(left, right, after, before):
+        groups = BLOCK // SUB
+        for block in range(STEPS):
+            for pair_of_channels in range(OWN // 2):
+                band = [
+                    total[
+                        pair_of_channels * 2 + k,
+                        block * BLOCK : (block + 1) * BLOCK,
+                        block * BLOCK : (block + STEPS) * BLOCK,
+                    ].reshape(groups, SUB, STEPS * BLOCK)
+                    for k in range(2)
+                ]
+                out_ref[
+                    block * groups : (block + 1) * groups,
+                    pair_of_channels * 16 : (pair_of_channels + 1) * 16,
+                    :,
+                ] = jnp.concatenate(band, axis=1).astype(BF16)
+
+
+def contract(left, pieces):
     length = left.shape[2]
-    width = 256
-    last = before is not None
-    shape = (OWN, BLOCK * STEPS, BLOCK * (2 * STEPS - 1))
-    part = lambda i: (0, 0, i)
-    whole = lambda i: (0, 0, 0)
-    in_specs = [pl.BlockSpec(v.shape[:2] + (width,), part) for v in (left, right, after)]
-    operands = [left, right, after]
-    if last:
-        in_specs.append(pl.BlockSpec(shape, whole))
-        operands.append(before)
-        out_shape = jax.ShapeDtypeStruct((PARTS, OWN * SUB, STEPS * BLOCK), BF16)
-    else:
-        out_shape = jax.ShapeDtypeStruct(shape, F32)
+    in_specs = [pl.BlockSpec(left.shape[:2] + (CHUNK,), lambda i: (0, 0, i))]
+    operands, steps, begin = [left], [], 0
+    for right, after in pieces:
+        count = right.shape[2] // CHUNK
+        place = lambda i, first=begin, most=count - 1: (0, 0, jnp.clip(i - first, 0, most))
+        in_specs += [pl.BlockSpec(v.shape[:2] + (CHUNK,), place) for v in (right, after)]
+        operands += [right, after]
+        steps.append((begin, begin + count))
+        begin += count
+    out_shape = jax.ShapeDtypeStruct((PARTS, OWN * SUB, STEPS * BLOCK), BF16)
     return pl.pallas_call(
-        functools.partial(contract_kernel, last),
-        grid=(length // width,),
+        functools.partial(contract_kernel, tuple(steps)),
+        grid=(length // CHUNK,),
         in_specs=in_specs,
-        out_specs=pl.BlockSpec(out_shape.shape, whole),
+        out_specs=pl.BlockSpec(out_shape.shape, lambda i: (0, 0, 0)),
         out_shape=out_shape,
-        scratch_shapes=[pltpu.VMEM(shape, F32)],
+        scratch_shapes=[pltpu.VMEM((OWN, BLOCK * STEPS, BLOCK * (2 * STEPS - 1)), F32)],
         compiler_params=pltpu.CompilerParams(vmem_limit_bytes=VMEM_LIMIT),
         cost_estimate=pl.CostEstimate(
             flops=2 * 4 * 256 * 448 * length, bytes_accessed=6 * 1024 * length, transcendentals=0
@@ -242,16 +238,19 @@
     def spread(value):
         return lax.all_to_all(value, PLANE, 0, 0, tiled=True)
 
-    rights = [spread(operand(1, chunk)) for chunk in HALVES]
-    afters = [
-        lax.ppermute(right[: (STEPS - 1) * BLOCK // SUB], "z", to_before) for right in rights
-    ]
-    lefts = [spread(operand(0, chunk)) for chunk in HALVES]
+    def shifted(right):
+        return lax.ppermute(right[: (STEPS - 1) * BLOCK // SUB], "z", to_before)
+
+    first = spread(operand(1, RIGHTS[0]))
+    first_after = shifted(first)
+    second = spread(operand(1, RIGHTS[1]))
+    second_after = shifted(second)
+    left = operand(0, (0, pair.shape[1]))
+    left, first_after = lax.optimization_barrier((left, first_after))
+    left = spread(left)
     block = lax.axis_index("z") * 4 + lax.axis_index("yhi") * 2 + lax.axis_index("core")
     gate = output_gate(pair, in_gain, in_bias, out_gate_w, block)
-    total = contract(lefts[0], rights[0], afters[0], None)
-    band = contract(lefts[1], rights[1], afters[1], total)
-    triangle = spread(band)
+    triangle = spread(contract(left, [(first, first_after), (second, second_after)]))
     return finish(triangle, gate, out_gain.reshape(1, 128), out_bias.reshape(1, 128), w_out)
 
 

time: 225 us -> 166 us (0.74)
  waiting for transfers between devices: 117 us -> 85.7 us
  Pallas kernels: 57 us -> 34.2 us
  starting transfers between devices: 39.8 us -> 35 us
    all_to_all x5 -> x4, waiting for transfers between devices: 60.1 us -> 28.8 us  [spread(): return lax.all_to_all(value, PLANE, 0, 0, tiled=True)]
    pallas_call x4 -> x3, Pallas kernels: 42 us -> 21.8 us  [project(): pl.pallas_call(project_kernel, grid=(length // width,), in_specs=[pl.Bloc...]
    all_to_all x5 -> x4, starting transfers between devices: 32.7 us -> 23.5 us  [spread(): return lax.all_to_all(value, PLANE, 0, 0, tiled=True)]
    ppermute x2, starting transfers between devices: 7.16 us -> 11.5 us  [shifted(): return lax.ppermute(right[:(STEPS - 1) * BLOCK // SUB], 'z', to_before)]
    pallas_call x2 -> x1, Pallas kernels: 12 us -> 9.43 us  [contract(): pl.pallas_call(functools.partial(contract_kernel, tuple(steps)), grid=(le...]
  transfers between devices with their start and end apart: 7 -> 6, of which waited for: 6 -> 6; matrix products, arithmetic and copies ran while one was open for 3% -> 4% of each run, Pallas kernels for 17% -> 10%
where the time goes in v2:
time: 166 us; the launch traced here: 164 us
  waiting for transfers between devices  85.7 us (52%)
  starting transfers between devices  35 us (21%)
  Pallas kernels  34.2 us (21%)
  local copies, waits for them, and re-layouts  5.91 us (4%)
  matrix products  1.78 us (1%)
    ppermute x2, waiting for transfers between devices, shifted(): return lax.ppermute(right[:(STEPS - 1) * BLOCK // SUB], 'z', to_before)  56.8 us
    all_to_all x4, waiting for transfers between devices, spread(): return lax.all_to_all(value, PLANE, 0, 0, tiled=True)  28.8 us
    all_to_all x4, starting transfers between devices, spread(): return lax.all_to_all(value, PLANE, 0, 0, tiled=True)  23.5 us
    pallas_call x3, Pallas kernels, project(): pl.pallas_call(project_kernel, grid=(length // width,), in_specs=[pl.Bloc...  21.8 us
    ppermute x2, starting transfers between devices, shifted(): return lax.ppermute(right[:(STEPS - 1) * BLOCK // SUB], 'z', to_before)  11.5 us
    pallas_call x1, Pallas kernels, contract(): pl.pallas_call(functools.partial(contract_kernel, tuple(steps)), grid=(le...  9.43 us
  transfers between devices with their start and end apart: 6, of which 6 were waited for; matrix products, arithmetic and copies ran while one was open for 4% of the time, Pallas kernels for 10%

profile of v2, /device:TPU:8, one launch (start us, length us, event | category | flops | bytes accessed | tf_op | source)
XLA Modules:
  0.0 163.5 jit_solution(8785382907117410936)
XLA Ops:
  0.0 0.0 copy-start
  0.0 5.0 %project.4 = bf16[32,32,768]{2,1,0:T(8,128)(2,1)} custom-call(bf16[8,2048,128]{2,1,0:T(8,128)(2,1)} %pair_ref.5, s32[8,2048]{1,0:T(8,128)} %mask_ref.5, f32[1,128]{1,0:T(1,128)} %bitcast.7, f32[1,128]{1,0:T(1,128)} %bitcast.10, bf16[128,256]{1,0:T(8,128)(2,1)} %value_ref.5, bf16[128,256]{1,0:T(8,128)(2,1)} %gate_ref.5), custom_call_target="tpu_custom_call" | custom-call | flops 603979776 | bytes 3145728 | tf_op jit(solution)/shard_map/project/pallas_call | solution.py:72
  5.0 7.5 %all-to-all-start = ((bf16[32,32,768]{2,1,0:T(8,128)(2,1)}), bf16[32,32,768]{2,1,0:T(8,128)(2,1)S(1)}, u32[]{:S(2)}, u32[]{:S(2)}) async-start(bf16[32,32,768]{2,1,0:T(8,128)(2,1)} %project.4), calls=%async_computation | async-start | bytes 3145728 | tf_op jit(solution)/shard_map/all_to_all | solution.py:239
  12.6 7.3 %project.5 = bf16[32,32,1280]{2,1,0:T(8,128)(2,1)} custom-call(bf16[8,2048,128]{2,1,0:T(8,128)(2,1)} %pair_ref.5, s32[8,2048]{1,0:T(8,128)} %mask_ref.5, f32[1,128]{1,0:T(1,128)} %bitcast.8, f32[1,128]{1,0:T(1,128)} %bitcast.11, bf16[128,256]{1,0:T(8,128)(2,1)} %value_ref.5, bf16[128,256]{1,0:T(8,128)(2,1)} %gate_ref.5), custom_call_target="tpu_custom_call" | custom-call | flops 1006632960 | bytes 5242880 | tf_op jit(solution)/shard_map/project/pallas_call | solution.py:72
  19.9 14.1 %all-to-all-done.rest_0_ = bf16[32,32,768]{2,1,0:T(8,128)(2,1)S(1)} async-done(((bf16[32,32,768]{2,1,0:T(8,128)(2,1)}), bf16[32,32,768]{2,1,0:T(8,128)(2,1)S(1)}, u32[]{:S(2)}, u32[]{:S(2)}) %all-to-all-start) | async-done | bytes 1572896 | tf_op jit(solution)/shard_map/all_to_all | solution.py:239
  34.0 0.0 copy-start.2
  34.0 1.1 copy-done.2
  35.2 5.7 %all-to-all-start.2 = ((bf16[32,32,1280]{2,1,0:T(8,128)(2,1)}), bf16[32,32,1280]{2,1,0:T(8,128)(2,1)S(1)}, u32[]{:S(2)}, u32[]{:S(2)}) async-start(bf16[32,32,1280]{2,1,0:T(8,128)(2,1)} %project.5), calls=%async_computation.2 | async-start | bytes 5242880 | tf_op jit(solution)/shard_map/all_to_all | solution.py:239
  40.9 1.3 slice.8
  42.3 5.9 %collective-permute-start = (bf16[24,32,768]{2,1,0:T(8,128)(2,1)S(1)}, bf16[24,32,768]{2,1,0:T(8,128)(2,1)}, u32[]{:S(2)}, u32[]{:S(2)}) collective-permute-start(bf16[24,32,768]{2,1,0:T(8,128)(2,1)S(1)} %slice.8), channel_id=1, source_target_pairs={{0,28},{4,0},{8,4},{12,8},{16,12},{20,16},{24,20},{28,24},{1,29},{... | collective-permute-start | bytes 3538952 | tf_op jit(solution)/shard_map/ppermute | solution.py:242
  48.2 9.4 %project.3 = bf16[32,32,2048]{2,1,0:T(8,128)(2,1)} custom-call(bf16[8,2048,128]{2,1,0:T(8,128)(2,1)} %pair_ref.5, s32[8,2048]{1,0:T(8,128)} %mask_ref.5, f32[1,128]{1,0:T(1,128)} %bitcast.9, f32[1,128]{1,0:T(1,128)} %bitcast.12, bf16[128,256]{1,0:T(8,128)(2,1)} %value_ref.5, bf16[128,256]{1,0:T(8,128)(2,1)} %gate_ref.5), custom_call_target="tpu_custom_call" | custom-call | flops 1610612736 | bytes 8388608 | tf_op jit(solution)/shard_map/project/pallas_call | solution.py:72
  57.6 16.1 %collective-permute-done.rest_1_ = bf16[24,32,768]{2,1,0:T(8,128)(2,1)} collective-permute-done((bf16[24,32,768]{2,1,0:T(8,128)(2,1)S(1)}, bf16[24,32,768]{2,1,0:T(8,128)(2,1)}, u32[]{:S(2)}, u32[]{:S(2)}) %collective-permute-start) | collective-permute-done | bytes 1179680 | tf_op jit(solution)/shard_map/ppermute | solution.py:242
  73.7 1.4 all-to-all-done.2.rest_2_
  75.1 0.0 copy-start.1
  75.1 6.1 %all-to-all-start.1 = ((bf16[32,32,2048]{2,1,0:T(8,128)(2,1)}), bf16[32,32,2048]{2,1,0:T(8,128)(2,1)}, u32[]{:S(2)}, u32[]{:S(2)}) async-start(bf16[32,32,2048]{2,1,0:T(8,128)(2,1)} %project.3), calls=%async_computation.1 | async-start | bytes 8388608 | tf_op jit(solution)/shard_map/all_to_all | solution.py:239
  81.2 0.0 copy-done.1
  81.2 1.5 slice.9
  82.7 5.6 %collective-permute-start.1 = (bf16[24,32,1280]{2,1,0:T(8,128)(2,1)}, bf16[24,32,1280]{2,1,0:T(8,128)(2,1)S(1)}, u32[]{:S(2)}, u32[]{:S(2)}) collective-permute-start(bf16[24,32,1280]{2,1,0:T(8,128)(2,1)} %slice.9), channel_id=1, source_target_pairs={{0,28},{4,0},{8,4},{12,8},{16,12},{20,16},{24,20},{28,24},{1,29},{... | collective-permute-start | bytes 5898248 | tf_op jit(solution)/shard_map/ppermute | solution.py:242
  88.2 1.1 constant_dynamic-slice_fusion.3
  89.4 0.2 convert_reduce_fusion
  89.6 0.6 fusion.5
  90.2 0.0 copy-start.5
  90.2 0.0 copy-start.6
  90.2 40.7 %collective-permute-done.1.rest_3_ = bf16[24,32,1280]{2,1,0:T(8,128)(2,1)S(1)} collective-permute-done((bf16[24,32,1280]{2,1,0:T(8,128)(2,1)}, bf16[24,32,1280]{2,1,0:T(8,128)(2,1)S(1)}, u32[]{:S(2)}, u32[]{:S(2)}) %collective-permute-start.1) | collective-permute-done | bytes 1966112 | tf_op jit(solution)/shard_map/ppermute | solution.py:242
  131.0 0.0 copy-start.4
  131.0 5.0 %all-to-all-done.1.left_ref = bf16[32,32,2048]{2,1,0:T(8,128)(2,1)} async-done(((bf16[32,32,2048]{2,1,0:T(8,128)(2,1)}), bf16[32,32,2048]{2,1,0:T(8,128)(2,1)}, u32[]{:S(2)}, u32[]{:S(2)}) %all-to-all-start.1) | async-done | bytes 4194336 | tf_op jit(solution)/shard_map/all_to_all | solution.py:239
  136.0 0.0 copy-done.4
  136.0 9.4 %contract.1 = bf16[32,32,256]{2,1,0:T(8,128)(2,1)} custom-call(bf16[32,32,2048]{2,1,0:T(8,128)(2,1)} %all-to-all-done.1.left_ref, bf16[32,32,768]{2,1,0:T(8,128)(2,1)} %copy-done.2, bf16[24,32,768]{2,1,0:T(8,128)(2,1)} %collective-permute-done.rest_1_, bf16[32,32,1280]{2,1,0:T(8,128)(2,1)} %copy-done.1, bf16[24,32,1280]{2,1,0:T(8,128)(2,1)} %copy-done.4), custom_call_target="tpu_custom_call" | custom-call | flops 1879048192 | bytes 12582912 | tf_op jit(solution)/shard_map/contract/pallas_call | solution.py:156
  145.4 4.2 %all-to-all-start.3 = ((bf16[32,32,256]{2,1,0:T(8,128)(2,1)}), bf16[32,32,256]{2,1,0:T(8,128)(2,1)S(1)}, u32[]{:S(2)}, u32[]{:S(2)}) async-start(bf16[32,32,256]{2,1,0:T(8,128)(2,1)} %contract.1), calls=%async_computation.3 | async-start | bytes 1048576 | tf_op jit(solution)/shard_map/all_to_all | solution.py:239
  149.6 0.0 copy-done
  149.6 0.0 copy-done.5
  149.6 0.0 copy-done.6
  149.6 1.8 %fusion.2.gate_ref = f32[8,256,128]{2,1,0:T(8,128)} fusion(f32[128]{0:T(128)S(1)} %copy-done.6, f32[128]{0:T(128)S(1)} %copy-done.5, f32[8,256]{1,0:T(8,128)S(1)} %add_rsqrt_fusion, f32[8,256]{1,0:T(8,128)S(1)} %broadcast_multiply_fusion, bf16[128,128]{1,0:T(8,128)(2,1)S(1)} %copy-done, bf16[8,64,128]{2,1,0:T(8,128)(2,1)S(1)} %get-tuple-element.11, ...), kind=kOutput, calls=%fused_computation.3 | convolution fusion | flops 71303168 | bytes 1623040 | tf_op jit(solution)/shard_map/dot_general | solution.py:26
  151.4 8.3 %all-to-all-done.3.triangle_ref = bf16[32,32,256]{2,1,0:T(8,128)(2,1)S(1)} async-done(((bf16[32,32,256]{2,1,0:T(8,128)(2,1)}), bf16[32,32,256]{2,1,0:T(8,128)(2,1)S(1)}, u32[]{:S(2)}, u32[]{:S(2)}) %all-to-all-start.3) | async-done | bytes 524320 | tf_op jit(solution)/shard_map/all_to_all | solution.py:239
  159.7 0.0 copy-start.3
  159.7 0.8 copy-done.3
  160.5 3.0 %finish.1 = bf16[8,256,128]{2,1,0:T(8,128)(2,1)} custom-call(bf16[32,32,256]{2,1,0:T(8,128)(2,1)} %copy-done.3, f32[8,256,128]{2,1,0:T(8,128)} %fusion.2.gate_ref, f32[1,128]{1,0:T(1,128)} %bitcast.13, f32[1,128]{1,0:T(1,128)} %bitcast.14, bf16[128,128]{1,0:T(8,128)(2,1)} %w_ref.1), custom_call_target="tpu_custom_call" | custom-call | flops 67108864 | bytes 2097152 | tf_op jit(solution)/shard_map/finish/pallas_call | solution.py:192
  (2 shorter events, 0.0 us)
Async XLA Ops:
  0.0 149.6 %copy-start = (bf16[128,128]{1,0:T(8,128)(2,1)S(1)}, bf16[128,128]{1,0:T(8,128)(2,1)}, u32[]{:S(2)}) copy-start(bf16[128,128]{1,0:T(8,128)(2,1)} %param.16) | copy-start | bytes 98308
  5.0 29.0 %all-to-all-start = ((bf16[32,32,768]{2,1,0:T(8,128)(2,1)}), bf16[32,32,768]{2,1,0:T(8,128)(2,1)S(1)}, u32[]{:S(2)}, u32[]{:S(2)}) async-start(bf16[32,32,768]{2,1,0:T(8,128)(2,1)} %project.4), calls=%async_computation | async-start | bytes 3145728 | tf_op jit(solution)/shard_map/all_to_all | solution.py:239
  34.0 1.1 copy-start.2
  35.2 40.0 %all-to-all-start.2 = ((bf16[32,32,1280]{2,1,0:T(8,128)(2,1)}), bf16[32,32,1280]{2,1,0:T(8,128)(2,1)S(1)}, u32[]{:S(2)}, u32[]{:S(2)}) async-start(bf16[32,32,1280]{2,1,0:T(8,128)(2,1)} %project.5), calls=%async_computation.2 | async-start | bytes 5242880 | tf_op jit(solution)/shard_map/all_to_all | solution.py:239
  42.3 31.5 %collective-permute-start = (bf16[24,32,768]{2,1,0:T(8,128)(2,1)S(1)}, bf16[24,32,768]{2,1,0:T(8,128)(2,1)}, u32[]{:S(2)}, u32[]{:S(2)}) collective-permute-start(bf16[24,32,768]{2,1,0:T(8,128)(2,1)S(1)} %slice.8), channel_id=1, source_target_pairs={{0,28},{4,0},{8,4},{12,8},{16,12},{20,16},{24,20},{28,24},{1,29},{... | collective-permute-start | bytes 3538952 | tf_op jit(solution)/shard_map/ppermute | solution.py:242
  75.1 6.1 %copy-start.1 = (bf16[32,32,1280]{2,1,0:T(8,128)(2,1)}, bf16[32,32,1280]{2,1,0:T(8,128)(2,1)S(1)}, u32[]{:S(2)}) copy-start(bf16[32,32,1280]{2,1,0:T(8,128)(2,1)S(1)} %all-to-all-done.2.rest_2_) | copy-start | bytes 7864324
  75.1 60.9 %all-to-all-start.1 = ((bf16[32,32,2048]{2,1,0:T(8,128)(2,1)}), bf16[32,32,2048]{2,1,0:T(8,128)(2,1)}, u32[]{:S(2)}, u32[]{:S(2)}) async-start(bf16[32,32,2048]{2,1,0:T(8,128)(2,1)} %project.3), calls=%async_computation.1 | async-start | bytes 8388608 | tf_op jit(solution)/shard_map/all_to_all | solution.py:239
  82.7 48.3 %collective-permute-start.1 = (bf16[24,32,1280]{2,1,0:T(8,128)(2,1)}, bf16[24,32,1280]{2,1,0:T(8,128)(2,1)S(1)}, u32[]{:S(2)}, u32[]{:S(2)}) collective-permute-start(bf16[24,32,1280]{2,1,0:T(8,128)(2,1)} %slice.9), channel_id=1, source_target_pairs={{0,28},{4,0},{8,4},{12,8},{16,12},{20,16},{24,20},{28,24},{1,29},{... | collective-permute-start | bytes 5898248 | tf_op jit(solution)/shard_map/ppermute | solution.py:242
  90.2 59.4 %copy-start.5 = (f32[128]{0:T(128)S(1)}, f32[128]{0:T(128)}, u32[]{:S(2)}) copy-start(f32[128]{0:T(128)} %param.12) | copy-start | bytes 1540
  90.2 59.4 %copy-start.6 = (f32[128]{0:T(128)S(1)}, f32[128]{0:T(128)}, u32[]{:S(2)}) copy-start(f32[128]{0:T(128)} %param.13) | copy-start | bytes 1540
  131.0 5.0 %copy-start.4 = (bf16[24,32,1280]{2,1,0:T(8,128)(2,1)}, bf16[24,32,1280]{2,1,0:T(8,128)(2,1)S(1)}, u32[]{:S(2)}) copy-start(bf16[24,32,1280]{2,1,0:T(8,128)(2,1)S(1)} %collective-permute-done.1.rest_3_) | copy-start | bytes 5898244
  145.4 14.3 %all-to-all-start.3 = ((bf16[32,32,256]{2,1,0:T(8,128)(2,1)}), bf16[32,32,256]{2,1,0:T(8,128)(2,1)S(1)}, u32[]{:S(2)}, u32[]{:S(2)}) async-start(bf16[32,32,256]{2,1,0:T(8,128)(2,1)} %contract.1), calls=%async_computation.3 | async-start | bytes 1048576 | tf_op jit(solution)/shard_map/all_to_all | solution.py:239
  159.7 0.8 copy-start.3

commit v3 on v2

--- a/solution.py
+++ b/solution.py
@@ -14,12 +14,14 @@
 PLANE = ("yhi", "core", "x", "ylo")
 PARTS = 32
 OWN = 4
-RIGHTS = ((0, 768), (768, 1280))
-CHUNK = 256
+RIGHTS = ((0, 640), (640, 1408))
+CHUNK = 128
 STRIDE = 136
 F32 = jnp.float32
 BF16 = jnp.bfloat16
-VMEM_LIMIT = 56 * 1024 * 1024
+VMEM_LIMIT = 24 * 1024 * 1024
+VMEM_CONTRACT = 36 * 1024 * 1024
+VMEM_FIRST = 60 * 1024 * 1024
 
 
 def dot(a, b, dims):
@@ -64,7 +66,7 @@
 
 
 def project(pair, mask, gain, bias, w_value, w_gate, side, start, length):
-    width = 512 if start % 512 == 0 and length % 512 == 0 else 256
+    width = max(w for w in range(128, 641, 128) if start % w == 0 and length % w == 0)
     first = start // width
     whole = lambda i: (0, 0)
     column = lambda i: (0, side)
@@ -83,7 +85,9 @@
         out_specs=pl.BlockSpec((PARTS, OWN * SUB, width), lambda i: (0, 0, i)),
         out_shape=jax.ShapeDtypeStruct((PARTS, OWN * SUB, length), BF16),
         scratch_shapes=[pltpu.VMEM((SUB * STRIDE * (width // 128), 128), F32)],
-        compiler_params=pltpu.CompilerParams(vmem_limit_bytes=VMEM_LIMIT),
+        compiler_params=pltpu.CompilerParams(
+            vmem_limit_bytes=VMEM_FIRST if side == 1 and start == 0 else VMEM_LIMIT
+        ),
         cost_estimate=pl.CostEstimate(
             flops=tokens * 128 * 384 * 2, bytes_accessed=tokens * 512, transcendentals=tokens * 128
         ),
@@ -100,39 +104,48 @@
     ]
 
 
-def contract_kernel(steps, left_ref, *rest):
-    pieces = rest[: 2 * len(steps)]
-    out_ref, total = rest[2 * len(steps) :]
-    step = pl.program_id(0)
-
-    @pl.when(step == 0)
-    def _():
-        total[...] = jnp.zeros_like(total)
-
-    for k, (begin, end) in enumerate(steps):
-
-        @pl.when((step >= begin) & (step < end))
-        def _(right_ref=pieces[2 * k], next_ref=pieces[2 * k + 1]):
-            for pair_of_channels in range(OWN // 2):
-                left = rows_of(left_ref, pair_of_channels)
-                right = rows_of(right_ref, pair_of_channels)
-                after = rows_of(next_ref, pair_of_channels)
-                for k in range(2):
-                    window = jnp.concatenate([right[k], after[k]], axis=0)
-                    total[pair_of_channels * 2 + k] += dot(left[k], window, ((1,), (1,)))
-
-    @pl.when(step == pl.num_programs(0) - 1)
-    def _():
-        groups = BLOCK // SUB
-        for block in range(STEPS):
-            for pair_of_channels in range(OWN // 2):
+def contract_kernel(steps, left_hbm, *rest):
+    count = len(steps)
+    pieces, out_ref, left_ref = rest[: 2 * count], rest[2 * count], rest[2 * count + 1]
+    held = rest[2 * count + 2 : 4 * count + 2]
+    total, sems = rest[4 * count + 2 :]
+    copies = []
+    for k, (begin, length) in enumerate(steps):
+        tokens = pl.ds(begin, length)
+        mine = [
+            pltpu.make_async_copy(
+                left_hbm.at[:, :, tokens], left_ref.at[:, :, tokens], sems.at[3 * k]
+            )
+        ] + [
+            pltpu.make_async_copy(pieces[2 * k + j], held[2 * k + j], sems.at[3 * k + 1 + j])
+            for j in range(2)
+        ]
+        for copy in mine:
+            copy.start()
+        copies.append(mine)
+    groups = BLOCK // SUB
+    for k, (begin, length) in enumerate(steps):
+        for copy in copies[k]:
+            copy.wait()
+        for pair_of_channels in range(OWN // 2):
+            left = rows_of(left_ref.at[:, :, pl.ds(begin, length)], pair_of_channels)
+            right = rows_of(held[2 * k], pair_of_channels)
+            after = rows_of(held[2 * k + 1], pair_of_channels)
+            for j in range(2):
+                window = jnp.concatenate([right[j], after[j]], axis=0)
+                product = dot(left[j], window, ((1,), (1,)))
+                channel = pair_of_channels * 2 + j
+                total[channel] = product if k == 0 else total[channel] + product
+            if k < count - 1:
+                continue
+            for block in range(STEPS):
                 band = [
                     total[
-                        pair_of_channels * 2 + k,
+                        pair_of_channels * 2 + j,
                         block * BLOCK : (block + 1) * BLOCK,
                         block * BLOCK : (block + STEPS) * BLOCK,
                     ].reshape(groups, SUB, STEPS * BLOCK)
-                    for k in range(2)
+                    for j in range(2)
                 ]
                 out_ref[
                     block * groups : (block + 1) * groups,
@@ -142,27 +155,26 @@
 
 
 def contract(left, pieces):
-    length = left.shape[2]
-    in_specs = [pl.BlockSpec(left.shape[:2] + (CHUNK,), lambda i: (0, 0, i))]
     operands, steps, begin = [left], [], 0
     for right, after in pieces:
-        count = right.shape[2] // CHUNK
-        place = lambda i, first=begin, most=count - 1: (0, 0, jnp.clip(i - first, 0, most))
-        in_specs += [pl.BlockSpec(v.shape[:2] + (CHUNK,), place) for v in (right, after)]
         operands += [right, after]
-        steps.append((begin, begin + count))
-        begin += count
-    out_shape = jax.ShapeDtypeStruct((PARTS, OWN * SUB, STEPS * BLOCK), BF16)
+        steps.append((begin, right.shape[2]))
+        begin += right.shape[2]
     return pl.pallas_call(
         functools.partial(contract_kernel, tuple(steps)),
-        grid=(length // CHUNK,),
-        in_specs=in_specs,
-        out_specs=pl.BlockSpec(out_shape.shape, lambda i: (0, 0, 0)),
-        out_shape=out_shape,
-        scratch_shapes=[pltpu.VMEM((OWN, BLOCK * STEPS, BLOCK * (2 * STEPS - 1)), F32)],
-        compiler_params=pltpu.CompilerParams(vmem_limit_bytes=VMEM_LIMIT),
+        in_specs=[pl.BlockSpec(memory_space=pl.ANY)] * len(operands),
+        out_specs=pl.BlockSpec(memory_space=pltpu.VMEM),
+        out_shape=jax.ShapeDtypeStruct((PARTS, OWN * SUB, STEPS * BLOCK), BF16),
+        scratch_shapes=[pltpu.VMEM(v.shape, BF16) for v in operands]
+        + [
+            pltpu.VMEM((OWN, BLOCK * STEPS, BLOCK * (2 * STEPS - 1)), F32),
+            pltpu.SemaphoreType.DMA((3 * len(pieces),)),
+        ],
+        compiler_params=pltpu.CompilerParams(vmem_limit_bytes=VMEM_CONTRACT),
         cost_estimate=pl.CostEstimate(
-            flops=2 * 4 * 256 * 448 * length, bytes_accessed=6 * 1024 * length, transcendentals=0
+            flops=2 * 4 * 256 * 448 * left.shape[2],
+            bytes_accessed=6 * 1024 * left.shape[2],
+            transcendentals=0,
         ),
         name="contract",
     )(*operands)
@@ -210,19 +222,47 @@
     )(triangle, gate, gain, bias, w_out)
 
 
-def output_gate(pair, in_gain, in_bias, out_gate_w, block):
+def gate_kernel(block_ref, p0, p1, p2, p3, gain_ref, bias_ref, w_ref, out_ref):
+    for k, ref in enumerate((p0, p1, p2, p3)):
+        rows = ref[...].reshape(SUB * BLOCK, 128).astype(F32)
+        centred = rows - jnp.sum(rows, axis=1, keepdims=True) * (1.0 / 128)
+        variance = jnp.sum(centred * centred, axis=1, keepdims=True) * (1.0 / 128)
+        normed = centred * lax.rsqrt(variance + EPS) * gain_ref[...] + bias_ref[...]
+        half = dot(normed.astype(BF16), w_ref[...], ((1,), (0,))) * 0.5
+        out_ref[:, k * BLOCK : (k + 1) * BLOCK, :] = (jnp.tanh(half) * 0.5 + 0.5).reshape(
+            SUB, BLOCK, 128
+        )
+
+
+def output_gate(pair, gain, bias, out_gate_w, block):
     blocks = pair.shape[1] // BLOCK
-    window = jnp.concatenate(
-        [
-            lax.dynamic_slice_in_dim(pair, lax.rem(block + k, blocks) * BLOCK, BLOCK, 1)
+    whole = lambda i, first: (0, 0)
+    spec = pltpu.PrefetchScalarGridSpec(
+        num_scalar_prefetch=1,
+        grid=(1,),
+        in_specs=[
+            pl.BlockSpec(
+                (SUB, BLOCK, 128), lambda i, first, k=k: (0, lax.rem(first[0] + k, blocks), 0)
+            )
             for k in range(STEPS)
+        ]
+        + [
+            pl.BlockSpec((1, 128), whole),
+            pl.BlockSpec((1, 128), whole),
+            pl.BlockSpec((128, 128), whole),
         ],
-        axis=1,
-    ).astype(F32)
-    centred = window - jnp.mean(window, axis=-1, keepdims=True)
-    variance = jnp.mean(centred * centred, axis=-1, keepdims=True)
-    normed = (centred * lax.rsqrt(variance + EPS) * in_gain + in_bias).astype(BF16)
-    return jax.nn.sigmoid(dot(normed, out_gate_w, ((2,), (0,))))
+        out_specs=pl.BlockSpec((SUB, STEPS * BLOCK, 128), lambda i, first: (0, 0, 0)),
+    )
+    return pl.pallas_call(
+        gate_kernel,
+        grid_spec=spec,
+        out_shape=jax.ShapeDtypeStruct((SUB, STEPS * BLOCK, 128), F32),
+        compiler_params=pltpu.CompilerParams(vmem_limit_bytes=VMEM_LIMIT),
+        cost_estimate=pl.CostEstimate(
+            flops=SUB * 256 * 128 * 256, bytes_accessed=2 * 1024 * 1024, transcendentals=2**18
+        ),
+        name="gate",
+    )(block.astype(jnp.int32).reshape(1), pair, pair, pair, pair, gain, bias, out_gate_w)
 
 
 def on_device(
@@ -249,7 +289,8 @@
     left, first_after = lax.optimization_barrier((left, first_after))
     left = spread(left)
     block = lax.axis_index("z") * 4 + lax.axis_index("yhi") * 2 + lax.axis_index("core")
-    gate = output_gate(pair, in_gain, in_bias, out_gate_w, block)
+    gate = output_gate(pair, gain, bias, out_gate_w, block)
+    first, gate = lax.optimization_barrier((first, gate))
     triangle = spread(contract(left, [(first, first_after), (second, second_after)]))
     return finish(triangle, gate, out_gain.reshape(1, 128), out_bias.reshape(1, 128), w_out)
 

time: 166 us -> 162 us (0.976)
  waiting for transfers between devices: 85.7 us -> 68 us
  blocking collectives: 0 us -> 16.9 us
  local copies, waits for them, and re-layouts: 5.91 us -> 16.1 us
  Pallas kernels: 34.2 us -> 27.3 us
  starting transfers between devices: 35 us -> 31.3 us
  matrix products: 1.78 us -> 0 us
    all_to_all x0 -> x1, blocking collectives: none -> 16.9 us  [spread(): return lax.all_to_all(value, PLANE, 0, 0, tiled=True)]
    all_to_all x4 -> x3, waiting for transfers between devices: 28.8 us -> 15.7 us  [spread(): return lax.all_to_all(value, PLANE, 0, 0, tiled=True)]
    unnamed x14 -> x36, local copies, waits for them, and re-layouts: 1.98 us -> 13.3 us
    ppermute x2, waiting for transfers between devices: 56.8 us -> 52.3 us  [shifted(): return lax.ppermute(right[:(STEPS - 1) * BLOCK // SUB], 'z', to_before)]
    all_to_all x4 -> x3, starting transfers between devices: 23.5 us -> 19.5 us  [spread(): return lax.all_to_all(value, PLANE, 0, 0, tiled=True)]
    pallas_call x1 -> x2, Pallas kernels: 9.43 us -> 6.25 us  [the longest x1 5.43 us: contract(): pl.pallas_call(functools.partial(contract_kernel, tuple(steps)), in_specs...]
    pallas_call x3, Pallas kernels: 21.8 us -> 19.5 us  [project(): pl.pallas_call(project_kernel, grid=(length // width,), in_specs=[pl.Bloc...]
    dot_general x1 -> x0, matrix products: 1.78 us -> none  [dot(): return lax.dot_general(a, b, (dims, ((), ())), preferred_element_type=F32)]
  transfers between devices with their start and end apart: 6 -> 5, of which waited for: 6 -> 5; matrix products, arithmetic and copies ran while one was open for 4% -> 2% of each run, Pallas kernels for 10% -> 10%
where the time goes in v3:
time: 162 us; the launch traced here: 160 us
  waiting for transfers between devices  68 us (42%)
  starting transfers between devices  31.3 us (19%)
  Pallas kernels  27.3 us (17%)
  blocking collectives  16.9 us (10%)
  local copies, waits for them, and re-layouts  16.1 us (10%)
    ppermute x2, waiting for transfers between devices, shifted(): return lax.ppermute(right[:(STEPS - 1) * BLOCK // SUB], 'z', to_before)  52.3 us
    all_to_all x3, starting transfers between devices, spread(): return lax.all_to_all(value, PLANE, 0, 0, tiled=True)  19.5 us
    pallas_call x3, Pallas kernels, project(): pl.pallas_call(project_kernel, grid=(length // width,), in_specs=[pl.Bloc...  19.5 us
    all_to_all x1, blocking collectives, spread(): return lax.all_to_all(value, PLANE, 0, 0, tiled=True)  16.9 us
    all_to_all x3, waiting for transfers between devices, spread(): return lax.all_to_all(value, PLANE, 0, 0, tiled=True)  15.7 us
    unnamed x36, local copies, waits for them, and re-layouts  13.3 us
    ppermute x2, starting transfers between devices, shifted(): return lax.ppermute(right[:(STEPS - 1) * BLOCK // SUB], 'z', to_before)  11.8 us
    pallas_call x1, Pallas kernels, contract(): pl.pallas_call(functools.partial(contract_kernel, tuple(steps)), in_specs...  5.43 us
  transfers between devices with their start and end apart: 5, of which 5 were waited for; matrix products, arithmetic and copies ran while one was open for 2% of the time, Pallas kernels for 10%

profile of v3, /device:TPU:8, one launch (start us, length us, event | category | flops | bytes accessed | tf_op | source)
XLA Modules:
  0.0 159.8 jit_solution(2798485545485348779)
XLA Ops:
  0.0 0.0 copy-start.9
  0.0 0.0 copy-start.10
  0.0 0.0 copy-start.11
  0.0 0.0 copy-start.14
  0.0 0.0 copy-start.15
  0.0 4.6 %project.4 = bf16[32,32,640]{2,1,0:T(8,128)(2,1)} custom-call(bf16[8,2048,128]{2,1,0:T(8,128)(2,1)} %pair_ref.5, s32[8,2048]{1,0:T(8,128)} %mask_ref.5, f32[1,128]{1,0:T(1,128)} %bitcast.5, f32[1,128]{1,0:T(1,128)} %bitcast.9, bf16[128,256]{1,0:T(8,128)(2,1)} %value_ref.5, bf16[128,256]{1,0:T(8,128)(2,1)} %gate_ref.5), custom_call_target="tpu_custom_call" | custom-call | flops 503316480 | bytes 2621440 | tf_op jit(solution)/shard_map/project/pallas_call | solution.py:74
  4.6 7.6 %all-to-all-start = ((bf16[32,32,640]{2,1,0:T(8,128)(2,1)}), bf16[32,32,640]{2,1,0:T(8,128)(2,1)}, u32[]{:S(2)}, u32[]{:S(2)}) async-start(bf16[32,32,640]{2,1,0:T(8,128)(2,1)} %project.4), calls=%async_computation | async-start | bytes 2621440 | tf_op jit(solution)/shard_map/all_to_all | solution.py:279
  12.2 0.0 copy-done.9
  12.2 0.0 copy-done.10
  12.2 0.0 copy-done.11
  12.3 0.0 copy-done.14
  12.3 0.0 copy-done.15
  12.3 0.0 copy-start
  12.3 2.2 %copy-done = bf16[8,2048,128]{2,1,0:T(8,128)(2,1)S(1)} copy-done((bf16[8,2048,128]{2,1,0:T(8,128)(2,1)S(1)}, bf16[8,2048,128]{2,1,0:T(8,128)(2,1)}, u32[]{:S(2)}) %copy-start) | copy-done | bytes 4194328
  14.5 7.1 %project.5 = bf16[32,32,1408]{2,1,0:T(8,128)(2,1)S(1)} custom-call(bf16[8,2048,128]{2,1,0:T(8,128)(2,1)S(1)} %copy-done, s32[8,2048]{1,0:T(8,128)S(1)} %copy-done.9, f32[1,128]{1,0:T(1,128)S(1)} %bitcast.6, f32[1,128]{1,0:T(1,128)S(1)} %bitcast.10, bf16[128,256]{1,0:T(8,128)(2,1)S(1)} %copy-done.10, bf16[128,256]{1,0:T(8,128)(2,1)S(1)} %copy-done.11), custom_call_target="tpu_custom_call" | custom-call | flops 1107296256 | bytes 5767168 | tf_op jit(solution)/shard_map/project/pallas_call | solution.py:74
  21.6 0.0 copy-start.4
  21.6 1.5 copy-done.4
  23.2 7.4 %all-to-all-done.rest_0_ = bf16[32,32,640]{2,1,0:T(8,128)(2,1)} async-done(((bf16[32,32,640]{2,1,0:T(8,128)(2,1)}), bf16[32,32,640]{2,1,0:T(8,128)(2,1)}, u32[]{:S(2)}, u32[]{:S(2)}) %all-to-all-start) | async-done | bytes 1310752 | tf_op jit(solution)/shard_map/all_to_all | solution.py:279
  30.5 6.1 %all-to-all-start.2 = ((bf16[32,32,1408]{2,1,0:T(8,128)(2,1)}), bf16[32,32,1408]{2,1,0:T(8,128)(2,1)S(1)}, u32[]{:S(2)}, u32[]{:S(2)}) async-start(bf16[32,32,1408]{2,1,0:T(8,128)(2,1)} %copy-done.4), calls=%async_computation.2 | async-start | bytes 5767168 | tf_op jit(solution)/shard_map/all_to_all | solution.py:279
  36.6 1.3 slice.8
  37.9 5.9 %collective-permute-start = (bf16[24,32,640]{2,1,0:T(8,128)(2,1)S(1)}, bf16[24,32,640]{2,1,0:T(8,128)(2,1)S(1)}, u32[]{:S(2)}, u32[]{:S(2)}) collective-permute-start(bf16[24,32,640]{2,1,0:T(8,128)(2,1)S(1)} %slice.8), channel_id=1, source_target_pairs={{0,28},{4,0},{8,4},{12,8},{16,12},{20,16},{24,20},{28,24},{1,29},{... | collective-permute-start | bytes 2949128 | tf_op jit(solution)/shard_map/ppermute | solution.py:282
  43.8 0.0 copy-start.1
  43.8 2.2 %copy-done.1 = bf16[8,2048,128]{2,1,0:T(8,128)(2,1)S(1)} copy-done((bf16[8,2048,128]{2,1,0:T(8,128)(2,1)S(1)}, bf16[8,2048,128]{2,1,0:T(8,128)(2,1)}, u32[]{:S(2)}) %copy-start.1) | copy-done | bytes 4194328
  46.0 7.7 %project.3 = bf16[32,32,2048]{2,1,0:T(8,128)(2,1)S(1)} custom-call(bf16[8,2048,128]{2,1,0:T(8,128)(2,1)S(1)} %copy-done.1, s32[8,2048]{1,0:T(8,128)S(1)} %copy-done.9, f32[1,128]{1,0:T(1,128)S(1)} %bitcast.7, f32[1,128]{1,0:T(1,128)S(1)} %bitcast.11, bf16[128,256]{1,0:T(8,128)(2,1)S(1)} %copy-done.10, bf16[128,256]{1,0:T(8,128)(2,1)S(1)} %copy-done.11), custom_call_target="tpu_custom_call" | custom-call | flops 1610612736 | bytes 8388608 | tf_op jit(solution)/shard_map/project/pallas_call | solution.py:74
  53.8 0.0 copy-start.3
  53.8 2.0 %copy-done.3 = bf16[32,32,2048]{2,1,0:T(8,128)(2,1)} copy-done((bf16[32,32,2048]{2,1,0:T(8,128)(2,1)}, bf16[32,32,2048]{2,1,0:T(8,128)(2,1)S(1)}, u32[]{:S(2)}) %copy-start.3) | copy-done | bytes 4194328
  55.8 9.4 %collective-permute-done.rest_1_ = bf16[24,32,640]{2,1,0:T(8,128)(2,1)S(1)} collective-permute-done((bf16[24,32,640]{2,1,0:T(8,128)(2,1)S(1)}, bf16[24,32,640]{2,1,0:T(8,128)(2,1)S(1)}, u32[]{:S(2)}, u32[]{:S(2)}) %collective-permute-start) | collective-permute-done | bytes 983072 | tf_op jit(solution)/shard_map/ppermute | solution.py:282
  65.2 1.0 copy-done.7
  66.1 7.8 %all-to-all-done.2.rest_2_ = bf16[32,32,1408]{2,1,0:T(8,128)(2,1)S(1)} async-done(((bf16[32,32,1408]{2,1,0:T(8,128)(2,1)}), bf16[32,32,1408]{2,1,0:T(8,128)(2,1)S(1)}, u32[]{:S(2)}, u32[]{:S(2)}) %all-to-all-start.2) | async-done | bytes 2883616 | tf_op jit(solution)/shard_map/all_to_all | solution.py:279
  73.9 5.8 %all-to-all-start.1 = ((bf16[32,32,2048]{2,1,0:T(8,128)(2,1)}), bf16[32,32,2048]{2,1,0:T(8,128)(2,1)}, u32[]{:S(2)}, u32[]{:S(2)}) async-start(bf16[32,32,2048]{2,1,0:T(8,128)(2,1)} %copy-done.3), calls=%async_computation.1 | async-start | bytes 8388608 | tf_op jit(solution)/shard_map/all_to_all | solution.py:279
  79.8 0.0 copy-start.12
  79.8 1.5 slice.9
  81.3 5.9 %collective-permute-start.1 = (bf16[24,32,1408]{2,1,0:T(8,128)(2,1)}, bf16[24,32,1408]{2,1,0:T(8,128)(2,1)}, u32[]{:S(2)}, u32[]{:S(2)}) collective-permute-start(bf16[24,32,1408]{2,1,0:T(8,128)(2,1)} %slice.9), channel_id=1, source_target_pairs={{0,28},{4,0},{8,4},{12,8},{16,12},{20,16},{24,20},{28,24},{1,29},{... | collective-permute-start | bytes 6488072 | tf_op jit(solution)/shard_map/ppermute | solution.py:282
  87.2 0.0 copy-done.12
  87.2 2.2 %copy-done.2 = bf16[8,2048,128]{2,1,0:T(8,128)(2,1)S(1)} copy-done((bf16[8,2048,128]{2,1,0:T(8,128)(2,1)S(1)}, bf16[8,2048,128]{2,1,0:T(8,128)(2,1)}, u32[]{:S(2)}) %copy-start.2) | copy-done | bytes 4194328
  89.4 0.8 gate.1.gate_ref
  90.2 0.0 copy-start.5
  90.2 1.0 copy-done.5
  91.2 42.9 %collective-permute-done.1.rest_3_ = bf16[24,32,1408]{2,1,0:T(8,128)(2,1)} collective-permute-done((bf16[24,32,1408]{2,1,0:T(8,128)(2,1)}, bf16[24,32,1408]{2,1,0:T(8,128)(2,1)}, u32[]{:S(2)}, u32[]{:S(2)}) %collective-permute-start.1) | collective-permute-done | bytes 2162720 | tf_op jit(solution)/shard_map/ppermute | solution.py:282
  134.1 0.5 all-to-all-done.1.left_hbm
  134.7 1.2 copy-done.8
  135.9 5.4 %contract.1 = bf16[32,32,256]{2,1,0:T(8,128)(2,1)S(1)} custom-call(bf16[32,32,2048]{2,1,0:T(8,128)(2,1)} %all-to-all-done.1.left_hbm, bf16[32,32,640]{2,1,0:T(8,128)(2,1)} %all-to-all-done.rest_0_, bf16[24,32,640]{2,1,0:T(8,128)(2,1)S(1)} %copy-done.8, bf16[32,32,1408]{2,1,0:T(8,128)(2,1)S(1)} %all-to-all-done.2.rest_2_, ...), custom_call_target="tpu_custom_call" | custom-call | flops 1879048192 | bytes 12582912 | tf_op jit(solution)/shard_map/contract/pallas_call | solution.py:163
  141.3 16.9 %all_to_all.20.triangle_ref = bf16[32,32,256]{2,1,0:T(8,128)(2,1)S(1)} all-to-all(bf16[32,32,256]{2,1,0:T(8,128)(2,1)S(1)} %contract.1), channel_id=1, replica_groups=mesh['x'=4,'ylo'=2,'z'=8,'yhi'=2,'core'=2] {'yhi','core','x','ylo'}, dimensions={0} | all-to-all | bytes 1048576 | tf_op jit(solution)/shard_map/all_to_all | solution.py:279
  158.2 0.0 copy-done.13
  158.2 0.0 copy-done.16
  158.2 0.0 copy-done.17
  158.2 0.0 copy-done.6
  158.2 1.6 finish.1
  (7 shorter events, 0.0 us)
Async XLA Ops:
  0.0 12.2 %copy-start.9 = (s32[8,2048]{1,0:T(8,128)S(1)}, s32[8,2048]{1,0:T(8,128)}, u32[]{:S(2)}) copy-start(s32[8,2048]{1,0:T(8,128)} %mask_ref.5) | copy-start | bytes 196612
  0.0 12.2 %copy-start.10 = (bf16[128,256]{1,0:T(8,128)(2,1)S(1)}, bf16[128,256]{1,0:T(8,128)(2,1)}, u32[]{:S(2)}) copy-start(bf16[128,256]{1,0:T(8,128)(2,1)} %value_ref.5) | copy-start | bytes 196612
  0.0 12.2 %copy-start.11 = (bf16[128,256]{1,0:T(8,128)(2,1)S(1)}, bf16[128,256]{1,0:T(8,128)(2,1)}, u32[]{:S(2)}) copy-start(bf16[128,256]{1,0:T(8,128)(2,1)} %gate_ref.5) | copy-start | bytes 196612
  0.0 12.2 %copy-start.14 = (f32[128]{0:T(128)S(1)}, f32[128]{0:T(128)}, u32[]{:S(2)}) copy-start(f32[128]{0:T(128)} %param.12) | copy-start | bytes 1540
  0.0 12.2 %copy-start.15 = (f32[128]{0:T(128)S(1)}, f32[128]{0:T(128)}, u32[]{:S(2)}) copy-start(f32[128]{0:T(128)} %param.13) | copy-start | bytes 1540
  4.6 25.9 %all-to-all-start = ((bf16[32,32,640]{2,1,0:T(8,128)(2,1)}), bf16[32,32,640]{2,1,0:T(8,128)(2,1)}, u32[]{:S(2)}, u32[]{:S(2)}) async-start(bf16[32,32,640]{2,1,0:T(8,128)(2,1)} %project.4), calls=%async_computation | async-start | bytes 2621440 | tf_op jit(solution)/shard_map/all_to_all | solution.py:279
  12.3 2.2 %copy-start = (bf16[8,2048,128]{2,1,0:T(8,128)(2,1)S(1)}, bf16[8,2048,128]{2,1,0:T(8,128)(2,1)}, u32[]{:S(2)}) copy-start(bf16[8,2048,128]{2,1,0:T(8,128)(2,1)} %pair_ref.5) | copy-start | bytes 12582916
  21.6 1.6 copy-start.4
  30.5 43.4 %all-to-all-start.2 = ((bf16[32,32,1408]{2,1,0:T(8,128)(2,1)}), bf16[32,32,1408]{2,1,0:T(8,128)(2,1)S(1)}, u32[]{:S(2)}, u32[]{:S(2)}) async-start(bf16[32,32,1408]{2,1,0:T(8,128)(2,1)} %copy-done.4), calls=%async_computation.2 | async-start | bytes 5767168 | tf_op jit(solution)/shard_map/all_to_all | solution.py:279
  37.9 27.3 %collective-permute-start = (bf16[24,32,640]{2,1,0:T(8,128)(2,1)S(1)}, bf16[24,32,640]{2,1,0:T(8,128)(2,1)S(1)}, u32[]{:S(2)}, u32[]{:S(2)}) collective-permute-start(bf16[24,32,640]{2,1,0:T(8,128)(2,1)S(1)} %slice.8), channel_id=1, source_target_pairs={{0,28},{4,0},{8,4},{12,8},{16,12},{20,16},{24,20},{28,24},{1,29},{... | collective-permute-start | bytes 2949128 | tf_op jit(solution)/shard_map/ppermute | solution.py:282
  43.8 2.2 %copy-start.1 = (bf16[8,2048,128]{2,1,0:T(8,128)(2,1)S(1)}, bf16[8,2048,128]{2,1,0:T(8,128)(2,1)}, u32[]{:S(2)}) copy-start(bf16[8,2048,128]{2,1,0:T(8,128)(2,1)} %pair_ref.5) | copy-start | bytes 12582916
  53.8 2.0 %copy-start.3 = (bf16[32,32,2048]{2,1,0:T(8,128)(2,1)}, bf16[32,32,2048]{2,1,0:T(8,128)(2,1)S(1)}, u32[]{:S(2)}) copy-start(bf16[32,32,2048]{2,1,0:T(8,128)(2,1)S(1)} %project.3) | copy-start | bytes 12582916
  65.2 1.0 copy-start.7
  73.9 60.8 %all-to-all-start.1 = ((bf16[32,32,2048]{2,1,0:T(8,128)(2,1)}), bf16[32,32,2048]{2,1,0:T(8,128)(2,1)}, u32[]{:S(2)}, u32[]{:S(2)}) async-start(bf16[32,32,2048]{2,1,0:T(8,128)(2,1)} %copy-done.3), calls=%async_computation.1 | async-start | bytes 8388608 | tf_op jit(solution)/shard_map/all_to_all | solution.py:279
  79.8 7.4 %copy-start.12 = (bf16[128,128]{1,0:T(8,128)(2,1)S(1)}, bf16[128,128]{1,0:T(8,128)(2,1)}, u32[]{:S(2)}) copy-start(bf16[128,128]{1,0:T(8,128)(2,1)} %w_ref.2) | copy-start | bytes 98308
  81.3 52.8 %collective-permute-start.1 = (bf16[24,32,1408]{2,1,0:T(8,128)(2,1)}, bf16[24,32,1408]{2,1,0:T(8,128)(2,1)}, u32[]{:S(2)}, u32[]{:S(2)}) collective-permute-start(bf16[24,32,1408]{2,1,0:T(8,128)(2,1)} %slice.9), channel_id=1, source_target_pairs={{0,28},{4,0},{8,4},{12,8},{16,12},{20,16},{24,20},{28,24},{1,29},{... | collective-permute-start | bytes 6488072 | tf_op jit(solution)/shard_map/ppermute | solution.py:282
  87.2 2.2 %copy-start.2 = (bf16[8,2048,128]{2,1,0:T(8,128)(2,1)S(1)}, bf16[8,2048,128]{2,1,0:T(8,128)(2,1)}, u32[]{:S(2)}) copy-start(bf16[8,2048,128]{2,1,0:T(8,128)(2,1)} %pair_ref.5) | copy-start | bytes 12582916
  89.4 68.8 %copy-start.13 = (bf16[128,128]{1,0:T(8,128)(2,1)S(1)}, bf16[128,128]{1,0:T(8,128)(2,1)}, u32[]{:S(2)}) copy-start(bf16[128,128]{1,0:T(8,128)(2,1)} %w_ref.3) | copy-start | bytes 98308
  89.4 68.8 %copy-start.16 = (f32[128]{0:T(128)S(1)}, f32[128]{0:T(128)}, u32[]{:S(2)}) copy-start(f32[128]{0:T(128)} %param.17) | copy-start | bytes 1540
  89.4 68.8 %copy-start.17 = (f32[128]{0:T(128)S(1)}, f32[128]{0:T(128)}, u32[]{:S(2)}) copy-start(f32[128]{0:T(128)} %param.18) | copy-start | bytes 1540
  90.2 1.0 copy-start.5
  134.7 1.2 copy-start.8
  135.9 22.3 %copy-start.6 = (f32[8,256,128]{2,1,0:T(8,128)S(1)}, f32[8,256,128]{2,1,0:T(8,128)}, u32[]{:S(2)}) copy-start(f32[8,256,128]{2,1,0:T(8,128)} %copy-done.5) | copy-start | bytes 3145732

commit v4 on v3

--- a/solution.py
+++ b/solution.py
@@ -14,14 +14,13 @@
 PLANE = ("yhi", "core", "x", "ylo")
 PARTS = 32
 OWN = 4
-RIGHTS = ((0, 640), (640, 1408))
+RIGHTS = ((0, 768), (768, 1280))
 CHUNK = 128
 STRIDE = 136
 F32 = jnp.float32
 BF16 = jnp.bfloat16
-VMEM_LIMIT = 24 * 1024 * 1024
-VMEM_CONTRACT = 36 * 1024 * 1024
-VMEM_FIRST = 60 * 1024 * 1024
+VMEM_LIMIT = 60 * 1024 * 1024
+VMEM_SMALL = 24 * 1024 * 1024
 
 
 def dot(a, b, dims):
@@ -36,37 +35,40 @@
     return jnp.concatenate([block] * (width // 128), axis=1)
 
 
-def project_kernel(pair_ref, mask_ref, gain_ref, bias_ref, value_ref, gate_ref, out_ref, mixed):
-    width = pair_ref.shape[1]
+def projection(gain_ref, bias_ref, value_ref, gate_ref):
     gain = across(columns(gain_ref[...]), CHUNK)
     bias = across(columns(bias_ref[...]), CHUNK)
     value_t = jnp.transpose(value_ref[...].astype(F32)).astype(BF16)
     gate_t = jnp.transpose(gate_ref[...].astype(F32) * 0.5).astype(BF16)
-    weight = jnp.concatenate([value_t, gate_t], axis=0)
-    for start in range(0, width, CHUNK):
-        for row in range(SUB):
-            turned = jnp.transpose(pair_ref[row, start : start + CHUNK, :]).astype(F32)
-            half_mask = mask_ref[row : row + 1, start : start + CHUNK].astype(F32) * 0.5
-            centred = turned - jnp.sum(turned, axis=0, keepdims=True) * (1.0 / 128)
-            variance = jnp.sum(centred * centred, axis=0, keepdims=True) * (1.0 / 128)
-            normed = (centred * lax.rsqrt(variance + EPS) * gain + bias).astype(BF16)
-            both = dot(weight, normed, ((1,), (0,)))
-            half = both[:128] * half_mask
-            result = half + half * jnp.tanh(both[128:])
-            for tile in range(CHUNK // 128):
-                first = ((start // 128 + tile) * SUB + row) * STRIDE
-                mixed[first : first + 128, :] = result[:, tile * 128 : (tile + 1) * 128]
-        for tile in range(start // 128, (start + CHUNK) // 128):
-            for part in range(PARTS):
-                first = tile * SUB * STRIDE + part * OWN
-                pieces = [mixed[pl.ds(first + k, SUB, stride=STRIDE), :] for k in range(OWN)]
-                out_ref[part, :, tile * 128 : (tile + 1) * 128] = jnp.concatenate(
-                    pieces, axis=0
-                ).astype(BF16)
+    return gain, bias, jnp.concatenate([value_t, gate_t], axis=0)
+
+
+def project_chunk(params, pair_ref, mask_ref, out_ref, mixed, start):
+    gain, bias, weight = params
+    for row in range(SUB):
+        turned = jnp.transpose(pair_ref[row, start : start + CHUNK, :]).astype(F32)
+        half_mask = mask_ref[row : row + 1, start : start + CHUNK].astype(F32) * 0.5
+        centred = turned - jnp.sum(turned, axis=0, keepdims=True) * (1.0 / 128)
+        variance = jnp.sum(centred * centred, axis=0, keepdims=True) * (1.0 / 128)
+        normed = (centred * lax.rsqrt(variance + EPS) * gain + bias).astype(BF16)
+        both = dot(weight, normed, ((1,), (0,)))
+        half = both[:128] * half_mask
+        first = (start // CHUNK * SUB + row) * STRIDE
+        mixed[first : first + 128, :] = half + half * jnp.tanh(both[128:])
+    for part in range(PARTS):
+        first = start // CHUNK * SUB * STRIDE + part * OWN
+        pieces = [mixed[pl.ds(first + k, SUB, stride=STRIDE), :] for k in range(OWN)]
+        out_ref[part, :, start : start + CHUNK] = jnp.concatenate(pieces, axis=0).astype(BF16)
+
+
+def project_kernel(pair_ref, mask_ref, gain_ref, bias_ref, value_ref, gate_ref, out_ref, mixed):
+    params = projection(gain_ref, bias_ref, value_ref, gate_ref)
+    for start in range(0, pair_ref.shape[1], CHUNK):
+        project_chunk(params, pair_ref, mask_ref, out_ref, mixed, start)
 
 
 def project(pair, mask, gain, bias, w_value, w_gate, side, start, length):
-    width = max(w for w in range(128, 641, 128) if start % w == 0 and length % w == 0)
+    width = max(w for w in range(CHUNK, 513, CHUNK) if start % w == 0 and length % w == 0)
     first = start // width
     whole = lambda i: (0, 0)
     column = lambda i: (0, side)
@@ -84,9 +86,9 @@
         ],
         out_specs=pl.BlockSpec((PARTS, OWN * SUB, width), lambda i: (0, 0, i)),
         out_shape=jax.ShapeDtypeStruct((PARTS, OWN * SUB, length), BF16),
-        scratch_shapes=[pltpu.VMEM((SUB * STRIDE * (width // 128), 128), F32)],
+        scratch_shapes=[pltpu.VMEM((SUB * STRIDE * (width // CHUNK), 128), F32)],
         compiler_params=pltpu.CompilerParams(
-            vmem_limit_bytes=VMEM_FIRST if side == 1 and start == 0 else VMEM_LIMIT
+            vmem_limit_bytes=VMEM_LIMIT if side == 1 and start == 0 else VMEM_SMALL
         ),
         cost_estimate=pl.CostEstimate(
             flops=tokens * 128 * 384 * 2, bytes_accessed=tokens * 512, transcendentals=tokens * 128
@@ -105,29 +107,33 @@
 
 
 def contract_kernel(steps, left_hbm, *rest):
-    count = len(steps)
+    count, halves = len(steps), OWN // 2
     pieces, out_ref, left_ref = rest[: 2 * count], rest[2 * count], rest[2 * count + 1]
     held = rest[2 * count + 2 : 4 * count + 2]
     total, sems = rest[4 * count + 2 :]
-    copies = []
+    copies = {}
     for k, (begin, length) in enumerate(steps):
         tokens = pl.ds(begin, length)
-        mine = [
-            pltpu.make_async_copy(
-                left_hbm.at[:, :, tokens], left_ref.at[:, :, tokens], sems.at[3 * k]
-            )
-        ] + [
-            pltpu.make_async_copy(pieces[2 * k + j], held[2 * k + j], sems.at[3 * k + 1 + j])
-            for j in range(2)
-        ]
-        for copy in mine:
-            copy.start()
-        copies.append(mine)
+        for half in range(halves):
+            rows = pl.ds(half * 16, 16)
+            sem = 3 * (k * halves + half)
+            copies[k, half] = [
+                pltpu.make_async_copy(
+                    left_hbm.at[:, rows, tokens], left_ref.at[:, rows, tokens], sems.at[sem]
+                )
+            ] + [
+                pltpu.make_async_copy(
+                    pieces[2 * k + j].at[:, rows, :], held[2 * k + j].at[:, rows, :], sems.at[sem + 1 + j]
+                )
+                for j in range(2)
+            ]
+            for copy in copies[k, half]:
+                copy.start()
     groups = BLOCK // SUB
     for k, (begin, length) in enumerate(steps):
-        for copy in copies[k]:
-            copy.wait()
-        for pair_of_channels in range(OWN // 2):
+        for pair_of_channels in range(halves):
+            for copy in copies[k, pair_of_channels]:
+                copy.wait()
             left = rows_of(left_ref.at[:, :, pl.ds(begin, length)], pair_of_channels)
             right = rows_of(held[2 * k], pair_of_channels)
             after = rows_of(held[2 * k + 1], pair_of_channels)
@@ -162,15 +168,15 @@
         begin += right.shape[2]
     return pl.pallas_call(
         functools.partial(contract_kernel, tuple(steps)),
-        in_specs=[pl.BlockSpec(memory_space=pl.ANY)] * len(operands),
+        in_specs=[pl.BlockSpec(memory_space=pltpu.HBM)] * len(operands),
         out_specs=pl.BlockSpec(memory_space=pltpu.VMEM),
         out_shape=jax.ShapeDtypeStruct((PARTS, OWN * SUB, STEPS * BLOCK), BF16),
         scratch_shapes=[pltpu.VMEM(v.shape, BF16) for v in operands]
         + [
             pltpu.VMEM((OWN, BLOCK * STEPS, BLOCK * (2 * STEPS - 1)), F32),
-            pltpu.SemaphoreType.DMA((3 * len(pieces),)),
+            pltpu.SemaphoreType.DMA((3 * OWN // 2 * len(pieces),)),
         ],
-        compiler_params=pltpu.CompilerParams(vmem_limit_bytes=VMEM_CONTRACT),
+        compiler_params=pltpu.CompilerParams(vmem_limit_bytes=VMEM_LIMIT),
         cost_estimate=pl.CostEstimate(
             flops=2 * 4 * 256 * 448 * left.shape[2],
             bytes_accessed=6 * 1024 * left.shape[2],
@@ -214,7 +220,7 @@
         out_specs=pl.BlockSpec((SUB, width, 128), lambda i: (0, i, 0)),
         out_shape=jax.ShapeDtypeStruct((SUB, STEPS * BLOCK, 128), BF16),
         scratch_shapes=[pltpu.VMEM((SUB * width, 128), F32)],
-        compiler_params=pltpu.CompilerParams(vmem_limit_bytes=VMEM_LIMIT),
+        compiler_params=pltpu.CompilerParams(vmem_limit_bytes=VMEM_SMALL),
         cost_estimate=pl.CostEstimate(
             flops=SUB * 256 * 128 * 256, bytes_accessed=2 * 1024 * 1024, transcendentals=2048
         ),
@@ -257,7 +263,7 @@
         gate_kernel,
         grid_spec=spec,
         out_shape=jax.ShapeDtypeStruct((SUB, STEPS * BLOCK, 128), F32),
-        compiler_params=pltpu.CompilerParams(vmem_limit_bytes=VMEM_LIMIT),
+        compiler_params=pltpu.CompilerParams(vmem_limit_bytes=VMEM_SMALL),
         cost_estimate=pl.CostEstimate(
             flops=SUB * 256 * 128 * 256, bytes_accessed=2 * 1024 * 1024, transcendentals=2**18
         ),
@@ -289,9 +295,10 @@
     left, first_after = lax.optimization_barrier((left, first_after))
     left = spread(left)
     block = lax.axis_index("z") * 4 + lax.axis_index("yhi") * 2 + lax.axis_index("core")
+    band = contract(left, [(first, first_after), (second, second_after)])
+    band, block = lax.optimization_barrier((band, block))
     gate = output_gate(pair, gain, bias, out_gate_w, block)
-    first, gate = lax.optimization_barrier((first, gate))
-    triangle = spread(contract(left, [(first, first_after), (second, second_after)]))
+    triangle = spread(band)
     return finish(triangle, gate, out_gain.reshape(1, 128), out_bias.reshape(1, 128), w_out)
 
 

time: 162 us -> 161 us (level)
  blocking collectives: 16.9 us -> 0 us
  waiting for transfers between devices: 68 us -> 83 us
  starting transfers between devices: 31.3 us -> 37 us
  local copies, waits for them, and re-layouts: 16.1 us -> 11.7 us
    all_to_all x1 -> x0, blocking collectives: 16.9 us -> none  [spread(): return lax.all_to_all(value, PLANE, 0, 0, tiled=True)]
    all_to_all x3 -> x4, waiting for transfers between devices: 15.7 us -> 26.6 us  [spread(): return lax.all_to_all(value, PLANE, 0, 0, tiled=True)]
    all_to_all x3 -> x4, starting transfers between devices: 19.5 us -> 25.2 us  [spread(): return lax.all_to_all(value, PLANE, 0, 0, tiled=True)]
    unnamed x36 -> x32, local copies, waits for them, and re-layouts: 13.3 us -> 8.61 us
    ppermute x2, waiting for transfers between devices: 52.3 us -> 56.3 us  [shifted(): return lax.ppermute(right[:(STEPS - 1) * BLOCK // SUB], 'z', to_before)]
  transfers between devices with their start and end apart: 5 -> 6, of which waited for: 5 -> 6; matrix products, arithmetic and copies ran while one was open for 2% -> 2% of each run, Pallas kernels for 10% -> 9%
where the time goes in v4:
time: 161 us; the launch traced here: 159 us
  waiting for transfers between devices  83 us (52%)
  starting transfers between devices  37 us (23%)
  Pallas kernels  26.9 us (17%)
  local copies, waits for them, and re-layouts  11.7 us (7%)
    ppermute x2, waiting for transfers between devices, shifted(): return lax.ppermute(right[:(STEPS - 1) * BLOCK // SUB], 'z', to_before)  56.3 us
    all_to_all x4, waiting for transfers between devices, spread(): return lax.all_to_all(value, PLANE, 0, 0, tiled=True)  26.6 us
    all_to_all x4, starting transfers between devices, spread(): return lax.all_to_all(value, PLANE, 0, 0, tiled=True)  25.2 us
    pallas_call x3, Pallas kernels, project(): pl.pallas_call(project_kernel, grid=(length // width,), in_specs=[pl.Bloc...  18.3 us
    ppermute x2, starting transfers between devices, shifted(): return lax.ppermute(right[:(STEPS - 1) * BLOCK // SUB], 'z', to_before)  11.8 us
    unnamed x32, local copies, waits for them, and re-layouts  8.61 us
    pallas_call x1, Pallas kernels, contract(): pl.pallas_call(functools.partial(contract_kernel, tuple(steps)), in_specs...  6.17 us
  transfers between devices with their start and end apart: 6, of which 6 were waited for; matrix products, arithmetic and copies ran while one was open for 2% of the time, Pallas kernels for 9%

profile of v4, /device:TPU:8, one launch (start us, length us, event | category | flops | bytes accessed | tf_op | source)
XLA Modules:
  0.0 158.7 jit_solution(17202459427285328232)
XLA Ops:
  0.0 4.8 %project.4 = bf16[32,32,768]{2,1,0:T(8,128)(2,1)} custom-call(bf16[8,2048,128]{2,1,0:T(8,128)(2,1)} %p3.1, s32[8,2048]{1,0:T(8,128)} %mask_ref.5, f32[1,128]{1,0:T(1,128)} %bitcast.5, f32[1,128]{1,0:T(1,128)} %bitcast.9, bf16[128,256]{1,0:T(8,128)(2,1)} %value_ref.5, bf16[128,256]{1,0:T(8,128)(2,1)} %gate_ref.5), custom_call_target="tpu_custom_call" | custom-call | flops 603979776 | bytes 3145728 | tf_op jit(solution)/shard_map/project/pallas_call | solution.py:76
  4.8 0.0 copy-start.4
  4.8 0.0 copy-start.6
  4.8 0.0 copy-start.9
  4.8 0.0 copy-start.10
  4.8 7.7 %all-to-all-start = ((bf16[32,32,768]{2,1,0:T(8,128)(2,1)}), bf16[32,32,768]{2,1,0:T(8,128)(2,1)S(1)}, u32[]{:S(2)}, u32[]{:S(2)}) async-start(bf16[32,32,768]{2,1,0:T(8,128)(2,1)} %project.4), calls=%async_computation | async-start | bytes 3145728 | tf_op jit(solution)/shard_map/all_to_all | solution.py:285
  12.5 0.0 copy-done.4
  12.5 0.0 copy-done.5
  12.5 0.0 copy-done.6
  12.6 0.0 copy-done.9
  12.6 0.0 copy-done.10
  12.6 0.0 copy-start
  12.6 2.2 %copy-done = bf16[8,2048,128]{2,1,0:T(8,128)(2,1)S(1)} copy-done((bf16[8,2048,128]{2,1,0:T(8,128)(2,1)S(1)}, bf16[8,2048,128]{2,1,0:T(8,128)(2,1)}, u32[]{:S(2)}) %copy-start) | copy-done | bytes 4194328
  14.8 5.8 %project.5 = bf16[32,32,1280]{2,1,0:T(8,128)(2,1)} custom-call(bf16[8,2048,128]{2,1,0:T(8,128)(2,1)S(1)} %copy-done, s32[8,2048]{1,0:T(8,128)S(1)} %copy-done.4, f32[1,128]{1,0:T(1,128)S(1)} %bitcast.6, f32[1,128]{1,0:T(1,128)S(1)} %bitcast.10, bf16[128,256]{1,0:T(8,128)(2,1)S(1)} %copy-done.5, bf16[128,256]{1,0:T(8,128)(2,1)S(1)} %copy-done.6), custom_call_target="tpu_custom_call" | custom-call | flops 1006632960 | bytes 5242880 | tf_op jit(solution)/shard_map/project/pallas_call | solution.py:76
  20.5 13.4 %all-to-all-done.rest_0_ = bf16[32,32,768]{2,1,0:T(8,128)(2,1)S(1)} async-done(((bf16[32,32,768]{2,1,0:T(8,128)(2,1)}), bf16[32,32,768]{2,1,0:T(8,128)(2,1)S(1)}, u32[]{:S(2)}, u32[]{:S(2)}) %all-to-all-start) | async-done | bytes 1572896 | tf_op jit(solution)/shard_map/all_to_all | solution.py:285
  33.9 0.0 copy-start.13
  33.9 6.2 %all-to-all-start.2 = ((bf16[32,32,1280]{2,1,0:T(8,128)(2,1)}), bf16[32,32,1280]{2,1,0:T(8,128)(2,1)}, u32[]{:S(2)}, u32[]{:S(2)}) async-start(bf16[32,32,1280]{2,1,0:T(8,128)(2,1)} %project.5), calls=%async_computation.2 | async-start | bytes 5242880 | tf_op jit(solution)/shard_map/all_to_all | solution.py:285
  40.1 0.0 copy-done.13
  40.2 0.1 slice.8
  40.2 5.9 %collective-permute-start = (bf16[24,32,768]{2,1,0:T(8,128)(2,1)S(1)}, bf16[24,32,768]{2,1,0:T(8,128)(2,1)S(1)}, u32[]{:S(2)}, u32[]{:S(2)}) collective-permute-start(bf16[24,32,768]{2,1,0:T(8,128)(2,1)S(1)} %slice.8), channel_id=1, source_target_pairs={{0,28},{4,0},{8,4},{12,8},{16,12},{20,16},{24,20},{28,24},{1,29},{... | collective-permute-start | bytes 3538952 | tf_op jit(solution)/shard_map/ppermute | solution.py:288
  46.2 0.0 copy-start.1
  46.2 2.2 %copy-done.1 = bf16[8,2048,128]{2,1,0:T(8,128)(2,1)S(1)} copy-done((bf16[8,2048,128]{2,1,0:T(8,128)(2,1)S(1)}, bf16[8,2048,128]{2,1,0:T(8,128)(2,1)}, u32[]{:S(2)}) %copy-start.1) | copy-done | bytes 4194328
  48.4 7.7 %project.3 = bf16[32,32,2048]{2,1,0:T(8,128)(2,1)S(1)} custom-call(bf16[8,2048,128]{2,1,0:T(8,128)(2,1)S(1)} %copy-done.1, s32[8,2048]{1,0:T(8,128)S(1)} %copy-done.4, f32[1,128]{1,0:T(1,128)S(1)} %bitcast.7, f32[1,128]{1,0:T(1,128)S(1)} %bitcast.11, bf16[128,256]{1,0:T(8,128)(2,1)S(1)} %copy-done.5, bf16[128,256]{1,0:T(8,128)(2,1)S(1)} %copy-done.6), custom_call_target="tpu_custom_call" | custom-call | flops 1610612736 | bytes 8388608 | tf_op jit(solution)/shard_map/project/pallas_call | solution.py:76
  56.1 0.0 copy-start.3
  56.1 2.0 %copy-done.3 = bf16[32,32,2048]{2,1,0:T(8,128)(2,1)} copy-done((bf16[32,32,2048]{2,1,0:T(8,128)(2,1)}, bf16[32,32,2048]{2,1,0:T(8,128)(2,1)S(1)}, u32[]{:S(2)}) %copy-start.3) | copy-done | bytes 4194328
  58.1 13.6 %collective-permute-done.rest_1_ = bf16[24,32,768]{2,1,0:T(8,128)(2,1)S(1)} collective-permute-done((bf16[24,32,768]{2,1,0:T(8,128)(2,1)S(1)}, bf16[24,32,768]{2,1,0:T(8,128)(2,1)S(1)}, u32[]{:S(2)}, u32[]{:S(2)}) %collective-permute-start) | collective-permute-done | bytes 1179680 | tf_op jit(solution)/shard_map/ppermute | solution.py:288
  71.7 0.0 copy-start.15
  71.7 2.8 %all-to-all-done.2.rest_2_ = bf16[32,32,1280]{2,1,0:T(8,128)(2,1)} async-done(((bf16[32,32,1280]{2,1,0:T(8,128)(2,1)}), bf16[32,32,1280]{2,1,0:T(8,128)(2,1)}, u32[]{:S(2)}, u32[]{:S(2)}) %all-to-all-start.2) | async-done | bytes 2621472 | tf_op jit(solution)/shard_map/all_to_all | solution.py:285
  74.6 0.0 copy-done.15
  74.6 5.8 %all-to-all-start.1 = ((bf16[32,32,2048]{2,1,0:T(8,128)(2,1)}), bf16[32,32,2048]{2,1,0:T(8,128)(2,1)}, u32[]{:S(2)}, u32[]{:S(2)}) async-start(bf16[32,32,2048]{2,1,0:T(8,128)(2,1)} %copy-done.3), calls=%async_computation.1 | async-start | bytes 8388608 | tf_op jit(solution)/shard_map/all_to_all | solution.py:285
  80.3 3.0 %slice.9 = bf16[24,32,1280]{2,1,0:T(8,128)(2,1)} slice(bf16[32,32,1280]{2,1,0:T(8,128)(2,1)} %all-to-all-done.2.rest_2_), slice={[0:24], [0:32], [0:1280]} | slice | bytes 3932160 | tf_op jit(solution)/shard_map/slice | solution.py:288
  83.4 5.8 %collective-permute-start.1 = (bf16[24,32,1280]{2,1,0:T(8,128)(2,1)}, bf16[24,32,1280]{2,1,0:T(8,128)(2,1)S(1)}, u32[]{:S(2)}, u32[]{:S(2)}) collective-permute-start(bf16[24,32,1280]{2,1,0:T(8,128)(2,1)} %slice.9), channel_id=1, source_target_pairs={{0,28},{4,0},{8,4},{12,8},{16,12},{20,16},{24,20},{28,24},{1,29},{... | collective-permute-start | bytes 5898248 | tf_op jit(solution)/shard_map/ppermute | solution.py:288
  89.2 0.0 copy-start.7
  89.2 42.7 %collective-permute-done.1.rest_3_ = bf16[24,32,1280]{2,1,0:T(8,128)(2,1)S(1)} collective-permute-done((bf16[24,32,1280]{2,1,0:T(8,128)(2,1)}, bf16[24,32,1280]{2,1,0:T(8,128)(2,1)S(1)}, u32[]{:S(2)}, u32[]{:S(2)}) %collective-permute-start.1) | collective-permute-done | bytes 1966112 | tf_op jit(solution)/shard_map/ppermute | solution.py:288
  131.9 0.0 copy-start.14
  131.9 3.3 %all-to-all-done.1.left_hbm = bf16[32,32,2048]{2,1,0:T(8,128)(2,1)} async-done(((bf16[32,32,2048]{2,1,0:T(8,128)(2,1)}), bf16[32,32,2048]{2,1,0:T(8,128)(2,1)}, u32[]{:S(2)}, u32[]{:S(2)}) %all-to-all-start.1) | async-done | bytes 4194336 | tf_op jit(solution)/shard_map/all_to_all | solution.py:285
  135.2 0.0 copy-done.14
  135.2 6.2 %contract.1 = bf16[32,32,256]{2,1,0:T(8,128)(2,1)} custom-call(bf16[32,32,2048]{2,1,0:T(8,128)(2,1)} %all-to-all-done.1.left_hbm, bf16[32,32,768]{2,1,0:T(8,128)(2,1)} %copy-done.13, bf16[24,32,768]{2,1,0:T(8,128)(2,1)} %copy-done.15, bf16[32,32,1280]{2,1,0:T(8,128)(2,1)} %all-to-all-done.2.rest_2_, bf16[24,32,1280]{2,1,0:T(8,128)(2,1)} %copy-done.14), custom_call_target="tpu_custom_call" | custom-call | flops 1879048192 | bytes 12582912 | tf_op jit(solution)/shard_map/contract/pallas_call | solution.py:169
  141.4 5.6 %all-to-all-start.3 = ((bf16[32,32,256]{2,1,0:T(8,128)(2,1)}), bf16[32,32,256]{2,1,0:T(8,128)(2,1)S(1)}, u32[]{:S(2)}, u32[]{:S(2)}) async-start(bf16[32,32,256]{2,1,0:T(8,128)(2,1)} %contract.1), calls=%async_computation.3 | async-start | bytes 1048576 | tf_op jit(solution)/shard_map/all_to_all | solution.py:285
  147.0 0.0 copy-done.7
  147.0 0.0 copy-start.2
  147.0 2.2 %copy-done.2 = bf16[8,2048,128]{2,1,0:T(8,128)(2,1)S(1)} copy-done((bf16[8,2048,128]{2,1,0:T(8,128)(2,1)S(1)}, bf16[8,2048,128]{2,1,0:T(8,128)(2,1)}, u32[]{:S(2)}) %copy-start.2) | copy-done | bytes 4194328
  149.2 0.8 gate.1.gate_ref
  150.0 7.1 %all-to-all-done.3.triangle_ref = bf16[32,32,256]{2,1,0:T(8,128)(2,1)S(1)} async-done(((bf16[32,32,256]{2,1,0:T(8,128)(2,1)}), bf16[32,32,256]{2,1,0:T(8,128)(2,1)S(1)}, u32[]{:S(2)}, u32[]{:S(2)}) %all-to-all-start.3) | async-done | bytes 524320 | tf_op jit(solution)/shard_map/all_to_all | solution.py:285
  157.1 0.0 copy-done.8
  157.1 0.0 copy-done.11
  157.1 0.0 copy-done.12
  157.1 1.6 %finish.1 = bf16[8,256,128]{2,1,0:T(8,128)(2,1)} custom-call(bf16[32,32,256]{2,1,0:T(8,128)(2,1)S(1)} %all-to-all-done.3.triangle_ref, f32[8,256,128]{2,1,0:T(8,128)S(1)} %gate.1.gate_ref, f32[1,128]{1,0:T(1,128)S(1)} %bitcast.13, f32[1,128]{1,0:T(1,128)S(1)} %bitcast.14, bf16[128,128]{1,0:T(8,128)(2,1)S(1)} %copy-done.8), custom_call_target="tpu_custom_call" | custom-call | flops 67108864 | bytes 2097152 | tf_op jit(solution)/shard_map/finish/pallas_call | solution.py:210
  (4 shorter events, 0.0 us)
Async XLA Ops:
  4.8 7.7 %copy-start.4 = (s32[8,2048]{1,0:T(8,128)S(1)}, s32[8,2048]{1,0:T(8,128)}, u32[]{:S(2)}) copy-start(s32[8,2048]{1,0:T(8,128)} %mask_ref.5) | copy-start | bytes 196612
  4.8 7.7 %copy-start.5 = (bf16[128,256]{1,0:T(8,128)(2,1)S(1)}, bf16[128,256]{1,0:T(8,128)(2,1)}, u32[]{:S(2)}) copy-start(bf16[128,256]{1,0:T(8,128)(2,1)} %value_ref.5) | copy-start | bytes 196612
  4.8 7.7 %copy-start.6 = (bf16[128,256]{1,0:T(8,128)(2,1)S(1)}, bf16[128,256]{1,0:T(8,128)(2,1)}, u32[]{:S(2)}) copy-start(bf16[128,256]{1,0:T(8,128)(2,1)} %gate_ref.5) | copy-start | bytes 196612
  4.8 7.7 %copy-start.9 = (f32[128]{0:T(128)S(1)}, f32[128]{0:T(128)}, u32[]{:S(2)}) copy-start(f32[128]{0:T(128)} %param.12) | copy-start | bytes 1540
  4.8 7.7 %copy-start.10 = (f32[128]{0:T(128)S(1)}, f32[128]{0:T(128)}, u32[]{:S(2)}) copy-start(f32[128]{0:T(128)} %param.13) | copy-start | bytes 1540
  4.8 29.1 %all-to-all-start = ((bf16[32,32,768]{2,1,0:T(8,128)(2,1)}), bf16[32,32,768]{2,1,0:T(8,128)(2,1)S(1)}, u32[]{:S(2)}, u32[]{:S(2)}) async-start(bf16[32,32,768]{2,1,0:T(8,128)(2,1)} %project.4), calls=%async_computation | async-start | bytes 3145728 | tf_op jit(solution)/shard_map/all_to_all | solution.py:285
  12.6 2.2 %copy-start = (bf16[8,2048,128]{2,1,0:T(8,128)(2,1)S(1)}, bf16[8,2048,128]{2,1,0:T(8,128)(2,1)}, u32[]{:S(2)}) copy-start(bf16[8,2048,128]{2,1,0:T(8,128)(2,1)} %p3.1) | copy-start | bytes 12582916
  33.9 6.2 %copy-start.13 = (bf16[32,32,768]{2,1,0:T(8,128)(2,1)}, bf16[32,32,768]{2,1,0:T(8,128)(2,1)S(1)}, u32[]{:S(2)}) copy-start(bf16[32,32,768]{2,1,0:T(8,128)(2,1)S(1)} %all-to-all-done.rest_0_) | copy-start | bytes 4718596
  33.9 40.6 %all-to-all-start.2 = ((bf16[32,32,1280]{2,1,0:T(8,128)(2,1)}), bf16[32,32,1280]{2,1,0:T(8,128)(2,1)}, u32[]{:S(2)}, u32[]{:S(2)}) async-start(bf16[32,32,1280]{2,1,0:T(8,128)(2,1)} %project.5), calls=%async_computation.2 | async-start | bytes 5242880 | tf_op jit(solution)/shard_map/all_to_all | solution.py:285
  40.2 31.5 %collective-permute-start = (bf16[24,32,768]{2,1,0:T(8,128)(2,1)S(1)}, bf16[24,32,768]{2,1,0:T(8,128)(2,1)S(1)}, u32[]{:S(2)}, u32[]{:S(2)}) collective-permute-start(bf16[24,32,768]{2,1,0:T(8,128)(2,1)S(1)} %slice.8), channel_id=1, source_target_pairs={{0,28},{4,0},{8,4},{12,8},{16,12},{20,16},{24,20},{28,24},{1,29},{... | collective-permute-start | bytes 3538952 | tf_op jit(solution)/shard_map/ppermute | solution.py:288
  46.2 2.2 %copy-start.1 = (bf16[8,2048,128]{2,1,0:T(8,128)(2,1)S(1)}, bf16[8,2048,128]{2,1,0:T(8,128)(2,1)}, u32[]{:S(2)}) copy-start(bf16[8,2048,128]{2,1,0:T(8,128)(2,1)} %p3.1) | copy-start | bytes 12582916
  56.1 2.0 %copy-start.3 = (bf16[32,32,2048]{2,1,0:T(8,128)(2,1)}, bf16[32,32,2048]{2,1,0:T(8,128)(2,1)S(1)}, u32[]{:S(2)}) copy-start(bf16[32,32,2048]{2,1,0:T(8,128)(2,1)S(1)} %project.3) | copy-start | bytes 12582916
  71.7 2.8 %copy-start.15 = (bf16[24,32,768]{2,1,0:T(8,128)(2,1)}, bf16[24,32,768]{2,1,0:T(8,128)(2,1)S(1)}, u32[]{:S(2)}) copy-start(bf16[24,32,768]{2,1,0:T(8,128)(2,1)S(1)} %collective-permute-done.rest_1_) | copy-start | bytes 3538948
  74.6 60.7 %all-to-all-start.1 = ((bf16[32,32,2048]{2,1,0:T(8,128)(2,1)}), bf16[32,32,2048]{2,1,0:T(8,128)(2,1)}, u32[]{:S(2)}, u32[]{:S(2)}) async-start(bf16[32,32,2048]{2,1,0:T(8,128)(2,1)} %copy-done.3), calls=%async_computation.1 | async-start | bytes 8388608 | tf_op jit(solution)/shard_map/all_to_all | solution.py:285
  83.4 48.6 %collective-permute-start.1 = (bf16[24,32,1280]{2,1,0:T(8,128)(2,1)}, bf16[24,32,1280]{2,1,0:T(8,128)(2,1)S(1)}, u32[]{:S(2)}, u32[]{:S(2)}) collective-permute-start(bf16[24,32,1280]{2,1,0:T(8,128)(2,1)} %slice.9), channel_id=1, source_target_pairs={{0,28},{4,0},{8,4},{12,8},{16,12},{20,16},{24,20},{28,24},{1,29},{... | collective-permute-start | bytes 5898248 | tf_op jit(solution)/shard_map/ppermute | solution.py:288
  89.2 57.8 %copy-start.7 = (bf16[128,128]{1,0:T(8,128)(2,1)S(1)}, bf16[128,128]{1,0:T(8,128)(2,1)}, u32[]{:S(2)}) copy-start(bf16[128,128]{1,0:T(8,128)(2,1)} %w_ref.2) | copy-start | bytes 98308
  131.9 3.3 %copy-start.14 = (bf16[24,32,1280]{2,1,0:T(8,128)(2,1)}, bf16[24,32,1280]{2,1,0:T(8,128)(2,1)S(1)}, u32[]{:S(2)}) copy-start(bf16[24,32,1280]{2,1,0:T(8,128)(2,1)S(1)} %collective-permute-done.1.rest_3_) | copy-start | bytes 5898244
  141.4 15.7 %all-to-all-start.3 = ((bf16[32,32,256]{2,1,0:T(8,128)(2,1)}), bf16[32,32,256]{2,1,0:T(8,128)(2,1)S(1)}, u32[]{:S(2)}, u32[]{:S(2)}) async-start(bf16[32,32,256]{2,1,0:T(8,128)(2,1)} %contract.1), calls=%async_computation.3 | async-start | bytes 1048576 | tf_op jit(solution)/shard_map/all_to_all | solution.py:285
  147.0 2.2 %copy-start.2 = (bf16[8,2048,128]{2,1,0:T(8,128)(2,1)S(1)}, bf16[8,2048,128]{2,1,0:T(8,128)(2,1)}, u32[]{:S(2)}) copy-start(bf16[8,2048,128]{2,1,0:T(8,128)(2,1)} %p3.1) | copy-start | bytes 12582916
  149.2 7.9 %copy-start.8 = (bf16[128,128]{1,0:T(8,128)(2,1)S(1)}, bf16[128,128]{1,0:T(8,128)(2,1)}, u32[]{:S(2)}) copy-start(bf16[128,128]{1,0:T(8,128)(2,1)} %w_ref.3) | copy-start | bytes 98308
  149.2 7.9 %copy-start.11 = (f32[128]{0:T(128)S(1)}, f32[128]{0:T(128)}, u32[]{:S(2)}) copy-start(f32[128]{0:T(128)} %param.17) | copy-start | bytes 1540
  149.2 7.9 %copy-start.12 = (f32[128]{0:T(128)S(1)}, f32[128]{0:T(128)}, u32[]{:S(2)}) copy-start(f32[128]{0:T(128)} %param.18) | copy-start | bytes 1540

commit v5 on v4

--- a/solution.py
+++ b/solution.py
@@ -14,9 +14,9 @@
 PLANE = ("yhi", "core", "x", "ylo")
 PARTS = 32
 OWN = 4
-RIGHTS = ((0, 768), (768, 1280))
+DOTS = ((0, 768), (768, 1280))
 CHUNK = 128
-STRIDE = 136
+STRIDE = 130
 F32 = jnp.float32
 BF16 = jnp.bfloat16
 VMEM_LIMIT = 60 * 1024 * 1024
@@ -61,129 +61,159 @@
         out_ref[part, :, start : start + CHUNK] = jnp.concatenate(pieces, axis=0).astype(BF16)
 
 
-def project_kernel(pair_ref, mask_ref, gain_ref, bias_ref, value_ref, gate_ref, out_ref, mixed):
+def project_kernel(side_ref, pair_ref, mask_ref, gain_ref, bias_ref, value_ref, gate_ref, out_ref, mixed):
     params = projection(gain_ref, bias_ref, value_ref, gate_ref)
     for start in range(0, pair_ref.shape[1], CHUNK):
         project_chunk(params, pair_ref, mask_ref, out_ref, mixed, start)
 
 
-def project(pair, mask, gain, bias, w_value, w_gate, side, start, length):
-    width = max(w for w in range(CHUNK, 513, CHUNK) if start % w == 0 and length % w == 0)
-    first = start // width
-    whole = lambda i: (0, 0)
-    column = lambda i: (0, side)
+def project(pair, mask, gain, bias, w_value, w_gate, side, limit):
+    length = pair.shape[1]
+    width = 512
     tokens = SUB * length
-    return pl.pallas_call(
-        project_kernel,
+    whole = lambda i, side: (0, 0)
+    column = lambda i, side: (0, side[0])
+    spec = pltpu.PrefetchScalarGridSpec(
+        num_scalar_prefetch=1,
         grid=(length // width,),
         in_specs=[
-            pl.BlockSpec((SUB, width, 128), lambda i: (0, first + i, 0)),
-            pl.BlockSpec((SUB, width), lambda i: (0, first + i)),
+            pl.BlockSpec((SUB, width, 128), lambda i, side: (0, i, 0)),
+            pl.BlockSpec((SUB, width), lambda i, side: (0, i)),
             pl.BlockSpec((1, 128), whole),
             pl.BlockSpec((1, 128), whole),
             pl.BlockSpec((128, 128), column),
             pl.BlockSpec((128, 128), column),
         ],
-        out_specs=pl.BlockSpec((PARTS, OWN * SUB, width), lambda i: (0, 0, i)),
+        out_specs=pl.BlockSpec((PARTS, OWN * SUB, width), lambda i, side: (0, 0, i)),
+        scratch_shapes=[pltpu.VMEM((SUB * STRIDE * (width // CHUNK), 128), F32)],
+    )
+    return pl.pallas_call(
+        project_kernel,
+        grid_spec=spec,
         out_shape=jax.ShapeDtypeStruct((PARTS, OWN * SUB, length), BF16),
-        scratch_shapes=[pltpu.VMEM((SUB * STRIDE * (width // CHUNK), 128), F32)],
-        compiler_params=pltpu.CompilerParams(
-            vmem_limit_bytes=VMEM_LIMIT if side == 1 and start == 0 else VMEM_SMALL
-        ),
+        compiler_params=pltpu.CompilerParams(vmem_limit_bytes=limit),
         cost_estimate=pl.CostEstimate(
             flops=tokens * 128 * 384 * 2, bytes_accessed=tokens * 512, transcendentals=tokens * 128
         ),
         name="project",
-    )(pair, mask, gain, bias, w_value, w_gate)
-
-
-def rows_of(ref, pair_of_channels):
-    parts, _, width = ref.shape
-    both = ref[:, pair_of_channels * 16 : (pair_of_channels + 1) * 16, :].astype(F32)
+    )(side.reshape(1), pair, mask, gain, bias, w_value, w_gate)
+
+
+def rows_of(ref, parts, tokens, half):
+    both = ref[parts, half * 16 : (half + 1) * 16, tokens].astype(F32)
+    count, _, width = both.shape
     return [
-        both[:, k * SUB : (k + 1) * SUB, :].reshape(parts * SUB, width).astype(BF16)
+        both[:, k * SUB : (k + 1) * SUB, :].reshape(count * SUB, width).astype(BF16)
         for k in range(2)
     ]
 
 
-def contract_kernel(steps, left_hbm, *rest):
-    count, halves = len(steps), OWN // 2
-    pieces, out_ref, left_ref = rest[: 2 * count], rest[2 * count], rest[2 * count + 1]
-    held = rest[2 * count + 2 : 4 * count + 2]
-    total, sems = rest[4 * count + 2 :]
+def corner_kernel(left_ref, right_ref, out_ref):
+    every = slice(None)
+    for half in range(OWN // 2):
+        left = rows_of(left_ref, every, every, half)
+        right = rows_of(right_ref, every, every, half)
+        for k in range(2):
+            out_ref[half * 2 + k] = dot(left[k], right[k], ((1,), (1,)))
+
+
+def corner(left, early):
+    shape = left.shape
+    return pl.pallas_call(
+        corner_kernel,
+        grid=(1,),
+        in_specs=[
+            pl.BlockSpec(shape, lambda i: (0, 0, 0)),
+            pl.BlockSpec(shape, lambda i: (STEPS - 2, 0, 0)),
+        ],
+        out_specs=pl.BlockSpec((OWN, BLOCK, BLOCK), lambda i: (0, 0, 0)),
+        out_shape=jax.ShapeDtypeStruct((OWN, BLOCK, BLOCK), F32),
+        compiler_params=pltpu.CompilerParams(vmem_limit_bytes=VMEM_SMALL),
+        cost_estimate=pl.CostEstimate(
+            flops=2 * 4 * 64 * 64 * 2048, bytes_accessed=2 * 1024 * 1024, transcendentals=0
+        ),
+        name="corner",
+    )(left, early)
+
+
+def contract_kernel(
+    early_hbm, late_hbm, after_hbm, corner_hbm, out_ref, early, late, after, corner_ref, total, sems, corner_sem
+):
+    halves = OWN // 2
+    pairs = ((early_hbm, early), (late_hbm, late), (after_hbm, after))
     copies = {}
-    for k, (begin, length) in enumerate(steps):
-        tokens = pl.ds(begin, length)
+    for k, tokens in enumerate(DOTS):
         for half in range(halves):
             rows = pl.ds(half * 16, 16)
-            sem = 3 * (k * halves + half)
             copies[k, half] = [
                 pltpu.make_async_copy(
-                    left_hbm.at[:, rows, tokens], left_ref.at[:, rows, tokens], sems.at[sem]
+                    source.at[:, rows, pl.ds(*tokens)],
+                    target.at[:, rows, pl.ds(*tokens)],
+                    sems.at[k * halves + half, j],
                 )
-            ] + [
-                pltpu.make_async_copy(
-                    pieces[2 * k + j].at[:, rows, :], held[2 * k + j].at[:, rows, :], sems.at[sem + 1 + j]
-                )
-                for j in range(2)
+                for j, (source, target) in enumerate(pairs)
             ]
             for copy in copies[k, half]:
                 copy.start()
+    corner_copy = pltpu.make_async_copy(corner_hbm, corner_ref, corner_sem)
+    corner_copy.start()
     groups = BLOCK // SUB
-    for k, (begin, length) in enumerate(steps):
-        for pair_of_channels in range(halves):
-            for copy in copies[k, pair_of_channels]:
+    rest = slice(0, (STEPS - 1) * groups)
+    last = slice((STEPS - 1) * groups, STEPS * groups)
+    for k, (begin, length) in enumerate(DOTS):
+        tokens = slice(begin, begin + length)
+        for half in range(halves):
+            for copy in copies[k, half]:
                 copy.wait()
-            left = rows_of(left_ref.at[:, :, pl.ds(begin, length)], pair_of_channels)
-            right = rows_of(held[2 * k], pair_of_channels)
-            after = rows_of(held[2 * k + 1], pair_of_channels)
+            early_rest, early_last = (rows_of(early, p, tokens, half) for p in (rest, last))
+            late_rest, late_last = (rows_of(late, p, tokens, half) for p in (rest, last))
+            following = rows_of(after, slice(None), tokens, half)
             for j in range(2):
-                window = jnp.concatenate([right[j], after[j]], axis=0)
-                product = dot(left[j], window, ((1,), (1,)))
-                channel = pair_of_channels * 2 + j
+                left = jnp.concatenate([late_rest[j], early_last[j]], axis=0)
+                window = jnp.concatenate([early_rest[j], late_last[j], following[j]], axis=0)
+                product = dot(left, window, ((1,), (1,)))
+                channel = half * 2 + j
                 total[channel] = product if k == 0 else total[channel] + product
-            if k < count - 1:
+            if k < len(DOTS) - 1:
                 continue
+            if half == 0:
+                corner_copy.wait()
             for block in range(STEPS):
-                band = [
-                    total[
-                        pair_of_channels * 2 + j,
-                        block * BLOCK : (block + 1) * BLOCK,
-                        block * BLOCK : (block + STEPS) * BLOCK,
-                    ].reshape(groups, SUB, STEPS * BLOCK)
-                    for j in range(2)
-                ]
+                band = []
+                for channel in (half * 2, half * 2 + 1):
+                    rows = total[
+                        channel, block * BLOCK : (block + 1) * BLOCK, block * BLOCK : (block + STEPS) * BLOCK
+                    ]
+                    if block == STEPS - 1:
+                        rows = jnp.concatenate([rows, corner_ref[channel]], axis=1)
+                    band.append(rows.reshape(groups, SUB, STEPS * BLOCK))
                 out_ref[
-                    block * groups : (block + 1) * groups,
-                    pair_of_channels * 16 : (pair_of_channels + 1) * 16,
-                    :,
+                    block * groups : (block + 1) * groups, half * 16 : (half + 1) * 16, :
                 ] = jnp.concatenate(band, axis=1).astype(BF16)
 
 
-def contract(left, pieces):
-    operands, steps, begin = [left], [], 0
-    for right, after in pieces:
-        operands += [right, after]
-        steps.append((begin, right.shape[2]))
-        begin += right.shape[2]
-    return pl.pallas_call(
-        functools.partial(contract_kernel, tuple(steps)),
-        in_specs=[pl.BlockSpec(memory_space=pltpu.HBM)] * len(operands),
-        out_specs=pl.BlockSpec(memory_space=pltpu.VMEM),
+def contract(early, late, after, returned):
+    hbm = pl.BlockSpec(memory_space=pltpu.HBM)
+    vmem = pl.BlockSpec(memory_space=pltpu.VMEM)
+    window = BLOCK * (2 * STEPS - 2)
+    return pl.pallas_call(
+        contract_kernel,
+        in_specs=[hbm] * 4,
+        out_specs=vmem,
         out_shape=jax.ShapeDtypeStruct((PARTS, OWN * SUB, STEPS * BLOCK), BF16),
-        scratch_shapes=[pltpu.VMEM(v.shape, BF16) for v in operands]
+        scratch_shapes=[pltpu.VMEM(v.shape, BF16) for v in (early, late, after)]
         + [
-            pltpu.VMEM((OWN, BLOCK * STEPS, BLOCK * (2 * STEPS - 1)), F32),
-            pltpu.SemaphoreType.DMA((3 * OWN // 2 * len(pieces),)),
+            pltpu.VMEM(returned.shape, F32),
+            pltpu.VMEM((OWN, BLOCK * STEPS, window), F32),
+            pltpu.SemaphoreType.DMA((OWN // 2 * len(DOTS), 3)),
+            pltpu.SemaphoreType.DMA(()),
         ],
         compiler_params=pltpu.CompilerParams(vmem_limit_bytes=VMEM_LIMIT),
         cost_estimate=pl.CostEstimate(
-            flops=2 * 4 * 256 * 448 * left.shape[2],
-            bytes_accessed=6 * 1024 * left.shape[2],
-            transcendentals=0,
+            flops=2 * 4 * 256 * window * 2048, bytes_accessed=11 * 2**20, transcendentals=0
         ),
         name="contract",
-    )(*operands)
+    )(early, late, after, returned)
 
 
 def finish_kernel(triangle_ref, gate_ref, gain_ref, bias_ref, w_ref, out_ref, scaled):
@@ -276,26 +306,25 @@
 ):
     gain, bias = in_gain.reshape(1, 128), in_bias.reshape(1, 128)
     planes = lax.axis_size("z")
-    to_before = [(i, (i - 1) % planes) for i in range(planes)]
-
-    def operand(side, chunk):
-        return project(pair, pair_mask, gain, bias, w_value, w_gate, side, *chunk)
+    down = [(i, (i - 1) % planes) for i in range(planes)]
+    up = [(i, (i + 1) % planes) for i in range(planes)]
+    place = lax.axis_index("yhi") * 2 + lax.axis_index("core")
+    block = lax.axis_index("z") * STEPS + place
+    groups = BLOCK // SUB
+
+    def operand(side, limit):
+        return project(pair, pair_mask, gain, bias, w_value, w_gate, side, limit)
 
     def spread(value):
         return lax.all_to_all(value, PLANE, 0, 0, tiled=True)
 
-    def shifted(right):
-        return lax.ppermute(right[: (STEPS - 1) * BLOCK // SUB], "z", to_before)
-
-    first = spread(operand(1, RIGHTS[0]))
-    first_after = shifted(first)
-    second = spread(operand(1, RIGHTS[1]))
-    second_after = shifted(second)
-    left = operand(0, (0, pair.shape[1]))
-    left, first_after = lax.optimization_barrier((left, first_after))
-    left = spread(left)
-    block = lax.axis_index("z") * 4 + lax.axis_index("yhi") * 2 + lax.axis_index("core")
-    band = contract(left, [(first, first_after), (second, second_after)])
+    side = jnp.where(place == STEPS - 1, 0, 1).astype(jnp.int32)
+    early = spread(operand(side, VMEM_LIMIT))
+    above = lax.ppermute(early[(STEPS - 1) * groups :], "z", up)
+    after = lax.ppermute(early[: 2 * groups], "z", down)
+    returned = lax.ppermute(corner(above, early), "z", down)
+    late = spread(operand(1 - side, VMEM_SMALL))
+    band = contract(early, late, after, returned)
     band, block = lax.optimization_barrier((band, block))
     gate = output_gate(pair, gain, bias, out_gate_w, block)
     triangle = spread(band)

time: 161 us -> 160 us (level)
  waiting for transfers between devices: 83 us -> 95.5 us
  starting transfers between devices: 37 us -> 26 us
  local copies, waits for them, and re-layouts: 11.7 us -> 10 us
    all_to_all x4 -> x3, waiting for transfers between devices: 26.6 us -> 68.7 us  [spread(): return lax.all_to_all(value, PLANE, 0, 0, tiled=True)]
    ppermute x2 -> x3, waiting for transfers between devices: 56.3 us -> 26.8 us  [the longest x1 26 us: on_device(): above = lax.ppermute(early[(STEPS - 1) * groups:], 'z', up)]
    ppermute x2 -> x3, starting transfers between devices: 11.8 us -> 6.11 us  [the longest x1 5.94 us: on_device(): after = lax.ppermute(early[:2 * groups], 'z', down)]
    all_to_all x4 -> x3, starting transfers between devices: 25.2 us -> 19.9 us  [spread(): return lax.all_to_all(value, PLANE, 0, 0, tiled=True)]
    unnamed x32 -> x26, local copies, waits for them, and re-layouts: 8.61 us -> 7.02 us
  transfers between devices with their start and end apart: 6 -> 6, of which waited for: 6 -> 5; matrix products, arithmetic and copies ran while one was open for 2% -> 2% of each run, Pallas kernels for 9% -> 6%
where the time goes in v5:
time: 160 us; the launch traced here: 157 us
  waiting for transfers between devices  95.5 us (60%)
  starting transfers between devices  26 us (16%)
  Pallas kernels  25.6 us (16%)
  local copies, waits for them, and re-layouts  10 us (6%)
    all_to_all x3, waiting for transfers between devices, spread(): return lax.all_to_all(value, PLANE, 0, 0, tiled=True)  68.7 us
    ppermute x1, waiting for transfers between devices, on_device(): above = lax.ppermute(early[(STEPS - 1) * groups:], 'z', up)  26 us
    all_to_all x3, starting transfers between devices, spread(): return lax.all_to_all(value, PLANE, 0, 0, tiled=True)  19.9 us
    pallas_call x2, Pallas kernels, project(): pl.pallas_call(project_kernel, grid_spec=spec, out_shape=jax.ShapeDtypeSt...  15.5 us
    unnamed x26, local copies, waits for them, and re-layouts  7.02 us
    pallas_call x1, Pallas kernels, contract(): pl.pallas_call(contract_kernel, in_specs=[hbm] * 4, out_specs=vmem, out_s...  6.01 us
    ppermute x1, starting transfers between devices, on_device(): after = lax.ppermute(early[:2 * groups], 'z', down)  5.94 us
  transfers between devices with their start and end apart: 6, of which 5 were waited for; matrix products, arithmetic and copies ran while one was open for 2% of the time, Pallas kernels for 6%

profile of v5, /device:TPU:8, one launch (start us, length us, event | category | flops | bytes accessed | tf_op | source)
XLA Modules:
  0.0 157.3 jit_solution(10001503108397691123)
XLA Ops:
  0.0 8.6 %project.2 = bf16[32,32,2048]{2,1,0:T(8,128)(2,1)} custom-call(s32[1]{0:T(128)} %bitcast.side_ref, bf16[8,2048,128]{2,1,0:T(8,128)(2,1)} %p3.1, s32[8,2048]{1,0:T(8,128)} %mask_ref.3, f32[1,128]{1,0:T(1,128)} %bitcast.7, f32[1,128]{1,0:T(1,128)} %bitcast.10, bf16[128,256]{1,0:T(8,128)(2,1)} %value_ref.3, bf16[128,256]{1,0:T(8,128)(2,1)} %gate_ref.3), custom_call_target="tpu_custom_call" | custom-call | flops 1610612736 | bytes 8388608 | tf_op jit(solution)/shard_map/project/pallas_call | solution.py:90
  8.6 0.0 copy-start.3
  8.6 0.0 copy-start.4
  8.6 0.0 copy-start.5
  8.6 0.0 copy-start.8
  8.6 0.0 copy-start.9
  8.6 7.7 %all-to-all-start = ((bf16[32,32,2048]{2,1,0:T(8,128)(2,1)}), bf16[32,32,2048]{2,1,0:T(8,128)(2,1)}, u32[]{:S(2)}, u32[]{:S(2)}) async-start(bf16[32,32,2048]{2,1,0:T(8,128)(2,1)} %project.2), calls=%async_computation | async-start | bytes 8388608 | tf_op jit(solution)/shard_map/all_to_all | solution.py:319
  16.4 0.0 copy-done.3
  16.4 0.0 copy-done.4
  16.4 0.0 copy-done.5
  16.4 0.0 copy-done.8
  16.4 0.0 copy-done.9
  16.4 0.0 copy-start
  16.4 2.2 %copy-done = bf16[8,2048,128]{2,1,0:T(8,128)(2,1)S(1)} copy-done((bf16[8,2048,128]{2,1,0:T(8,128)(2,1)S(1)}, bf16[8,2048,128]{2,1,0:T(8,128)(2,1)}, u32[]{:S(2)}) %copy-start) | copy-done | bytes 4194328
  18.6 6.9 %project.3 = bf16[32,32,2048]{2,1,0:T(8,128)(2,1)S(1)} custom-call(s32[1]{0:T(128)} %bitcast.3.side_ref, bf16[8,2048,128]{2,1,0:T(8,128)(2,1)S(1)} %copy-done, s32[8,2048]{1,0:T(8,128)S(1)} %copy-done.3, f32[1,128]{1,0:T(1,128)S(1)} %bitcast.8, f32[1,128]{1,0:T(1,128)S(1)} %bitcast.11, bf16[128,256]{1,0:T(8,128)(2,1)S(1)} %copy-done.4, ...), custom_call_target="tpu_custom_call" | custom-call | flops 1610612736 | bytes 8388608 | tf_op jit(solution)/shard_map/project/pallas_call | solution.py:90
  25.5 0.0 copy-start.2
  25.6 2.0 %copy-done.2 = bf16[32,32,2048]{2,1,0:T(8,128)(2,1)} copy-done((bf16[32,32,2048]{2,1,0:T(8,128)(2,1)}, bf16[32,32,2048]{2,1,0:T(8,128)(2,1)S(1)}, u32[]{:S(2)}) %copy-start.2) | copy-done | bytes 4194328
  27.5 43.6 %all-to-all-done.right_ref.early_hbm = bf16[32,32,2048]{2,1,0:T(8,128)(2,1)} async-done(((bf16[32,32,2048]{2,1,0:T(8,128)(2,1)}), bf16[32,32,2048]{2,1,0:T(8,128)(2,1)}, u32[]{:S(2)}, u32[]{:S(2)}) %all-to-all-start) | async-done | bytes 4194336 | tf_op jit(solution)/shard_map/all_to_all | solution.py:319
  71.1 4.7 %all-to-all-start.1 = ((bf16[32,32,2048]{2,1,0:T(8,128)(2,1)}), bf16[32,32,2048]{2,1,0:T(8,128)(2,1)}, u32[]{:S(2)}, u32[]{:S(2)}) async-start(bf16[32,32,2048]{2,1,0:T(8,128)(2,1)} %copy-done.2), calls=%async_computation.1 | async-start | bytes 8388608 | tf_op jit(solution)/shard_map/all_to_all | solution.py:319
  75.8 1.7 %slice.8 = bf16[16,32,2048]{2,1,0:T(8,128)(2,1)S(1)} slice(bf16[32,32,2048]{2,1,0:T(8,128)(2,1)} %all-to-all-done.right_ref.early_hbm), slice={[0:16], [0:32], [0:2048]} | slice | bytes 4194304 | tf_op jit(solution)/shard_map/slice | solution.py:324
  77.5 5.9 %collective-permute-start = (bf16[16,32,2048]{2,1,0:T(8,128)(2,1)S(1)}, bf16[16,32,2048]{2,1,0:T(8,128)(2,1)}, u32[]{:S(2)}, u32[]{:S(2)}) collective-permute-start(bf16[16,32,2048]{2,1,0:T(8,128)(2,1)S(1)} %slice.8), channel_id=1, source_target_pairs={{0,28},{4,0},{8,4},{12,8},{16,12},{20,16},{24,20},{28,24},{1,29},{... | collective-permute-start | bytes 6291464 | tf_op jit(solution)/shard_map/ppermute | solution.py:324
  83.5 1.3 slice.9
  84.8 0.1 collective-permute-start.1
  84.9 26.0 %collective-permute-done.1.left_ref = bf16[8,32,2048]{2,1,0:T(8,128)(2,1)S(1)} collective-permute-done((bf16[8,32,2048]{2,1,0:T(8,128)(2,1)S(1)}, bf16[8,32,2048]{2,1,0:T(8,128)(2,1)S(1)}, u32[]{:S(2)}, u32[]{:S(2)}) %collective-permute-start.1) | collective-permute-done | bytes 1048608 | tf_op jit(solution)/shard_map/ppermute | solution.py:323
  110.9 1.6 %corner.1 = f32[4,64,64]{2,1,0:T(8,128)S(1)} custom-call(bf16[8,32,2048]{2,1,0:T(8,128)(2,1)S(1)} %collective-permute-done.1.left_ref, bf16[32,32,2048]{2,1,0:T(8,128)(2,1)} %all-to-all-done.right_ref.early_hbm), custom_call_target="tpu_custom_call" | custom-call | flops 67108864 | bytes 2097152 | tf_op jit(solution)/shard_map/corner/pallas_call | solution.py:122
  112.5 0.1 collective-permute-start.2
  112.6 0.0 copy-start.6
  112.7 17.9 %all-to-all-done.1.late_hbm = bf16[32,32,2048]{2,1,0:T(8,128)(2,1)} async-done(((bf16[32,32,2048]{2,1,0:T(8,128)(2,1)}), bf16[32,32,2048]{2,1,0:T(8,128)(2,1)}, u32[]{:S(2)}, u32[]{:S(2)}) %all-to-all-start.1) | async-done | bytes 4194336 | tf_op jit(solution)/shard_map/all_to_all | solution.py:319
  130.6 0.8 collective-permute-done.2.corner_hbm
  131.4 0.0 copy-start.12
  131.4 0.0 collective-permute-done.after_hbm
  131.4 0.6 copy-done.12
  132.0 6.0 %contract.1 = bf16[32,32,256]{2,1,0:T(8,128)(2,1)} custom-call(bf16[32,32,2048]{2,1,0:T(8,128)(2,1)} %all-to-all-done.right_ref.early_hbm, bf16[32,32,2048]{2,1,0:T(8,128)(2,1)} %all-to-all-done.1.late_hbm, bf16[16,32,2048]{2,1,0:T(8,128)(2,1)} %collective-permute-done.after_hbm, f32[4,64,64]{2,1,0:T(8,128)} %copy-done.12), custom_call_target="tpu_custom_call" | custom-call | flops 1610612736 | bytes 11534336 | tf_op jit(solution)/shard_map/contract/pallas_call | solution.py:199
  138.1 7.5 %all-to-all-start.2 = ((bf16[32,32,256]{2,1,0:T(8,128)(2,1)}), bf16[32,32,256]{2,1,0:T(8,128)(2,1)S(1)}, u32[]{:S(2)}, u32[]{:S(2)}) async-start(bf16[32,32,256]{2,1,0:T(8,128)(2,1)} %contract.1), calls=%async_computation.2 | async-start | bytes 1048576 | tf_op jit(solution)/shard_map/all_to_all | solution.py:319
  145.6 0.0 copy-done.6
  145.6 0.0 copy-start.1
  145.6 2.2 %copy-done.1 = bf16[8,2048,128]{2,1,0:T(8,128)(2,1)S(1)} copy-done((bf16[8,2048,128]{2,1,0:T(8,128)(2,1)S(1)}, bf16[8,2048,128]{2,1,0:T(8,128)(2,1)}, u32[]{:S(2)}) %copy-start.1) | copy-done | bytes 4194328
  147.8 0.0 copy-start.7
  147.8 0.0 copy-start.10
  147.8 0.0 copy-start.11
  147.8 0.8 gate.1.gate_ref
  148.6 7.1 %all-to-all-done.2.triangle_ref = bf16[32,32,256]{2,1,0:T(8,128)(2,1)S(1)} async-done(((bf16[32,32,256]{2,1,0:T(8,128)(2,1)}), bf16[32,32,256]{2,1,0:T(8,128)(2,1)S(1)}, u32[]{:S(2)}, u32[]{:S(2)}) %all-to-all-start.2) | async-done | bytes 524320 | tf_op jit(solution)/shard_map/all_to_all | solution.py:319
  155.7 0.0 copy-done.7
  155.7 0.0 copy-done.10
  155.7 0.0 copy-done.11
  155.7 1.6 %finish.1 = bf16[8,256,128]{2,1,0:T(8,128)(2,1)} custom-call(bf16[32,32,256]{2,1,0:T(8,128)(2,1)S(1)} %all-to-all-done.2.triangle_ref, f32[8,256,128]{2,1,0:T(8,128)S(1)} %gate.1.gate_ref, f32[1,128]{1,0:T(1,128)S(1)} %bitcast.13, f32[1,128]{1,0:T(1,128)S(1)} %bitcast.14, bf16[128,128]{1,0:T(8,128)(2,1)S(1)} %copy-done.7), custom_call_target="tpu_custom_call" | custom-call | flops 67108864 | bytes 2097152 | tf_op jit(solution)/shard_map/finish/pallas_call | solution.py:240
Async XLA Ops:
  8.6 7.8 %copy-start.3 = (s32[8,2048]{1,0:T(8,128)S(1)}, s32[8,2048]{1,0:T(8,128)}, u32[]{:S(2)}) copy-start(s32[8,2048]{1,0:T(8,128)} %mask_ref.3) | copy-start | bytes 196612
  8.6 7.8 %copy-start.4 = (bf16[128,256]{1,0:T(8,128)(2,1)S(1)}, bf16[128,256]{1,0:T(8,128)(2,1)}, u32[]{:S(2)}) copy-start(bf16[128,256]{1,0:T(8,128)(2,1)} %value_ref.3) | copy-start | bytes 196612
  8.6 7.8 %copy-start.5 = (bf16[128,256]{1,0:T(8,128)(2,1)S(1)}, bf16[128,256]{1,0:T(8,128)(2,1)}, u32[]{:S(2)}) copy-start(bf16[128,256]{1,0:T(8,128)(2,1)} %gate_ref.3) | copy-start | bytes 196612
  8.6 7.8 %copy-start.8 = (f32[128]{0:T(128)S(1)}, f32[128]{0:T(128)}, u32[]{:S(2)}) copy-start(f32[128]{0:T(128)} %param.12) | copy-start | bytes 1540
  8.6 7.8 %copy-start.9 = (f32[128]{0:T(128)S(1)}, f32[128]{0:T(128)}, u32[]{:S(2)}) copy-start(f32[128]{0:T(128)} %param.13) | copy-start | bytes 1540
  8.6 62.5 %all-to-all-start = ((bf16[32,32,2048]{2,1,0:T(8,128)(2,1)}), bf16[32,32,2048]{2,1,0:T(8,128)(2,1)}, u32[]{:S(2)}, u32[]{:S(2)}) async-start(bf16[32,32,2048]{2,1,0:T(8,128)(2,1)} %project.2), calls=%async_computation | async-start | bytes 8388608 | tf_op jit(solution)/shard_map/all_to_all | solution.py:319
  16.4 2.2 %copy-start = (bf16[8,2048,128]{2,1,0:T(8,128)(2,1)S(1)}, bf16[8,2048,128]{2,1,0:T(8,128)(2,1)}, u32[]{:S(2)}) copy-start(bf16[8,2048,128]{2,1,0:T(8,128)(2,1)} %p3.1) | copy-start | bytes 12582916
  25.5 2.0 %copy-start.2 = (bf16[32,32,2048]{2,1,0:T(8,128)(2,1)}, bf16[32,32,2048]{2,1,0:T(8,128)(2,1)S(1)}, u32[]{:S(2)}) copy-start(bf16[32,32,2048]{2,1,0:T(8,128)(2,1)S(1)} %project.3) | copy-start | bytes 12582916
  71.1 59.5 %all-to-all-start.1 = ((bf16[32,32,2048]{2,1,0:T(8,128)(2,1)}), bf16[32,32,2048]{2,1,0:T(8,128)(2,1)}, u32[]{:S(2)}, u32[]{:S(2)}) async-start(bf16[32,32,2048]{2,1,0:T(8,128)(2,1)} %copy-done.2), calls=%async_computation.1 | async-start | bytes 8388608 | tf_op jit(solution)/shard_map/all_to_all | solution.py:319
  77.5 53.9 %collective-permute-start = (bf16[16,32,2048]{2,1,0:T(8,128)(2,1)S(1)}, bf16[16,32,2048]{2,1,0:T(8,128)(2,1)}, u32[]{:S(2)}, u32[]{:S(2)}) collective-permute-start(bf16[16,32,2048]{2,1,0:T(8,128)(2,1)S(1)} %slice.8), channel_id=1, source_target_pairs={{0,28},{4,0},{8,4},{12,8},{16,12},{20,16},{24,20},{28,24},{1,29},{... | collective-permute-start | bytes 6291464 | tf_op jit(solution)/shard_map/ppermute | solution.py:324
  84.8 26.1 %collective-permute-start.1 = (bf16[8,32,2048]{2,1,0:T(8,128)(2,1)S(1)}, bf16[8,32,2048]{2,1,0:T(8,128)(2,1)S(1)}, u32[]{:S(2)}, u32[]{:S(2)}) collective-permute-start(bf16[8,32,2048]{2,1,0:T(8,128)(2,1)S(1)} %slice.9), channel_id=1, source_target_pairs={{0,4},{4,8},{8,12},{12,16},{16,20},{20,24},{24,28},{28,0},{1,5},{5... | collective-permute-start | bytes 3145736 | tf_op jit(solution)/shard_map/ppermute | solution.py:323
  112.5 18.9 %collective-permute-start.2 = (f32[4,64,64]{2,1,0:T(8,128)S(1)}, f32[4,64,64]{2,1,0:T(8,128)S(1)}, u32[]{:S(2)}, u32[]{:S(2)}) collective-permute-start(f32[4,64,64]{2,1,0:T(8,128)S(1)} %corner.1), channel_id=1, source_target_pairs={{0,28},{4,0},{8,4},{12,8},{16,12},{20,16},{24,20},{28,24},{1,29},{... | collective-permute-start | bytes 196616 | tf_op jit(solution)/shard_map/ppermute | solution.py:325
  112.6 32.9 %copy-start.6 = (bf16[128,128]{1,0:T(8,128)(2,1)S(1)}, bf16[128,128]{1,0:T(8,128)(2,1)}, u32[]{:S(2)}) copy-start(bf16[128,128]{1,0:T(8,128)(2,1)} %w_ref.2) | copy-start | bytes 98308
  131.4 0.7 copy-start.12
  138.1 17.6 %all-to-all-start.2 = ((bf16[32,32,256]{2,1,0:T(8,128)(2,1)}), bf16[32,32,256]{2,1,0:T(8,128)(2,1)S(1)}, u32[]{:S(2)}, u32[]{:S(2)}) async-start(bf16[32,32,256]{2,1,0:T(8,128)(2,1)} %contract.1), calls=%async_computation.2 | async-start | bytes 1048576 | tf_op jit(solution)/shard_map/all_to_all | solution.py:319
  145.6 2.2 %copy-start.1 = (bf16[8,2048,128]{2,1,0:T(8,128)(2,1)S(1)}, bf16[8,2048,128]{2,1,0:T(8,128)(2,1)}, u32[]{:S(2)}) copy-start(bf16[8,2048,128]{2,1,0:T(8,128)(2,1)} %p3.1) | copy-start | bytes 12582916
  147.8 7.9 %copy-start.7 = (bf16[128,128]{1,0:T(8,128)(2,1)S(1)}, bf16[128,128]{1,0:T(8,128)(2,1)}, u32[]{:S(2)}) copy-start(bf16[128,128]{1,0:T(8,128)(2,1)} %w_ref.3) | copy-start | bytes 98308
  147.8 7.9 %copy-start.10 = (f32[128]{0:T(128)S(1)}, f32[128]{0:T(128)}, u32[]{:S(2)}) copy-start(f32[128]{0:T(128)} %param.17) | copy-start | bytes 1540
  147.8 7.9 %copy-start.11 = (f32[128]{0:T(128)S(1)}, f32[128]{0:T(128)}, u32[]{:S(2)}) copy-start(f32[128]{0:T(128)} %param.18) | copy-start | bytes 1540

commit v6 on v5

--- a/solution.py
+++ b/solution.py
@@ -21,6 +21,7 @@
 BF16 = jnp.bfloat16
 VMEM_LIMIT = 60 * 1024 * 1024
 VMEM_SMALL = 24 * 1024 * 1024
+VMEM_CONTRACT = 52 * 1024 * 1024
 
 
 def dot(a, b, dims):
@@ -114,7 +115,10 @@
         left = rows_of(left_ref, every, every, half)
         right = rows_of(right_ref, every, every, half)
         for k in range(2):
-            out_ref[half * 2 + k] = dot(left[k], right[k], ((1,), (1,)))
+            product = dot(left[k], right[k], ((1,), (1,)))
+            out_ref[half * 2 + k] = jnp.concatenate(
+                [product[: BLOCK // 2], product[BLOCK // 2 :]], axis=1
+            ).astype(BF16)
 
 
 def corner(left, early):
@@ -126,8 +130,8 @@
             pl.BlockSpec(shape, lambda i: (0, 0, 0)),
             pl.BlockSpec(shape, lambda i: (STEPS - 2, 0, 0)),
         ],
-        out_specs=pl.BlockSpec((OWN, BLOCK, BLOCK), lambda i: (0, 0, 0)),
-        out_shape=jax.ShapeDtypeStruct((OWN, BLOCK, BLOCK), F32),
+        out_specs=pl.BlockSpec((OWN, BLOCK // 2, 2 * BLOCK), lambda i: (0, 0, 0)),
+        out_shape=jax.ShapeDtypeStruct((OWN, BLOCK // 2, 2 * BLOCK), BF16),
         compiler_params=pltpu.CompilerParams(vmem_limit_bytes=VMEM_SMALL),
         cost_estimate=pl.CostEstimate(
             flops=2 * 4 * 64 * 64 * 2048, bytes_accessed=2 * 1024 * 1024, transcendentals=0
@@ -185,7 +189,9 @@
                         channel, block * BLOCK : (block + 1) * BLOCK, block * BLOCK : (block + STEPS) * BLOCK
                     ]
                     if block == STEPS - 1:
-                        rows = jnp.concatenate([rows, corner_ref[channel]], axis=1)
+                        folded = corner_ref[channel].astype(F32)
+                        final = jnp.concatenate([folded[:, :BLOCK], folded[:, BLOCK:]], axis=0)
+                        rows = jnp.concatenate([rows, final], axis=1)
                     band.append(rows.reshape(groups, SUB, STEPS * BLOCK))
                 out_ref[
                     block * groups : (block + 1) * groups, half * 16 : (half + 1) * 16, :
@@ -194,21 +200,22 @@
 
 def contract(early, late, after, returned):
     hbm = pl.BlockSpec(memory_space=pltpu.HBM)
+    anywhere = pl.BlockSpec(memory_space=pl.ANY)
     vmem = pl.BlockSpec(memory_space=pltpu.VMEM)
     window = BLOCK * (2 * STEPS - 2)
     return pl.pallas_call(
         contract_kernel,
-        in_specs=[hbm] * 4,
+        in_specs=[hbm, hbm, anywhere, anywhere],
         out_specs=vmem,
         out_shape=jax.ShapeDtypeStruct((PARTS, OWN * SUB, STEPS * BLOCK), BF16),
         scratch_shapes=[pltpu.VMEM(v.shape, BF16) for v in (early, late, after)]
         + [
-            pltpu.VMEM(returned.shape, F32),
+            pltpu.VMEM(returned.shape, BF16),
             pltpu.VMEM((OWN, BLOCK * STEPS, window), F32),
             pltpu.SemaphoreType.DMA((OWN // 2 * len(DOTS), 3)),
             pltpu.SemaphoreType.DMA(()),
         ],
-        compiler_params=pltpu.CompilerParams(vmem_limit_bytes=VMEM_LIMIT),
+        compiler_params=pltpu.CompilerParams(vmem_limit_bytes=VMEM_CONTRACT),
         cost_estimate=pl.CostEstimate(
             flops=2 * 4 * 256 * window * 2048, bytes_accessed=11 * 2**20, transcendentals=0
         ),

time: 160 us -> 157 us (0.981)
    unnamed x26 -> x24, local copies, waits for them, and re-layouts: 7.02 us -> 6.38 us
  transfers between devices with their start and end apart: 6 -> 6, of which waited for: 5 -> 4; matrix products, arithmetic and copies ran while one was open for 2% -> 2% of each run, Pallas kernels for 6% -> 6%
where the time goes in v6:
time: 157 us; the launch traced here: 155 us
  waiting for transfers between devices  94.6 us (60%)
  Pallas kernels  25.6 us (16%)
  starting transfers between devices  24.7 us (16%)
  local copies, waits for them, and re-layouts  9.4 us (6%)
    all_to_all x3, waiting for transfers between devices, spread(): return lax.all_to_all(value, PLANE, 0, 0, tiled=True)  68.6 us
    ppermute x1, waiting for transfers between devices, on_device(): above = lax.ppermute(early[(STEPS - 1) * groups:], 'z', up)  26.1 us
    all_to_all x3, starting transfers between devices, spread(): return lax.all_to_all(value, PLANE, 0, 0, tiled=True)  18.6 us
    pallas_call x2, Pallas kernels, project(): pl.pallas_call(project_kernel, grid_spec=spec, out_shape=jax.ShapeDtypeSt...  15.5 us
    unnamed x24, local copies, waits for them, and re-layouts  6.38 us
    pallas_call x1, Pallas kernels, contract(): pl.pallas_call(contract_kernel, in_specs=[hbm, hbm, anywhere, anywhere],...  5.97 us
    ppermute x1, starting transfers between devices, on_device(): after = lax.ppermute(early[:2 * groups], 'z', down)  5.94 us
  transfers between devices with their start and end apart: 6, of which 4 were waited for; matrix products, arithmetic and copies ran while one was open for 2% of the time, Pallas kernels for 6%

profile of v6, /device:TPU:8, one launch (start us, length us, event | category | flops | bytes accessed | tf_op | source)
XLA Modules:
  0.0 154.5 jit_solution(2015296976313906656)
XLA Ops:
  0.0 8.6 %project.2 = bf16[32,32,2048]{2,1,0:T(8,128)(2,1)} custom-call(s32[1]{0:T(128)} %bitcast.side_ref, bf16[8,2048,128]{2,1,0:T(8,128)(2,1)} %p3.1, s32[8,2048]{1,0:T(8,128)} %mask_ref.3, f32[1,128]{1,0:T(1,128)} %bitcast.7, f32[1,128]{1,0:T(1,128)} %bitcast.10, bf16[128,256]{1,0:T(8,128)(2,1)} %value_ref.3, bf16[128,256]{1,0:T(8,128)(2,1)} %gate_ref.3), custom_call_target="tpu_custom_call" | custom-call | flops 1610612736 | bytes 8388608 | tf_op jit(solution)/shard_map/project/pallas_call | solution.py:91
  8.6 0.0 copy-start.3
  8.6 0.0 copy-start.4
  8.6 0.0 copy-start.5
  8.6 0.0 copy-start.8
  8.6 0.0 copy-start.9
  8.6 7.7 %all-to-all-start = ((bf16[32,32,2048]{2,1,0:T(8,128)(2,1)}), bf16[32,32,2048]{2,1,0:T(8,128)(2,1)}, u32[]{:S(2)}, u32[]{:S(2)}) async-start(bf16[32,32,2048]{2,1,0:T(8,128)(2,1)} %project.2), calls=%async_computation | async-start | bytes 8388608 | tf_op jit(solution)/shard_map/all_to_all | solution.py:326
  16.4 0.0 copy-done.3
  16.4 0.0 copy-done.4
  16.4 0.0 copy-done.5
  16.4 0.0 copy-done.8
  16.4 0.0 copy-done.9
  16.4 0.0 copy-start
  16.4 2.2 %copy-done = bf16[8,2048,128]{2,1,0:T(8,128)(2,1)S(1)} copy-done((bf16[8,2048,128]{2,1,0:T(8,128)(2,1)S(1)}, bf16[8,2048,128]{2,1,0:T(8,128)(2,1)}, u32[]{:S(2)}) %copy-start) | copy-done | bytes 4194328
  18.6 6.9 %project.3 = bf16[32,32,2048]{2,1,0:T(8,128)(2,1)S(1)} custom-call(s32[1]{0:T(128)} %bitcast.3.side_ref, bf16[8,2048,128]{2,1,0:T(8,128)(2,1)S(1)} %copy-done, s32[8,2048]{1,0:T(8,128)S(1)} %copy-done.3, f32[1,128]{1,0:T(1,128)S(1)} %bitcast.8, f32[1,128]{1,0:T(1,128)S(1)} %bitcast.11, bf16[128,256]{1,0:T(8,128)(2,1)S(1)} %copy-done.4, ...), custom_call_target="tpu_custom_call" | custom-call | flops 1610612736 | bytes 8388608 | tf_op jit(solution)/shard_map/project/pallas_call | solution.py:91
  25.6 0.0 copy-start.2
  25.6 2.0 %copy-done.2 = bf16[32,32,2048]{2,1,0:T(8,128)(2,1)} copy-done((bf16[32,32,2048]{2,1,0:T(8,128)(2,1)}, bf16[32,32,2048]{2,1,0:T(8,128)(2,1)S(1)}, u32[]{:S(2)}) %copy-start.2) | copy-done | bytes 4194328
  27.5 43.6 %all-to-all-done.right_ref.early_hbm = bf16[32,32,2048]{2,1,0:T(8,128)(2,1)} async-done(((bf16[32,32,2048]{2,1,0:T(8,128)(2,1)}), bf16[32,32,2048]{2,1,0:T(8,128)(2,1)}, u32[]{:S(2)}, u32[]{:S(2)}) %all-to-all-start) | async-done | bytes 4194336 | tf_op jit(solution)/shard_map/all_to_all | solution.py:326
  71.2 4.6 %all-to-all-start.1 = ((bf16[32,32,2048]{2,1,0:T(8,128)(2,1)}), bf16[32,32,2048]{2,1,0:T(8,128)(2,1)}, u32[]{:S(2)}, u32[]{:S(2)}) async-start(bf16[32,32,2048]{2,1,0:T(8,128)(2,1)} %copy-done.2), calls=%async_computation.1 | async-start | bytes 8388608 | tf_op jit(solution)/shard_map/all_to_all | solution.py:326
  75.8 1.7 %slice.8 = bf16[16,32,2048]{2,1,0:T(8,128)(2,1)S(1)} slice(bf16[32,32,2048]{2,1,0:T(8,128)(2,1)} %all-to-all-done.right_ref.early_hbm), slice={[0:16], [0:32], [0:2048]} | slice | bytes 4194304 | tf_op jit(solution)/shard_map/slice | solution.py:331
  77.6 5.9 %collective-permute-start = (bf16[16,32,2048]{2,1,0:T(8,128)(2,1)S(1)}, bf16[16,32,2048]{2,1,0:T(8,128)(2,1)}, u32[]{:S(2)}, u32[]{:S(2)}) collective-permute-start(bf16[16,32,2048]{2,1,0:T(8,128)(2,1)S(1)} %slice.8), channel_id=1, source_target_pairs={{0,28},{4,0},{8,4},{12,8},{16,12},{20,16},{24,20},{28,24},{1,29},{... | collective-permute-start | bytes 6291464 | tf_op jit(solution)/shard_map/ppermute | solution.py:331
  83.5 1.3 slice.9
  84.8 0.1 collective-permute-start.1
  84.9 26.1 %collective-permute-done.1.left_ref = bf16[8,32,2048]{2,1,0:T(8,128)(2,1)S(1)} collective-permute-done((bf16[8,32,2048]{2,1,0:T(8,128)(2,1)S(1)}, bf16[8,32,2048]{2,1,0:T(8,128)(2,1)S(1)}, u32[]{:S(2)}, u32[]{:S(2)}) %collective-permute-start.1) | collective-permute-done | bytes 1048608 | tf_op jit(solution)/shard_map/ppermute | solution.py:330
  110.9 1.7 %corner.1 = bf16[4,32,128]{2,1,0:T(8,128)(2,1)S(1)} custom-call(bf16[8,32,2048]{2,1,0:T(8,128)(2,1)S(1)} %collective-permute-done.1.left_ref, bf16[32,32,2048]{2,1,0:T(8,128)(2,1)} %all-to-all-done.right_ref.early_hbm), custom_call_target="tpu_custom_call" | custom-call | flops 67108864 | bytes 2097152 | tf_op jit(solution)/shard_map/corner/pallas_call | solution.py:126
  112.6 0.1 collective-permute-start.2
  112.7 0.0 copy-start.6
  112.8 17.9 %all-to-all-done.1.late_hbm = bf16[32,32,2048]{2,1,0:T(8,128)(2,1)} async-done(((bf16[32,32,2048]{2,1,0:T(8,128)(2,1)}), bf16[32,32,2048]{2,1,0:T(8,128)(2,1)}, u32[]{:S(2)}, u32[]{:S(2)}) %all-to-all-start.1) | async-done | bytes 4194336 | tf_op jit(solution)/shard_map/all_to_all | solution.py:326
  130.6 0.0 collective-permute-done.2.corner_hbm
  130.6 0.0 collective-permute-done.after_hbm
  130.6 6.0 %contract.1 = bf16[32,32,256]{2,1,0:T(8,128)(2,1)} custom-call(bf16[32,32,2048]{2,1,0:T(8,128)(2,1)} %all-to-all-done.right_ref.early_hbm, bf16[32,32,2048]{2,1,0:T(8,128)(2,1)} %all-to-all-done.1.late_hbm, bf16[16,32,2048]{2,1,0:T(8,128)(2,1)} %collective-permute-done.after_hbm, bf16[4,32,128]{2,1,0:T(8,128)(2,1)S(1)} %collective-permute-done.2.corner_hbm), custom_call_target="tpu_custom_call" | custom-call | flops 1610612736 | bytes 11534336 | tf_op jit(solution)/shard_map/contract/pallas_call | solution.py:206
  136.6 6.2 %all-to-all-start.2 = ((bf16[32,32,256]{2,1,0:T(8,128)(2,1)}), bf16[32,32,256]{2,1,0:T(8,128)(2,1)S(1)}, u32[]{:S(2)}, u32[]{:S(2)}) async-start(bf16[32,32,256]{2,1,0:T(8,128)(2,1)} %contract.1), calls=%async_computation.2 | async-start | bytes 1048576 | tf_op jit(solution)/shard_map/all_to_all | solution.py:326
  142.8 0.0 copy-done.6
  142.8 0.0 copy-start.1
  142.8 2.2 %copy-done.1 = bf16[8,2048,128]{2,1,0:T(8,128)(2,1)S(1)} copy-done((bf16[8,2048,128]{2,1,0:T(8,128)(2,1)S(1)}, bf16[8,2048,128]{2,1,0:T(8,128)(2,1)}, u32[]{:S(2)}) %copy-start.1) | copy-done | bytes 4194328
  145.0 0.0 copy-start.7
  145.0 0.0 copy-start.10
  145.0 0.0 copy-start.11
  145.0 0.8 gate.1.gate_ref
  145.8 7.1 %all-to-all-done.2.triangle_ref = bf16[32,32,256]{2,1,0:T(8,128)(2,1)S(1)} async-done(((bf16[32,32,256]{2,1,0:T(8,128)(2,1)}), bf16[32,32,256]{2,1,0:T(8,128)(2,1)S(1)}, u32[]{:S(2)}, u32[]{:S(2)}) %all-to-all-start.2) | async-done | bytes 524320 | tf_op jit(solution)/shard_map/all_to_all | solution.py:326
  152.9 0.0 copy-done.7
  152.9 0.0 copy-done.10
  152.9 0.0 copy-done.11
  152.9 1.6 %finish.1 = bf16[8,256,128]{2,1,0:T(8,128)(2,1)} custom-call(bf16[32,32,256]{2,1,0:T(8,128)(2,1)S(1)} %all-to-all-done.2.triangle_ref, f32[8,256,128]{2,1,0:T(8,128)S(1)} %gate.1.gate_ref, f32[1,128]{1,0:T(1,128)S(1)} %bitcast.13, f32[1,128]{1,0:T(1,128)S(1)} %bitcast.14, bf16[128,128]{1,0:T(8,128)(2,1)S(1)} %copy-done.7), custom_call_target="tpu_custom_call" | custom-call | flops 67108864 | bytes 2097152 | tf_op jit(solution)/shard_map/finish/pallas_call | solution.py:247
Async XLA Ops:
  8.6 7.8 %copy-start.3 = (s32[8,2048]{1,0:T(8,128)S(1)}, s32[8,2048]{1,0:T(8,128)}, u32[]{:S(2)}) copy-start(s32[8,2048]{1,0:T(8,128)} %mask_ref.3) | copy-start | bytes 196612
  8.6 7.8 %copy-start.4 = (bf16[128,256]{1,0:T(8,128)(2,1)S(1)}, bf16[128,256]{1,0:T(8,128)(2,1)}, u32[]{:S(2)}) copy-start(bf16[128,256]{1,0:T(8,128)(2,1)} %value_ref.3) | copy-start | bytes 196612
  8.6 7.8 %copy-start.5 = (bf16[128,256]{1,0:T(8,128)(2,1)S(1)}, bf16[128,256]{1,0:T(8,128)(2,1)}, u32[]{:S(2)}) copy-start(bf16[128,256]{1,0:T(8,128)(2,1)} %gate_ref.3) | copy-start | bytes 196612
  8.6 7.8 %copy-start.8 = (f32[128]{0:T(128)S(1)}, f32[128]{0:T(128)}, u32[]{:S(2)}) copy-start(f32[128]{0:T(128)} %param.12) | copy-start | bytes 1540
  8.6 7.8 %copy-start.9 = (f32[128]{0:T(128)S(1)}, f32[128]{0:T(128)}, u32[]{:S(2)}) copy-start(f32[128]{0:T(128)} %param.13) | copy-start | bytes 1540
  8.6 62.5 %all-to-all-start = ((bf16[32,32,2048]{2,1,0:T(8,128)(2,1)}), bf16[32,32,2048]{2,1,0:T(8,128)(2,1)}, u32[]{:S(2)}, u32[]{:S(2)}) async-start(bf16[32,32,2048]{2,1,0:T(8,128)(2,1)} %project.2), calls=%async_computation | async-start | bytes 8388608 | tf_op jit(solution)/shard_map/all_to_all | solution.py:326
  16.4 2.2 %copy-start = (bf16[8,2048,128]{2,1,0:T(8,128)(2,1)S(1)}, bf16[8,2048,128]{2,1,0:T(8,128)(2,1)}, u32[]{:S(2)}) copy-start(bf16[8,2048,128]{2,1,0:T(8,128)(2,1)} %p3.1) | copy-start | bytes 12582916
  25.6 2.0 %copy-start.2 = (bf16[32,32,2048]{2,1,0:T(8,128)(2,1)}, bf16[32,32,2048]{2,1,0:T(8,128)(2,1)S(1)}, u32[]{:S(2)}) copy-start(bf16[32,32,2048]{2,1,0:T(8,128)(2,1)S(1)} %project.3) | copy-start | bytes 12582916
  71.2 59.5 %all-to-all-start.1 = ((bf16[32,32,2048]{2,1,0:T(8,128)(2,1)}), bf16[32,32,2048]{2,1,0:T(8,128)(2,1)}, u32[]{:S(2)}, u32[]{:S(2)}) async-start(bf16[32,32,2048]{2,1,0:T(8,128)(2,1)} %copy-done.2), calls=%async_computation.1 | async-start | bytes 8388608 | tf_op jit(solution)/shard_map/all_to_all | solution.py:326
  77.6 53.1 %collective-permute-start = (bf16[16,32,2048]{2,1,0:T(8,128)(2,1)S(1)}, bf16[16,32,2048]{2,1,0:T(8,128)(2,1)}, u32[]{:S(2)}, u32[]{:S(2)}) collective-permute-start(bf16[16,32,2048]{2,1,0:T(8,128)(2,1)S(1)} %slice.8), channel_id=1, source_target_pairs={{0,28},{4,0},{8,4},{12,8},{16,12},{20,16},{24,20},{28,24},{1,29},{... | collective-permute-start | bytes 6291464 | tf_op jit(solution)/shard_map/ppermute | solution.py:331
  84.8 26.1 %collective-permute-start.1 = (bf16[8,32,2048]{2,1,0:T(8,128)(2,1)S(1)}, bf16[8,32,2048]{2,1,0:T(8,128)(2,1)S(1)}, u32[]{:S(2)}, u32[]{:S(2)}) collective-permute-start(bf16[8,32,2048]{2,1,0:T(8,128)(2,1)S(1)} %slice.9), channel_id=1, source_target_pairs={{0,4},{4,8},{8,12},{12,16},{16,20},{20,24},{24,28},{28,0},{1,5},{5... | collective-permute-start | bytes 3145736 | tf_op jit(solution)/shard_map/ppermute | solution.py:330
  112.6 18.0 %collective-permute-start.2 = (bf16[4,32,128]{2,1,0:T(8,128)(2,1)S(1)}, bf16[4,32,128]{2,1,0:T(8,128)(2,1)S(1)}, u32[]{:S(2)}, u32[]{:S(2)}) collective-permute-start(bf16[4,32,128]{2,1,0:T(8,128)(2,1)S(1)} %corner.1), channel_id=1, source_target_pairs={{0,28},{4,0},{8,4},{12,8},{16,12},{20,16},{24,20},{28,24},{1,29},{... | collective-permute-start | bytes 98312 | tf_op jit(solution)/shard_map/ppermute | solution.py:332
  112.7 30.1 %copy-start.6 = (bf16[128,128]{1,0:T(8,128)(2,1)S(1)}, bf16[128,128]{1,0:T(8,128)(2,1)}, u32[]{:S(2)}) copy-start(bf16[128,128]{1,0:T(8,128)(2,1)} %w_ref.2) | copy-start | bytes 98308
  136.6 16.3 %all-to-all-start.2 = ((bf16[32,32,256]{2,1,0:T(8,128)(2,1)}), bf16[32,32,256]{2,1,0:T(8,128)(2,1)S(1)}, u32[]{:S(2)}, u32[]{:S(2)}) async-start(bf16[32,32,256]{2,1,0:T(8,128)(2,1)} %contract.1), calls=%async_computation.2 | async-start | bytes 1048576 | tf_op jit(solution)/shard_map/all_to_all | solution.py:326
  142.8 2.2 %copy-start.1 = (bf16[8,2048,128]{2,1,0:T(8,128)(2,1)S(1)}, bf16[8,2048,128]{2,1,0:T(8,128)(2,1)}, u32[]{:S(2)}) copy-start(bf16[8,2048,128]{2,1,0:T(8,128)(2,1)} %p3.1) | copy-start | bytes 12582916
  145.0 7.9 %copy-start.7 = (bf16[128,128]{1,0:T(8,128)(2,1)S(1)}, bf16[128,128]{1,0:T(8,128)(2,1)}, u32[]{:S(2)}) copy-start(bf16[128,128]{1,0:T(8,128)(2,1)} %w_ref.3) | copy-start | bytes 98308
  145.0 7.9 %copy-start.10 = (f32[128]{0:T(128)S(1)}, f32[128]{0:T(128)}, u32[]{:S(2)}) copy-start(f32[128]{0:T(128)} %param.17) | copy-start | bytes 1540
  145.0 7.9 %copy-start.11 = (f32[128]{0:T(128)S(1)}, f32[128]{0:T(128)}, u32[]{:S(2)}) copy-start(f32[128]{0:T(128)} %param.18) | copy-start | bytes 1540

commit v7 on v6

--- a/solution.py
+++ b/solution.py
@@ -86,7 +86,7 @@
             pl.BlockSpec((128, 128), column),
         ],
         out_specs=pl.BlockSpec((PARTS, OWN * SUB, width), lambda i, side: (0, 0, i)),
-        scratch_shapes=[pltpu.VMEM((SUB * STRIDE * (width // CHUNK), 128), F32)],
+        scratch_shapes=[pltpu.VMEM((SUB * STRIDE * (width // CHUNK) + 136, 128), F32)],
     )
     return pl.pallas_call(
         project_kernel,
@@ -175,9 +175,17 @@
             for j in range(2):
                 left = jnp.concatenate([late_rest[j], early_last[j]], axis=0)
                 window = jnp.concatenate([early_rest[j], late_last[j], following[j]], axis=0)
-                product = dot(left, window, ((1,), (1,)))
                 channel = half * 2 + j
-                total[channel] = product if k == 0 else total[channel] + product
+                near = dot(left, window[: STEPS * BLOCK], ((1,), (1,)))
+                far = dot(left[BLOCK:], window[STEPS * BLOCK :], ((1,), (1,)))
+                for part, rows, columns_ in (
+                    (near, slice(0, None), slice(0, STEPS * BLOCK)),
+                    (far, slice(BLOCK, None), slice(STEPS * BLOCK, None)),
+                ):
+                    if k == 0:
+                        total[channel, rows, columns_] = part
+                    else:
+                        total[channel, rows, columns_] += part
             if k < len(DOTS) - 1:
                 continue
             if half == 0:
@@ -256,7 +264,7 @@
         ],
         out_specs=pl.BlockSpec((SUB, width, 128), lambda i: (0, i, 0)),
         out_shape=jax.ShapeDtypeStruct((SUB, STEPS * BLOCK, 128), BF16),
-        scratch_shapes=[pltpu.VMEM((SUB * width, 128), F32)],
+        scratch_shapes=[pltpu.VMEM((SUB * width + SUB, 128), F32)],
         compiler_params=pltpu.CompilerParams(vmem_limit_bytes=VMEM_SMALL),
         cost_estimate=pl.CostEstimate(
             flops=SUB * 256 * 128 * 256, bytes_accessed=2 * 1024 * 1024, transcendentals=2048

time: 157 us -> 157 us (level)
  no operation moved by 1% of the time
where the time goes in v7:
time: 157 us; the launch traced here: 154 us
  waiting for transfers between devices  94.6 us (60%)
  Pallas kernels  25.5 us (16%)
  starting transfers between devices  24.7 us (16%)
  local copies, waits for them, and re-layouts  9.4 us (6%)
    all_to_all x3, waiting for transfers between devices, spread(): return lax.all_to_all(value, PLANE, 0, 0, tiled=True)  68.5 us
    ppermute x1, waiting for transfers between devices, on_device(): above = lax.ppermute(early[(STEPS - 1) * groups:], 'z', up)  26.1 us
    all_to_all x3, starting transfers between devices, spread(): return lax.all_to_all(value, PLANE, 0, 0, tiled=True)  18.6 us
    pallas_call x2, Pallas kernels, project(): pl.pallas_call(project_kernel, grid_spec=spec, out_shape=jax.ShapeDtypeSt...  15.6 us
    unnamed x24, local copies, waits for them, and re-layouts  6.38 us
    ppermute x1, starting transfers between devices, on_device(): after = lax.ppermute(early[:2 * groups], 'z', down)  5.94 us
    pallas_call x1, Pallas kernels, contract(): pl.pallas_call(contract_kernel, in_specs=[hbm, hbm, anywhere, anywhere],...  5.78 us
  transfers between devices with their start and end apart: 6, of which 4 were waited for; matrix products, arithmetic and copies ran while one was open for 2% of the time, Pallas kernels for 6%

profile of v7, /device:TPU:8, one launch (start us, length us, event | category | flops | bytes accessed | tf_op | source)
XLA Modules:
  0.0 154.4 jit_solution(1445362357407064244)
XLA Ops:
  0.0 8.6 %project.2 = bf16[32,32,2048]{2,1,0:T(8,128)(2,1)} custom-call(s32[1]{0:T(128)} %bitcast.side_ref, bf16[8,2048,128]{2,1,0:T(8,128)(2,1)} %p3.1, s32[8,2048]{1,0:T(8,128)} %mask_ref.3, f32[1,128]{1,0:T(1,128)} %bitcast.7, f32[1,128]{1,0:T(1,128)} %bitcast.10, bf16[128,256]{1,0:T(8,128)(2,1)} %value_ref.3, bf16[128,256]{1,0:T(8,128)(2,1)} %gate_ref.3), custom_call_target="tpu_custom_call" | custom-call | flops 1610612736 | bytes 8388608 | tf_op jit(solution)/shard_map/project/pallas_call | solution.py:91
  8.6 0.0 copy-start.3
  8.6 0.0 copy-start.4
  8.6 0.0 copy-start.5
  8.6 0.0 copy-start.8
  8.7 0.0 copy-start.9
  8.7 7.7 %all-to-all-start = ((bf16[32,32,2048]{2,1,0:T(8,128)(2,1)}), bf16[32,32,2048]{2,1,0:T(8,128)(2,1)}, u32[]{:S(2)}, u32[]{:S(2)}) async-start(bf16[32,32,2048]{2,1,0:T(8,128)(2,1)} %project.2), calls=%async_computation | async-start | bytes 8388608 | tf_op jit(solution)/shard_map/all_to_all | solution.py:334
  16.4 0.0 copy-done.3
  16.4 0.0 copy-done.4
  16.4 0.0 copy-done.5
  16.4 0.0 copy-done.8
  16.5 0.0 copy-done.9
  16.5 0.0 copy-start
  16.5 2.2 %copy-done = bf16[8,2048,128]{2,1,0:T(8,128)(2,1)S(1)} copy-done((bf16[8,2048,128]{2,1,0:T(8,128)(2,1)S(1)}, bf16[8,2048,128]{2,1,0:T(8,128)(2,1)}, u32[]{:S(2)}) %copy-start) | copy-done | bytes 4194328
  18.7 7.0 %project.3 = bf16[32,32,2048]{2,1,0:T(8,128)(2,1)S(1)} custom-call(s32[1]{0:T(128)} %bitcast.3.side_ref, bf16[8,2048,128]{2,1,0:T(8,128)(2,1)S(1)} %copy-done, s32[8,2048]{1,0:T(8,128)S(1)} %copy-done.3, f32[1,128]{1,0:T(1,128)S(1)} %bitcast.8, f32[1,128]{1,0:T(1,128)S(1)} %bitcast.11, bf16[128,256]{1,0:T(8,128)(2,1)S(1)} %copy-done.4, ...), custom_call_target="tpu_custom_call" | custom-call | flops 1610612736 | bytes 8388608 | tf_op jit(solution)/shard_map/project/pallas_call | solution.py:91
  25.7 0.0 copy-start.2
  25.7 2.0 %copy-done.2 = bf16[32,32,2048]{2,1,0:T(8,128)(2,1)} copy-done((bf16[32,32,2048]{2,1,0:T(8,128)(2,1)}, bf16[32,32,2048]{2,1,0:T(8,128)(2,1)S(1)}, u32[]{:S(2)}) %copy-start.2) | copy-done | bytes 4194328
  27.6 43.6 %all-to-all-done.right_ref.early_hbm = bf16[32,32,2048]{2,1,0:T(8,128)(2,1)} async-done(((bf16[32,32,2048]{2,1,0:T(8,128)(2,1)}), bf16[32,32,2048]{2,1,0:T(8,128)(2,1)}, u32[]{:S(2)}, u32[]{:S(2)}) %all-to-all-start) | async-done | bytes 4194336 | tf_op jit(solution)/shard_map/all_to_all | solution.py:334
  71.2 4.6 %all-to-all-start.1 = ((bf16[32,32,2048]{2,1,0:T(8,128)(2,1)}), bf16[32,32,2048]{2,1,0:T(8,128)(2,1)}, u32[]{:S(2)}, u32[]{:S(2)}) async-start(bf16[32,32,2048]{2,1,0:T(8,128)(2,1)} %copy-done.2), calls=%async_computation.1 | async-start | bytes 8388608 | tf_op jit(solution)/shard_map/all_to_all | solution.py:334
  75.9 1.7 %slice.8 = bf16[16,32,2048]{2,1,0:T(8,128)(2,1)S(1)} slice(bf16[32,32,2048]{2,1,0:T(8,128)(2,1)} %all-to-all-done.right_ref.early_hbm), slice={[0:16], [0:32], [0:2048]} | slice | bytes 4194304 | tf_op jit(solution)/shard_map/slice | solution.py:339
  77.6 5.9 %collective-permute-start = (bf16[16,32,2048]{2,1,0:T(8,128)(2,1)S(1)}, bf16[16,32,2048]{2,1,0:T(8,128)(2,1)}, u32[]{:S(2)}, u32[]{:S(2)}) collective-permute-start(bf16[16,32,2048]{2,1,0:T(8,128)(2,1)S(1)} %slice.8), channel_id=1, source_target_pairs={{0,28},{4,0},{8,4},{12,8},{16,12},{20,16},{24,20},{28,24},{1,29},{... | collective-permute-start | bytes 6291464 | tf_op jit(solution)/shard_map/ppermute | solution.py:339
  83.5 1.3 slice.9
  84.8 0.1 collective-permute-start.1
  84.9 26.1 %collective-permute-done.1.left_ref = bf16[8,32,2048]{2,1,0:T(8,128)(2,1)S(1)} collective-permute-done((bf16[8,32,2048]{2,1,0:T(8,128)(2,1)S(1)}, bf16[8,32,2048]{2,1,0:T(8,128)(2,1)S(1)}, u32[]{:S(2)}, u32[]{:S(2)}) %collective-permute-start.1) | collective-permute-done | bytes 1048608 | tf_op jit(solution)/shard_map/ppermute | solution.py:338
  111.0 1.7 %corner.1 = bf16[4,32,128]{2,1,0:T(8,128)(2,1)S(1)} custom-call(bf16[8,32,2048]{2,1,0:T(8,128)(2,1)S(1)} %collective-permute-done.1.left_ref, bf16[32,32,2048]{2,1,0:T(8,128)(2,1)} %all-to-all-done.right_ref.early_hbm), custom_call_target="tpu_custom_call" | custom-call | flops 67108864 | bytes 2097152 | tf_op jit(solution)/shard_map/corner/pallas_call | solution.py:126
  112.7 0.1 collective-permute-start.2
  112.8 0.0 copy-start.6
  112.8 17.9 %all-to-all-done.1.late_hbm = bf16[32,32,2048]{2,1,0:T(8,128)(2,1)} async-done(((bf16[32,32,2048]{2,1,0:T(8,128)(2,1)}), bf16[32,32,2048]{2,1,0:T(8,128)(2,1)}, u32[]{:S(2)}, u32[]{:S(2)}) %all-to-all-start.1) | async-done | bytes 4194336 | tf_op jit(solution)/shard_map/all_to_all | solution.py:334
  130.7 0.0 collective-permute-done.2.corner_hbm
  130.7 0.0 collective-permute-done.after_hbm
  130.7 5.8 %contract.1 = bf16[32,32,256]{2,1,0:T(8,128)(2,1)} custom-call(bf16[32,32,2048]{2,1,0:T(8,128)(2,1)} %all-to-all-done.right_ref.early_hbm, bf16[32,32,2048]{2,1,0:T(8,128)(2,1)} %all-to-all-done.1.late_hbm, bf16[16,32,2048]{2,1,0:T(8,128)(2,1)} %collective-permute-done.after_hbm, bf16[4,32,128]{2,1,0:T(8,128)(2,1)S(1)} %collective-permute-done.2.corner_hbm), custom_call_target="tpu_custom_call" | custom-call | flops 1610612736 | bytes 11534336 | tf_op jit(solution)/shard_map/contract/pallas_call | solution.py:214
  136.5 6.2 %all-to-all-start.2 = ((bf16[32,32,256]{2,1,0:T(8,128)(2,1)}), bf16[32,32,256]{2,1,0:T(8,128)(2,1)S(1)}, u32[]{:S(2)}, u32[]{:S(2)}) async-start(bf16[32,32,256]{2,1,0:T(8,128)(2,1)} %contract.1), calls=%async_computation.2 | async-start | bytes 1048576 | tf_op jit(solution)/shard_map/all_to_all | solution.py:334
  142.7 0.0 copy-done.6
  142.7 0.0 copy-start.1
  142.7 2.2 %copy-done.1 = bf16[8,2048,128]{2,1,0:T(8,128)(2,1)S(1)} copy-done((bf16[8,2048,128]{2,1,0:T(8,128)(2,1)S(1)}, bf16[8,2048,128]{2,1,0:T(8,128)(2,1)}, u32[]{:S(2)}) %copy-start.1) | copy-done | bytes 4194328
  144.9 0.0 copy-start.7
  144.9 0.0 copy-start.10
  144.9 0.0 copy-start.11
  144.9 0.8 gate.1.gate_ref
  145.7 7.1 %all-to-all-done.2.triangle_ref = bf16[32,32,256]{2,1,0:T(8,128)(2,1)S(1)} async-done(((bf16[32,32,256]{2,1,0:T(8,128)(2,1)}), bf16[32,32,256]{2,1,0:T(8,128)(2,1)S(1)}, u32[]{:S(2)}, u32[]{:S(2)}) %all-to-all-start.2) | async-done | bytes 524320 | tf_op jit(solution)/shard_map/all_to_all | solution.py:334
  152.8 0.0 copy-done.7
  152.8 0.0 copy-done.10
  152.8 0.0 copy-done.11
  152.8 1.6 %finish.1 = bf16[8,256,128]{2,1,0:T(8,128)(2,1)} custom-call(bf16[32,32,256]{2,1,0:T(8,128)(2,1)S(1)} %all-to-all-done.2.triangle_ref, f32[8,256,128]{2,1,0:T(8,128)S(1)} %gate.1.gate_ref, f32[1,128]{1,0:T(1,128)S(1)} %bitcast.13, f32[1,128]{1,0:T(1,128)S(1)} %bitcast.14, bf16[128,128]{1,0:T(8,128)(2,1)S(1)} %copy-done.7), custom_call_target="tpu_custom_call" | custom-call | flops 67108864 | bytes 2097152 | tf_op jit(solution)/shard_map/finish/pallas_call | solution.py:255
Async XLA Ops:
  8.6 7.8 %copy-start.3 = (s32[8,2048]{1,0:T(8,128)S(1)}, s32[8,2048]{1,0:T(8,128)}, u32[]{:S(2)}) copy-start(s32[8,2048]{1,0:T(8,128)} %mask_ref.3) | copy-start | bytes 196612
  8.6 7.8 %copy-start.4 = (bf16[128,256]{1,0:T(8,128)(2,1)S(1)}, bf16[128,256]{1,0:T(8,128)(2,1)}, u32[]{:S(2)}) copy-start(bf16[128,256]{1,0:T(8,128)(2,1)} %value_ref.3) | copy-start | bytes 196612
  8.6 7.8 %copy-start.5 = (bf16[128,256]{1,0:T(8,128)(2,1)S(1)}, bf16[128,256]{1,0:T(8,128)(2,1)}, u32[]{:S(2)}) copy-start(bf16[128,256]{1,0:T(8,128)(2,1)} %gate_ref.3) | copy-start | bytes 196612
  8.6 7.8 %copy-start.8 = (f32[128]{0:T(128)S(1)}, f32[128]{0:T(128)}, u32[]{:S(2)}) copy-start(f32[128]{0:T(128)} %param.12) | copy-start | bytes 1540
  8.7 7.8 %copy-start.9 = (f32[128]{0:T(128)S(1)}, f32[128]{0:T(128)}, u32[]{:S(2)}) copy-start(f32[128]{0:T(128)} %param.13) | copy-start | bytes 1540
  8.7 62.5 %all-to-all-start = ((bf16[32,32,2048]{2,1,0:T(8,128)(2,1)}), bf16[32,32,2048]{2,1,0:T(8,128)(2,1)}, u32[]{:S(2)}, u32[]{:S(2)}) async-start(bf16[32,32,2048]{2,1,0:T(8,128)(2,1)} %project.2), calls=%async_computation | async-start | bytes 8388608 | tf_op jit(solution)/shard_map/all_to_all | solution.py:334
  16.5 2.2 %copy-start = (bf16[8,2048,128]{2,1,0:T(8,128)(2,1)S(1)}, bf16[8,2048,128]{2,1,0:T(8,128)(2,1)}, u32[]{:S(2)}) copy-start(bf16[8,2048,128]{2,1,0:T(8,128)(2,1)} %p3.1) | copy-start | bytes 12582916
  25.7 2.0 %copy-start.2 = (bf16[32,32,2048]{2,1,0:T(8,128)(2,1)}, bf16[32,32,2048]{2,1,0:T(8,128)(2,1)S(1)}, u32[]{:S(2)}) copy-start(bf16[32,32,2048]{2,1,0:T(8,128)(2,1)S(1)} %project.3) | copy-start | bytes 12582916
  71.2 59.5 %all-to-all-start.1 = ((bf16[32,32,2048]{2,1,0:T(8,128)(2,1)}), bf16[32,32,2048]{2,1,0:T(8,128)(2,1)}, u32[]{:S(2)}, u32[]{:S(2)}) async-start(bf16[32,32,2048]{2,1,0:T(8,128)(2,1)} %copy-done.2), calls=%async_computation.1 | async-start | bytes 8388608 | tf_op jit(solution)/shard_map/all_to_all | solution.py:334
  77.6 53.1 %collective-permute-start = (bf16[16,32,2048]{2,1,0:T(8,128)(2,1)S(1)}, bf16[16,32,2048]{2,1,0:T(8,128)(2,1)}, u32[]{:S(2)}, u32[]{:S(2)}) collective-permute-start(bf16[16,32,2048]{2,1,0:T(8,128)(2,1)S(1)} %slice.8), channel_id=1, source_target_pairs={{0,28},{4,0},{8,4},{12,8},{16,12},{20,16},{24,20},{28,24},{1,29},{... | collective-permute-start | bytes 6291464 | tf_op jit(solution)/shard_map/ppermute | solution.py:339
  84.8 26.1 %collective-permute-start.1 = (bf16[8,32,2048]{2,1,0:T(8,128)(2,1)S(1)}, bf16[8,32,2048]{2,1,0:T(8,128)(2,1)S(1)}, u32[]{:S(2)}, u32[]{:S(2)}) collective-permute-start(bf16[8,32,2048]{2,1,0:T(8,128)(2,1)S(1)} %slice.9), channel_id=1, source_target_pairs={{0,4},{4,8},{8,12},{12,16},{16,20},{20,24},{24,28},{28,0},{1,5},{5... | collective-permute-start | bytes 3145736 | tf_op jit(solution)/shard_map/ppermute | solution.py:338
  112.7 18.0 %collective-permute-start.2 = (bf16[4,32,128]{2,1,0:T(8,128)(2,1)S(1)}, bf16[4,32,128]{2,1,0:T(8,128)(2,1)S(1)}, u32[]{:S(2)}, u32[]{:S(2)}) collective-permute-start(bf16[4,32,128]{2,1,0:T(8,128)(2,1)S(1)} %corner.1), channel_id=1, source_target_pairs={{0,28},{4,0},{8,4},{12,8},{16,12},{20,16},{24,20},{28,24},{1,29},{... | collective-permute-start | bytes 98312 | tf_op jit(solution)/shard_map/ppermute | solution.py:340
  112.8 29.9 %copy-start.6 = (bf16[128,128]{1,0:T(8,128)(2,1)S(1)}, bf16[128,128]{1,0:T(8,128)(2,1)}, u32[]{:S(2)}) copy-start(bf16[128,128]{1,0:T(8,128)(2,1)} %w_ref.2) | copy-start | bytes 98308
  136.5 16.3 %all-to-all-start.2 = ((bf16[32,32,256]{2,1,0:T(8,128)(2,1)}), bf16[32,32,256]{2,1,0:T(8,128)(2,1)S(1)}, u32[]{:S(2)}, u32[]{:S(2)}) async-start(bf16[32,32,256]{2,1,0:T(8,128)(2,1)} %contract.1), calls=%async_computation.2 | async-start | bytes 1048576 | tf_op jit(solution)/shard_map/all_to_all | solution.py:334
  142.7 2.2 %copy-start.1 = (bf16[8,2048,128]{2,1,0:T(8,128)(2,1)S(1)}, bf16[8,2048,128]{2,1,0:T(8,128)(2,1)}, u32[]{:S(2)}) copy-start(bf16[8,2048,128]{2,1,0:T(8,128)(2,1)} %p3.1) | copy-start | bytes 12582916
  144.9 7.9 %copy-start.7 = (bf16[128,128]{1,0:T(8,128)(2,1)S(1)}, bf16[128,128]{1,0:T(8,128)(2,1)}, u32[]{:S(2)}) copy-start(bf16[128,128]{1,0:T(8,128)(2,1)} %w_ref.3) | copy-start | bytes 98308
  144.9 7.9 %copy-start.10 = (f32[128]{0:T(128)S(1)}, f32[128]{0:T(128)}, u32[]{:S(2)}) copy-start(f32[128]{0:T(128)} %param.17) | copy-start | bytes 1540
  144.9 7.9 %copy-start.11 = (f32[128]{0:T(128)S(1)}, f32[128]{0:T(128)}, u32[]{:S(2)}) copy-start(f32[128]{0:T(128)} %param.18) | copy-start | bytes 1540

commit v8 on v7

--- a/solution.py
+++ b/solution.py
@@ -141,7 +141,8 @@
 
 
 def contract_kernel(
-    early_hbm, late_hbm, after_hbm, corner_hbm, out_ref, early, late, after, corner_ref, total, sems, corner_sem
+    early_hbm, late_hbm, after_hbm, corner_hbm, out_hbm, early, late, after, corner_ref, out_ref, total, sems,
+    corner_sem, out_sems
 ):
     halves = OWN // 2
     pairs = ((early_hbm, early), (late_hbm, late), (after_hbm, after))
@@ -161,6 +162,12 @@
                 copy.start()
     corner_copy = pltpu.make_async_copy(corner_hbm, corner_ref, corner_sem)
     corner_copy.start()
+    stores = [
+        pltpu.make_async_copy(
+            out_ref.at[:, pl.ds(half * 16, 16), :], out_hbm.at[:, pl.ds(half * 16, 16), :], out_sems.at[half]
+        )
+        for half in range(halves)
+    ]
     groups = BLOCK // SUB
     rest = slice(0, (STEPS - 1) * groups)
     last = slice((STEPS - 1) * groups, STEPS * groups)
@@ -204,24 +211,28 @@
                 out_ref[
                     block * groups : (block + 1) * groups, half * 16 : (half + 1) * 16, :
                 ] = jnp.concatenate(band, axis=1).astype(BF16)
+            stores[half].start()
+    for store in stores:
+        store.wait()
 
 
 def contract(early, late, after, returned):
     hbm = pl.BlockSpec(memory_space=pltpu.HBM)
     anywhere = pl.BlockSpec(memory_space=pl.ANY)
-    vmem = pl.BlockSpec(memory_space=pltpu.VMEM)
     window = BLOCK * (2 * STEPS - 2)
     return pl.pallas_call(
         contract_kernel,
         in_specs=[hbm, hbm, anywhere, anywhere],
-        out_specs=vmem,
+        out_specs=hbm,
         out_shape=jax.ShapeDtypeStruct((PARTS, OWN * SUB, STEPS * BLOCK), BF16),
         scratch_shapes=[pltpu.VMEM(v.shape, BF16) for v in (early, late, after)]
         + [
             pltpu.VMEM(returned.shape, BF16),
+            pltpu.VMEM((PARTS, OWN * SUB, STEPS * BLOCK), BF16),
             pltpu.VMEM((OWN, BLOCK * STEPS, window), F32),
             pltpu.SemaphoreType.DMA((OWN // 2 * len(DOTS), 3)),
             pltpu.SemaphoreType.DMA(()),
+            pltpu.SemaphoreType.DMA((OWN // 2,)),
         ],
         compiler_params=pltpu.CompilerParams(vmem_limit_bytes=VMEM_CONTRACT),
         cost_estimate=pl.CostEstimate(

time: 157 us -> 157 us (level)
  no operation moved by 1% of the time
where the time goes in v8:
time: 157 us; the launch traced here: 154 us
  waiting for transfers between devices  94.6 us (60%)
  Pallas kernels  25.4 us (16%)
  starting transfers between devices  24.7 us (16%)
  local copies, waits for them, and re-layouts  9.4 us (6%)
    all_to_all x3, waiting for transfers between devices, spread(): return lax.all_to_all(value, PLANE, 0, 0, tiled=True)  68.5 us
    ppermute x1, waiting for transfers between devices, on_device(): above = lax.ppermute(early[(STEPS - 1) * groups:], 'z', up)  26.1 us
    all_to_all x3, starting transfers between devices, spread(): return lax.all_to_all(value, PLANE, 0, 0, tiled=True)  18.6 us
    pallas_call x2, Pallas kernels, project(): pl.pallas_call(project_kernel, grid_spec=spec, out_shape=jax.ShapeDtypeSt...  15.6 us
    unnamed x24, local copies, waits for them, and re-layouts  6.38 us
    ppermute x1, starting transfers between devices, on_device(): after = lax.ppermute(early[:2 * groups], 'z', down)  5.94 us
    pallas_call x1, Pallas kernels, contract(): pl.pallas_call(contract_kernel, in_specs=[hbm, hbm, anywhere, anywhere],...  5.71 us
  transfers between devices with their start and end apart: 6, of which 4 were waited for; matrix products, arithmetic and copies ran while one was open for 2% of the time, Pallas kernels for 6%

profile of v8, /device:TPU:8, one launch (start us, length us, event | category | flops | bytes accessed | tf_op | source)
XLA Modules:
  0.0 154.3 jit_solution(13449945461466096468)
XLA Ops:
  0.0 8.6 %project.2 = bf16[32,32,2048]{2,1,0:T(8,128)(2,1)} custom-call(s32[1]{0:T(128)} %bitcast.side_ref, bf16[8,2048,128]{2,1,0:T(8,128)(2,1)} %p3.1, s32[8,2048]{1,0:T(8,128)} %mask_ref.3, f32[1,128]{1,0:T(1,128)} %bitcast.7, f32[1,128]{1,0:T(1,128)} %bitcast.10, bf16[128,256]{1,0:T(8,128)(2,1)} %value_ref.3, bf16[128,256]{1,0:T(8,128)(2,1)} %gate_ref.3), custom_call_target="tpu_custom_call" | custom-call | flops 1610612736 | bytes 8388608 | tf_op jit(solution)/shard_map/project/pallas_call | solution.py:91
  8.6 0.0 copy-start.3
  8.6 0.0 copy-start.4
  8.6 0.0 copy-start.5
  8.6 0.0 copy-start.8
  8.7 0.0 copy-start.9
  8.7 7.7 %all-to-all-start = ((bf16[32,32,2048]{2,1,0:T(8,128)(2,1)}), bf16[32,32,2048]{2,1,0:T(8,128)(2,1)}, u32[]{:S(2)}, u32[]{:S(2)}) async-start(bf16[32,32,2048]{2,1,0:T(8,128)(2,1)} %project.2), calls=%async_computation | async-start | bytes 8388608 | tf_op jit(solution)/shard_map/all_to_all | solution.py:345
  16.4 0.0 copy-done.3
  16.4 0.0 copy-done.4
  16.4 0.0 copy-done.5
  16.4 0.0 copy-done.8
  16.5 0.0 copy-done.9
  16.5 0.0 copy-start
  16.5 2.2 %copy-done = bf16[8,2048,128]{2,1,0:T(8,128)(2,1)S(1)} copy-done((bf16[8,2048,128]{2,1,0:T(8,128)(2,1)S(1)}, bf16[8,2048,128]{2,1,0:T(8,128)(2,1)}, u32[]{:S(2)}) %copy-start) | copy-done | bytes 4194328
  18.7 7.0 %project.3 = bf16[32,32,2048]{2,1,0:T(8,128)(2,1)S(1)} custom-call(s32[1]{0:T(128)} %bitcast.3.side_ref, bf16[8,2048,128]{2,1,0:T(8,128)(2,1)S(1)} %copy-done, s32[8,2048]{1,0:T(8,128)S(1)} %copy-done.3, f32[1,128]{1,0:T(1,128)S(1)} %bitcast.8, f32[1,128]{1,0:T(1,128)S(1)} %bitcast.11, bf16[128,256]{1,0:T(8,128)(2,1)S(1)} %copy-done.4, ...), custom_call_target="tpu_custom_call" | custom-call | flops 1610612736 | bytes 8388608 | tf_op jit(solution)/shard_map/project/pallas_call | solution.py:91
  25.7 0.0 copy-start.2
  25.7 2.0 %copy-done.2 = bf16[32,32,2048]{2,1,0:T(8,128)(2,1)} copy-done((bf16[32,32,2048]{2,1,0:T(8,128)(2,1)}, bf16[32,32,2048]{2,1,0:T(8,128)(2,1)S(1)}, u32[]{:S(2)}) %copy-start.2) | copy-done | bytes 4194328
  27.6 43.6 %all-to-all-done.right_ref.early_hbm = bf16[32,32,2048]{2,1,0:T(8,128)(2,1)} async-done(((bf16[32,32,2048]{2,1,0:T(8,128)(2,1)}), bf16[32,32,2048]{2,1,0:T(8,128)(2,1)}, u32[]{:S(2)}, u32[]{:S(2)}) %all-to-all-start) | async-done | bytes 4194336 | tf_op jit(solution)/shard_map/all_to_all | solution.py:345
  71.2 4.6 %all-to-all-start.1 = ((bf16[32,32,2048]{2,1,0:T(8,128)(2,1)}), bf16[32,32,2048]{2,1,0:T(8,128)(2,1)}, u32[]{:S(2)}, u32[]{:S(2)}) async-start(bf16[32,32,2048]{2,1,0:T(8,128)(2,1)} %copy-done.2), calls=%async_computation.1 | async-start | bytes 8388608 | tf_op jit(solution)/shard_map/all_to_all | solution.py:345
  75.9 1.7 %slice.8 = bf16[16,32,2048]{2,1,0:T(8,128)(2,1)S(1)} slice(bf16[32,32,2048]{2,1,0:T(8,128)(2,1)} %all-to-all-done.right_ref.early_hbm), slice={[0:16], [0:32], [0:2048]} | slice | bytes 4194304 | tf_op jit(solution)/shard_map/slice | solution.py:350
  77.6 5.9 %collective-permute-start = (bf16[16,32,2048]{2,1,0:T(8,128)(2,1)S(1)}, bf16[16,32,2048]{2,1,0:T(8,128)(2,1)}, u32[]{:S(2)}, u32[]{:S(2)}) collective-permute-start(bf16[16,32,2048]{2,1,0:T(8,128)(2,1)S(1)} %slice.8), channel_id=1, source_target_pairs={{0,28},{4,0},{8,4},{12,8},{16,12},{20,16},{24,20},{28,24},{1,29},{... | collective-permute-start | bytes 6291464 | tf_op jit(solution)/shard_map/ppermute | solution.py:350
  83.5 1.3 slice.9
  84.8 0.1 collective-permute-start.1
  84.9 26.1 %collective-permute-done.1.left_ref = bf16[8,32,2048]{2,1,0:T(8,128)(2,1)S(1)} collective-permute-done((bf16[8,32,2048]{2,1,0:T(8,128)(2,1)S(1)}, bf16[8,32,2048]{2,1,0:T(8,128)(2,1)S(1)}, u32[]{:S(2)}, u32[]{:S(2)}) %collective-permute-start.1) | collective-permute-done | bytes 1048608 | tf_op jit(solution)/shard_map/ppermute | solution.py:349
  111.0 1.7 %corner.1 = bf16[4,32,128]{2,1,0:T(8,128)(2,1)S(1)} custom-call(bf16[8,32,2048]{2,1,0:T(8,128)(2,1)S(1)} %collective-permute-done.1.left_ref, bf16[32,32,2048]{2,1,0:T(8,128)(2,1)} %all-to-all-done.right_ref.early_hbm), custom_call_target="tpu_custom_call" | custom-call | flops 67108864 | bytes 2097152 | tf_op jit(solution)/shard_map/corner/pallas_call | solution.py:126
  112.7 0.1 collective-permute-start.2
  112.8 0.0 copy-start.6
  112.8 17.9 %all-to-all-done.1.late_hbm = bf16[32,32,2048]{2,1,0:T(8,128)(2,1)} async-done(((bf16[32,32,2048]{2,1,0:T(8,128)(2,1)}), bf16[32,32,2048]{2,1,0:T(8,128)(2,1)}, u32[]{:S(2)}, u32[]{:S(2)}) %all-to-all-start.1) | async-done | bytes 4194336 | tf_op jit(solution)/shard_map/all_to_all | solution.py:345
  130.7 0.0 collective-permute-done.2.corner_hbm
  130.7 0.0 collective-permute-done.after_hbm
  130.7 5.7 %contract.1 = bf16[32,32,256]{2,1,0:T(8,128)(2,1)} custom-call(bf16[32,32,2048]{2,1,0:T(8,128)(2,1)} %all-to-all-done.right_ref.early_hbm, bf16[32,32,2048]{2,1,0:T(8,128)(2,1)} %all-to-all-done.1.late_hbm, bf16[16,32,2048]{2,1,0:T(8,128)(2,1)} %collective-permute-done.after_hbm, bf16[4,32,128]{2,1,0:T(8,128)(2,1)S(1)} %collective-permute-done.2.corner_hbm), custom_call_target="tpu_custom_call" | custom-call | flops 1610612736 | bytes 11534336 | tf_op jit(solution)/shard_map/contract/pallas_call | solution.py:223
  136.4 6.2 %all-to-all-start.2 = ((bf16[32,32,256]{2,1,0:T(8,128)(2,1)}), bf16[32,32,256]{2,1,0:T(8,128)(2,1)S(1)}, u32[]{:S(2)}, u32[]{:S(2)}) async-start(bf16[32,32,256]{2,1,0:T(8,128)(2,1)} %contract.1), calls=%async_computation.2 | async-start | bytes 1048576 | tf_op jit(solution)/shard_map/all_to_all | solution.py:345
  142.6 0.0 copy-done.6
  142.6 0.0 copy-start.1
  142.6 2.2 %copy-done.1 = bf16[8,2048,128]{2,1,0:T(8,128)(2,1)S(1)} copy-done((bf16[8,2048,128]{2,1,0:T(8,128)(2,1)S(1)}, bf16[8,2048,128]{2,1,0:T(8,128)(2,1)}, u32[]{:S(2)}) %copy-start.1) | copy-done | bytes 4194328
  144.8 0.0 copy-start.7
  144.8 0.0 copy-start.10
  144.8 0.0 copy-start.11
  144.8 0.8 gate.1.gate_ref
  145.6 7.1 %all-to-all-done.2.triangle_ref = bf16[32,32,256]{2,1,0:T(8,128)(2,1)S(1)} async-done(((bf16[32,32,256]{2,1,0:T(8,128)(2,1)}), bf16[32,32,256]{2,1,0:T(8,128)(2,1)S(1)}, u32[]{:S(2)}, u32[]{:S(2)}) %all-to-all-start.2) | async-done | bytes 524320 | tf_op jit(solution)/shard_map/all_to_all | solution.py:345
  152.7 0.0 copy-done.7
  152.7 0.0 copy-done.10
  152.7 0.0 copy-done.11
  152.7 1.6 %finish.1 = bf16[8,256,128]{2,1,0:T(8,128)(2,1)} custom-call(bf16[32,32,256]{2,1,0:T(8,128)(2,1)S(1)} %all-to-all-done.2.triangle_ref, f32[8,256,128]{2,1,0:T(8,128)S(1)} %gate.1.gate_ref, f32[1,128]{1,0:T(1,128)S(1)} %bitcast.13, f32[1,128]{1,0:T(1,128)S(1)} %bitcast.14, bf16[128,128]{1,0:T(8,128)(2,1)S(1)} %copy-done.7), custom_call_target="tpu_custom_call" | custom-call | flops 67108864 | bytes 2097152 | tf_op jit(solution)/shard_map/finish/pallas_call | solution.py:266
Async XLA Ops:
  8.6 7.8 %copy-start.3 = (s32[8,2048]{1,0:T(8,128)S(1)}, s32[8,2048]{1,0:T(8,128)}, u32[]{:S(2)}) copy-start(s32[8,2048]{1,0:T(8,128)} %mask_ref.3) | copy-start | bytes 196612
  8.6 7.8 %copy-start.4 = (bf16[128,256]{1,0:T(8,128)(2,1)S(1)}, bf16[128,256]{1,0:T(8,128)(2,1)}, u32[]{:S(2)}) copy-start(bf16[128,256]{1,0:T(8,128)(2,1)} %value_ref.3) | copy-start | bytes 196612
  8.6 7.8 %copy-start.5 = (bf16[128,256]{1,0:T(8,128)(2,1)S(1)}, bf16[128,256]{1,0:T(8,128)(2,1)}, u32[]{:S(2)}) copy-start(bf16[128,256]{1,0:T(8,128)(2,1)} %gate_ref.3) | copy-start | bytes 196612
  8.6 7.8 %copy-start.8 = (f32[128]{0:T(128)S(1)}, f32[128]{0:T(128)}, u32[]{:S(2)}) copy-start(f32[128]{0:T(128)} %param.12) | copy-start | bytes 1540
  8.7 7.8 %copy-start.9 = (f32[128]{0:T(128)S(1)}, f32[128]{0:T(128)}, u32[]{:S(2)}) copy-start(f32[128]{0:T(128)} %param.13) | copy-start | bytes 1540
  8.7 62.5 %all-to-all-start = ((bf16[32,32,2048]{2,1,0:T(8,128)(2,1)}), bf16[32,32,2048]{2,1,0:T(8,128)(2,1)}, u32[]{:S(2)}, u32[]{:S(2)}) async-start(bf16[32,32,2048]{2,1,0:T(8,128)(2,1)} %project.2), calls=%async_computation | async-start | bytes 8388608 | tf_op jit(solution)/shard_map/all_to_all | solution.py:345
  16.5 2.2 %copy-start = (bf16[8,2048,128]{2,1,0:T(8,128)(2,1)S(1)}, bf16[8,2048,128]{2,1,0:T(8,128)(2,1)}, u32[]{:S(2)}) copy-start(bf16[8,2048,128]{2,1,0:T(8,128)(2,1)} %p3.1) | copy-start | bytes 12582916
  25.7 2.0 %copy-start.2 = (bf16[32,32,2048]{2,1,0:T(8,128)(2,1)}, bf16[32,32,2048]{2,1,0:T(8,128)(2,1)S(1)}, u32[]{:S(2)}) copy-start(bf16[32,32,2048]{2,1,0:T(8,128)(2,1)S(1)} %project.3) | copy-start | bytes 12582916
  71.2 59.5 %all-to-all-start.1 = ((bf16[32,32,2048]{2,1,0:T(8,128)(2,1)}), bf16[32,32,2048]{2,1,0:T(8,128)(2,1)}, u32[]{:S(2)}, u32[]{:S(2)}) async-start(bf16[32,32,2048]{2,1,0:T(8,128)(2,1)} %copy-done.2), calls=%async_computation.1 | async-start | bytes 8388608 | tf_op jit(solution)/shard_map/all_to_all | solution.py:345
  77.6 53.1 %collective-permute-start = (bf16[16,32,2048]{2,1,0:T(8,128)(2,1)S(1)}, bf16[16,32,2048]{2,1,0:T(8,128)(2,1)}, u32[]{:S(2)}, u32[]{:S(2)}) collective-permute-start(bf16[16,32,2048]{2,1,0:T(8,128)(2,1)S(1)} %slice.8), channel_id=1, source_target_pairs={{0,28},{4,0},{8,4},{12,8},{16,12},{20,16},{24,20},{28,24},{1,29},{... | collective-permute-start | bytes 6291464 | tf_op jit(solution)/shard_map/ppermute | solution.py:350
  84.8 26.1 %collective-permute-start.1 = (bf16[8,32,2048]{2,1,0:T(8,128)(2,1)S(1)}, bf16[8,32,2048]{2,1,0:T(8,128)(2,1)S(1)}, u32[]{:S(2)}, u32[]{:S(2)}) collective-permute-start(bf16[8,32,2048]{2,1,0:T(8,128)(2,1)S(1)} %slice.9), channel_id=1, source_target_pairs={{0,4},{4,8},{8,12},{12,16},{16,20},{20,24},{24,28},{28,0},{1,5},{5... | collective-permute-start | bytes 3145736 | tf_op jit(solution)/shard_map/ppermute | solution.py:349
  112.7 18.0 %collective-permute-start.2 = (bf16[4,32,128]{2,1,0:T(8,128)(2,1)S(1)}, bf16[4,32,128]{2,1,0:T(8,128)(2,1)S(1)}, u32[]{:S(2)}, u32[]{:S(2)}) collective-permute-start(bf16[4,32,128]{2,1,0:T(8,128)(2,1)S(1)} %corner.1), channel_id=1, source_target_pairs={{0,28},{4,0},{8,4},{12,8},{16,12},{20,16},{24,20},{28,24},{1,29},{... | collective-permute-start | bytes 98312 | tf_op jit(solution)/shard_map/ppermute | solution.py:351
  112.8 29.8 %copy-start.6 = (bf16[128,128]{1,0:T(8,128)(2,1)S(1)}, bf16[128,128]{1,0:T(8,128)(2,1)}, u32[]{:S(2)}) copy-start(bf16[128,128]{1,0:T(8,128)(2,1)} %w_ref.2) | copy-start | bytes 98308
  136.4 16.3 %all-to-all-start.2 = ((bf16[32,32,256]{2,1,0:T(8,128)(2,1)}), bf16[32,32,256]{2,1,0:T(8,128)(2,1)S(1)}, u32[]{:S(2)}, u32[]{:S(2)}) async-start(bf16[32,32,256]{2,1,0:T(8,128)(2,1)} %contract.1), calls=%async_computation.2 | async-start | bytes 1048576 | tf_op jit(solution)/shard_map/all_to_all | solution.py:345
  142.6 2.2 %copy-start.1 = (bf16[8,2048,128]{2,1,0:T(8,128)(2,1)S(1)}, bf16[8,2048,128]{2,1,0:T(8,128)(2,1)}, u32[]{:S(2)}) copy-start(bf16[8,2048,128]{2,1,0:T(8,128)(2,1)} %p3.1) | copy-start | bytes 12582916
  144.8 7.9 %copy-start.7 = (bf16[128,128]{1,0:T(8,128)(2,1)S(1)}, bf16[128,128]{1,0:T(8,128)(2,1)}, u32[]{:S(2)}) copy-start(bf16[128,128]{1,0:T(8,128)(2,1)} %w_ref.3) | copy-start | bytes 98308
  144.8 7.9 %copy-start.10 = (f32[128]{0:T(128)S(1)}, f32[128]{0:T(128)}, u32[]{:S(2)}) copy-start(f32[128]{0:T(128)} %param.17) | copy-start | bytes 1540
  144.8 7.9 %copy-start.11 = (f32[128]{0:T(128)S(1)}, f32[128]{0:T(128)}, u32[]{:S(2)}) copy-start(f32[128]{0:T(128)} %param.18) | copy-start | bytes 1540

commit v9 on v8

--- a/solution.py
+++ b/solution.py
@@ -242,7 +242,7 @@
     )(early, late, after, returned)
 
 
-def finish_kernel(triangle_ref, gate_ref, gain_ref, bias_ref, w_ref, out_ref, scaled):
+def finish_kernel(triangle_ref, gate_ref, gain_ref, bias_ref, w_ref, out_hbm, scaled, out_ref, sems):
     width = triangle_ref.shape[2]
     values = triangle_ref[...].astype(F32).reshape(128, SUB, width)
     centred = values - jnp.sum(values, axis=0, keepdims=True) * (1.0 / 128)
@@ -258,6 +258,9 @@
         held = (jnp.concatenate(mine, axis=1) * gain + bias).astype(BF16)
         projected = dot(held, w_ref[...], ((0,), (0,)))
         out_ref[row] = (projected * gate_ref[row]).astype(BF16)
+        pltpu.make_async_copy(out_ref.at[row], out_hbm.at[row], sems.at[row]).start()
+    for row in range(SUB):
+        pltpu.make_async_copy(out_ref.at[row], out_hbm.at[row], sems.at[row]).wait()
 
 
 def finish(triangle, gate, gain, bias, w_out):
@@ -273,9 +276,13 @@
             pl.BlockSpec((1, 128), whole),
             pl.BlockSpec((128, 128), whole),
         ],
-        out_specs=pl.BlockSpec((SUB, width, 128), lambda i: (0, i, 0)),
+        out_specs=pl.BlockSpec(memory_space=pltpu.HBM),
         out_shape=jax.ShapeDtypeStruct((SUB, STEPS * BLOCK, 128), BF16),
-        scratch_shapes=[pltpu.VMEM((SUB * width + SUB, 128), F32)],
+        scratch_shapes=[
+            pltpu.VMEM((SUB * width + SUB, 128), F32),
+            pltpu.VMEM((SUB, width, 128), BF16),
+            pltpu.SemaphoreType.DMA((SUB,)),
+        ],
         compiler_params=pltpu.CompilerParams(vmem_limit_bytes=VMEM_SMALL),
         cost_estimate=pl.CostEstimate(
             flops=SUB * 256 * 128 * 256, bytes_accessed=2 * 1024 * 1024, transcendentals=2048

time: 157 us -> 157 us (level)
  no operation moved by 1% of the time
where the time goes in v9:
time: 157 us; the launch traced here: 154 us
  waiting for transfers between devices  94.6 us (60%)
  Pallas kernels  25.4 us (16%)
  starting transfers between devices  24.7 us (16%)
  local copies, waits for them, and re-layouts  9.4 us (6%)
    all_to_all x3, waiting for transfers between devices, spread(): return lax.all_to_all(value, PLANE, 0, 0, tiled=True)  68.5 us
    ppermute x1, waiting for transfers between devices, on_device(): above = lax.ppermute(early[(STEPS - 1) * groups:], 'z', up)  26.1 us
    all_to_all x3, starting transfers between devices, spread(): return lax.all_to_all(value, PLANE, 0, 0, tiled=True)  18.6 us
    pallas_call x2, Pallas kernels, project(): pl.pallas_call(project_kernel, grid_spec=spec, out_shape=jax.ShapeDtypeSt...  15.6 us
    unnamed x24, local copies, waits for them, and re-layouts  6.38 us
    ppermute x1, starting transfers between devices, on_device(): after = lax.ppermute(early[:2 * groups], 'z', down)  5.94 us
    pallas_call x1, Pallas kernels, contract(): pl.pallas_call(contract_kernel, in_specs=[hbm, hbm, anywhere, anywhere],...  5.71 us
  transfers between devices with their start and end apart: 6, of which 4 were waited for; matrix products, arithmetic and copies ran while one was open for 2% of the time, Pallas kernels for 6%

profile of v9, /device:TPU:8, one launch (start us, length us, event | category | flops | bytes accessed | tf_op | source)
XLA Modules:
  0.0 154.3 jit_solution(12350683252331904403)
XLA Ops:
  0.0 8.6 %project.2 = bf16[32,32,2048]{2,1,0:T(8,128)(2,1)} custom-call(s32[1]{0:T(128)} %bitcast.side_ref, bf16[8,2048,128]{2,1,0:T(8,128)(2,1)} %p3.1, s32[8,2048]{1,0:T(8,128)} %mask_ref.3, f32[1,128]{1,0:T(1,128)} %bitcast.7, f32[1,128]{1,0:T(1,128)} %bitcast.10, bf16[128,256]{1,0:T(8,128)(2,1)} %value_ref.3, bf16[128,256]{1,0:T(8,128)(2,1)} %gate_ref.3), custom_call_target="tpu_custom_call" | custom-call | flops 1610612736 | bytes 8388608 | tf_op jit(solution)/shard_map/project/pallas_call | solution.py:91
  8.6 0.0 copy-start.3
  8.6 0.0 copy-start.4
  8.6 0.0 copy-start.5
  8.6 0.0 copy-start.8
  8.7 0.0 copy-start.9
  8.7 7.7 %all-to-all-start = ((bf16[32,32,2048]{2,1,0:T(8,128)(2,1)}), bf16[32,32,2048]{2,1,0:T(8,128)(2,1)}, u32[]{:S(2)}, u32[]{:S(2)}) async-start(bf16[32,32,2048]{2,1,0:T(8,128)(2,1)} %project.2), calls=%async_computation | async-start | bytes 8388608 | tf_op jit(solution)/shard_map/all_to_all | solution.py:352
  16.4 0.0 copy-done.3
  16.4 0.0 copy-done.4
  16.4 0.0 copy-done.5
  16.4 0.0 copy-done.8
  16.5 0.0 copy-done.9
  16.5 0.0 copy-start
  16.5 2.2 %copy-done = bf16[8,2048,128]{2,1,0:T(8,128)(2,1)S(1)} copy-done((bf16[8,2048,128]{2,1,0:T(8,128)(2,1)S(1)}, bf16[8,2048,128]{2,1,0:T(8,128)(2,1)}, u32[]{:S(2)}) %copy-start) | copy-done | bytes 4194328
  18.7 7.0 %project.3 = bf16[32,32,2048]{2,1,0:T(8,128)(2,1)S(1)} custom-call(s32[1]{0:T(128)} %bitcast.3.side_ref, bf16[8,2048,128]{2,1,0:T(8,128)(2,1)S(1)} %copy-done, s32[8,2048]{1,0:T(8,128)S(1)} %copy-done.3, f32[1,128]{1,0:T(1,128)S(1)} %bitcast.8, f32[1,128]{1,0:T(1,128)S(1)} %bitcast.11, bf16[128,256]{1,0:T(8,128)(2,1)S(1)} %copy-done.4, ...), custom_call_target="tpu_custom_call" | custom-call | flops 1610612736 | bytes 8388608 | tf_op jit(solution)/shard_map/project/pallas_call | solution.py:91
  25.7 0.0 copy-start.2
  25.7 2.0 %copy-done.2 = bf16[32,32,2048]{2,1,0:T(8,128)(2,1)} copy-done((bf16[32,32,2048]{2,1,0:T(8,128)(2,1)}, bf16[32,32,2048]{2,1,0:T(8,128)(2,1)S(1)}, u32[]{:S(2)}) %copy-start.2) | copy-done | bytes 4194328
  27.6 43.6 %all-to-all-done.right_ref.early_hbm = bf16[32,32,2048]{2,1,0:T(8,128)(2,1)} async-done(((bf16[32,32,2048]{2,1,0:T(8,128)(2,1)}), bf16[32,32,2048]{2,1,0:T(8,128)(2,1)}, u32[]{:S(2)}, u32[]{:S(2)}) %all-to-all-start) | async-done | bytes 4194336 | tf_op jit(solution)/shard_map/all_to_all | solution.py:352
  71.2 4.6 %all-to-all-start.1 = ((bf16[32,32,2048]{2,1,0:T(8,128)(2,1)}), bf16[32,32,2048]{2,1,0:T(8,128)(2,1)}, u32[]{:S(2)}, u32[]{:S(2)}) async-start(bf16[32,32,2048]{2,1,0:T(8,128)(2,1)} %copy-done.2), calls=%async_computation.1 | async-start | bytes 8388608 | tf_op jit(solution)/shard_map/all_to_all | solution.py:352
  75.9 1.7 %slice.8 = bf16[16,32,2048]{2,1,0:T(8,128)(2,1)S(1)} slice(bf16[32,32,2048]{2,1,0:T(8,128)(2,1)} %all-to-all-done.right_ref.early_hbm), slice={[0:16], [0:32], [0:2048]} | slice | bytes 4194304 | tf_op jit(solution)/shard_map/slice | solution.py:357
  77.6 5.9 %collective-permute-start = (bf16[16,32,2048]{2,1,0:T(8,128)(2,1)S(1)}, bf16[16,32,2048]{2,1,0:T(8,128)(2,1)}, u32[]{:S(2)}, u32[]{:S(2)}) collective-permute-start(bf16[16,32,2048]{2,1,0:T(8,128)(2,1)S(1)} %slice.8), channel_id=1, source_target_pairs={{0,28},{4,0},{8,4},{12,8},{16,12},{20,16},{24,20},{28,24},{1,29},{... | collective-permute-start | bytes 6291464 | tf_op jit(solution)/shard_map/ppermute | solution.py:357
  83.5 1.3 slice.9
  84.8 0.1 collective-permute-start.1
  84.9 26.1 %collective-permute-done.1.left_ref = bf16[8,32,2048]{2,1,0:T(8,128)(2,1)S(1)} collective-permute-done((bf16[8,32,2048]{2,1,0:T(8,128)(2,1)S(1)}, bf16[8,32,2048]{2,1,0:T(8,128)(2,1)S(1)}, u32[]{:S(2)}, u32[]{:S(2)}) %collective-permute-start.1) | collective-permute-done | bytes 1048608 | tf_op jit(solution)/shard_map/ppermute | solution.py:356
  111.0 1.7 %corner.1 = bf16[4,32,128]{2,1,0:T(8,128)(2,1)S(1)} custom-call(bf16[8,32,2048]{2,1,0:T(8,128)(2,1)S(1)} %collective-permute-done.1.left_ref, bf16[32,32,2048]{2,1,0:T(8,128)(2,1)} %all-to-all-done.right_ref.early_hbm), custom_call_target="tpu_custom_call" | custom-call | flops 67108864 | bytes 2097152 | tf_op jit(solution)/shard_map/corner/pallas_call | solution.py:126
  112.7 0.1 collective-permute-start.2
  112.8 0.0 copy-start.6
  112.8 17.9 %all-to-all-done.1.late_hbm = bf16[32,32,2048]{2,1,0:T(8,128)(2,1)} async-done(((bf16[32,32,2048]{2,1,0:T(8,128)(2,1)}), bf16[32,32,2048]{2,1,0:T(8,128)(2,1)}, u32[]{:S(2)}, u32[]{:S(2)}) %all-to-all-start.1) | async-done | bytes 4194336 | tf_op jit(solution)/shard_map/all_to_all | solution.py:352
  130.7 0.0 collective-permute-done.2.corner_hbm
  130.7 0.0 collective-permute-done.after_hbm
  130.7 5.7 %contract.1 = bf16[32,32,256]{2,1,0:T(8,128)(2,1)} custom-call(bf16[32,32,2048]{2,1,0:T(8,128)(2,1)} %all-to-all-done.right_ref.early_hbm, bf16[32,32,2048]{2,1,0:T(8,128)(2,1)} %all-to-all-done.1.late_hbm, bf16[16,32,2048]{2,1,0:T(8,128)(2,1)} %collective-permute-done.after_hbm, bf16[4,32,128]{2,1,0:T(8,128)(2,1)S(1)} %collective-permute-done.2.corner_hbm), custom_call_target="tpu_custom_call" | custom-call | flops 1610612736 | bytes 11534336 | tf_op jit(solution)/shard_map/contract/pallas_call | solution.py:223
  136.4 6.2 %all-to-all-start.2 = ((bf16[32,32,256]{2,1,0:T(8,128)(2,1)}), bf16[32,32,256]{2,1,0:T(8,128)(2,1)S(1)}, u32[]{:S(2)}, u32[]{:S(2)}) async-start(bf16[32,32,256]{2,1,0:T(8,128)(2,1)} %contract.1), calls=%async_computation.2 | async-start | bytes 1048576 | tf_op jit(solution)/shard_map/all_to_all | solution.py:352
  142.6 0.0 copy-done.6
  142.6 0.0 copy-start.1
  142.6 2.2 %copy-done.1 = bf16[8,2048,128]{2,1,0:T(8,128)(2,1)S(1)} copy-done((bf16[8,2048,128]{2,1,0:T(8,128)(2,1)S(1)}, bf16[8,2048,128]{2,1,0:T(8,128)(2,1)}, u32[]{:S(2)}) %copy-start.1) | copy-done | bytes 4194328
  144.8 0.0 copy-start.7
  144.8 0.0 copy-start.10
  144.8 0.0 copy-start.11
  144.8 0.8 gate.1.gate_ref
  145.6 7.1 %all-to-all-done.2.triangle_ref = bf16[32,32,256]{2,1,0:T(8,128)(2,1)S(1)} async-done(((bf16[32,32,256]{2,1,0:T(8,128)(2,1)}), bf16[32,32,256]{2,1,0:T(8,128)(2,1)S(1)}, u32[]{:S(2)}, u32[]{:S(2)}) %all-to-all-start.2) | async-done | bytes 524320 | tf_op jit(solution)/shard_map/all_to_all | solution.py:352
  152.7 0.0 copy-done.7
  152.7 0.0 copy-done.10
  152.7 0.0 copy-done.11
  152.7 1.6 %finish.1 = bf16[8,256,128]{2,1,0:T(8,128)(2,1)} custom-call(bf16[32,32,256]{2,1,0:T(8,128)(2,1)S(1)} %all-to-all-done.2.triangle_ref, f32[8,256,128]{2,1,0:T(8,128)S(1)} %gate.1.gate_ref, f32[1,128]{1,0:T(1,128)S(1)} %bitcast.13, f32[1,128]{1,0:T(1,128)S(1)} %bitcast.14, bf16[128,128]{1,0:T(8,128)(2,1)S(1)} %copy-done.7), custom_call_target="tpu_custom_call" | custom-call | flops 67108864 | bytes 2097152 | tf_op jit(solution)/shard_map/finish/pallas_call | solution.py:269
Async XLA Ops:
  8.6 7.8 %copy-start.3 = (s32[8,2048]{1,0:T(8,128)S(1)}, s32[8,2048]{1,0:T(8,128)}, u32[]{:S(2)}) copy-start(s32[8,2048]{1,0:T(8,128)} %mask_ref.3) | copy-start | bytes 196612
  8.6 7.8 %copy-start.4 = (bf16[128,256]{1,0:T(8,128)(2,1)S(1)}, bf16[128,256]{1,0:T(8,128)(2,1)}, u32[]{:S(2)}) copy-start(bf16[128,256]{1,0:T(8,128)(2,1)} %value_ref.3) | copy-start | bytes 196612
  8.6 7.8 %copy-start.5 = (bf16[128,256]{1,0:T(8,128)(2,1)S(1)}, bf16[128,256]{1,0:T(8,128)(2,1)}, u32[]{:S(2)}) copy-start(bf16[128,256]{1,0:T(8,128)(2,1)} %gate_ref.3) | copy-start | bytes 196612
  8.6 7.8 %copy-start.8 = (f32[128]{0:T(128)S(1)}, f32[128]{0:T(128)}, u32[]{:S(2)}) copy-start(f32[128]{0:T(128)} %param.12) | copy-start | bytes 1540
  8.7 7.8 %copy-start.9 = (f32[128]{0:T(128)S(1)}, f32[128]{0:T(128)}, u32[]{:S(2)}) copy-start(f32[128]{0:T(128)} %param.13) | copy-start | bytes 1540
  8.7 62.5 %all-to-all-start = ((bf16[32,32,2048]{2,1,0:T(8,128)(2,1)}), bf16[32,32,2048]{2,1,0:T(8,128)(2,1)}, u32[]{:S(2)}, u32[]{:S(2)}) async-start(bf16[32,32,2048]{2,1,0:T(8,128)(2,1)} %project.2), calls=%async_computation | async-start | bytes 8388608 | tf_op jit(solution)/shard_map/all_to_all | solution.py:352
  16.5 2.2 %copy-start = (bf16[8,2048,128]{2,1,0:T(8,128)(2,1)S(1)}, bf16[8,2048,128]{2,1,0:T(8,128)(2,1)}, u32[]{:S(2)}) copy-start(bf16[8,2048,128]{2,1,0:T(8,128)(2,1)} %p3.1) | copy-start | bytes 12582916
  25.7 2.0 %copy-start.2 = (bf16[32,32,2048]{2,1,0:T(8,128)(2,1)}, bf16[32,32,2048]{2,1,0:T(8,128)(2,1)S(1)}, u32[]{:S(2)}) copy-start(bf16[32,32,2048]{2,1,0:T(8,128)(2,1)S(1)} %project.3) | copy-start | bytes 12582916
  71.2 59.5 %all-to-all-start.1 = ((bf16[32,32,2048]{2,1,0:T(8,128)(2,1)}), bf16[32,32,2048]{2,1,0:T(8,128)(2,1)}, u32[]{:S(2)}, u32[]{:S(2)}) async-start(bf16[32,32,2048]{2,1,0:T(8,128)(2,1)} %copy-done.2), calls=%async_computation.1 | async-start | bytes 8388608 | tf_op jit(solution)/shard_map/all_to_all | solution.py:352
  77.6 53.1 %collective-permute-start = (bf16[16,32,2048]{2,1,0:T(8,128)(2,1)S(1)}, bf16[16,32,2048]{2,1,0:T(8,128)(2,1)}, u32[]{:S(2)}, u32[]{:S(2)}) collective-permute-start(bf16[16,32,2048]{2,1,0:T(8,128)(2,1)S(1)} %slice.8), channel_id=1, source_target_pairs={{0,28},{4,0},{8,4},{12,8},{16,12},{20,16},{24,20},{28,24},{1,29},{... | collective-permute-start | bytes 6291464 | tf_op jit(solution)/shard_map/ppermute | solution.py:357
  84.8 26.1 %collective-permute-start.1 = (bf16[8,32,2048]{2,1,0:T(8,128)(2,1)S(1)}, bf16[8,32,2048]{2,1,0:T(8,128)(2,1)S(1)}, u32[]{:S(2)}, u32[]{:S(2)}) collective-permute-start(bf16[8,32,2048]{2,1,0:T(8,128)(2,1)S(1)} %slice.9), channel_id=1, source_target_pairs={{0,4},{4,8},{8,12},{12,16},{16,20},{20,24},{24,28},{28,0},{1,5},{5... | collective-permute-start | bytes 3145736 | tf_op jit(solution)/shard_map/ppermute | solution.py:356
  112.7 18.0 %collective-permute-start.2 = (bf16[4,32,128]{2,1,0:T(8,128)(2,1)S(1)}, bf16[4,32,128]{2,1,0:T(8,128)(2,1)S(1)}, u32[]{:S(2)}, u32[]{:S(2)}) collective-permute-start(bf16[4,32,128]{2,1,0:T(8,128)(2,1)S(1)} %corner.1), channel_id=1, source_target_pairs={{0,28},{4,0},{8,4},{12,8},{16,12},{20,16},{24,20},{28,24},{1,29},{... | collective-permute-start | bytes 98312 | tf_op jit(solution)/shard_map/ppermute | solution.py:358
  112.8 29.8 %copy-start.6 = (bf16[128,128]{1,0:T(8,128)(2,1)S(1)}, bf16[128,128]{1,0:T(8,128)(2,1)}, u32[]{:S(2)}) copy-start(bf16[128,128]{1,0:T(8,128)(2,1)} %w_ref.2) | copy-start | bytes 98308
  136.4 16.3 %all-to-all-start.2 = ((bf16[32,32,256]{2,1,0:T(8,128)(2,1)}), bf16[32,32,256]{2,1,0:T(8,128)(2,1)S(1)}, u32[]{:S(2)}, u32[]{:S(2)}) async-start(bf16[32,32,256]{2,1,0:T(8,128)(2,1)} %contract.1), calls=%async_computation.2 | async-start | bytes 1048576 | tf_op jit(solution)/shard_map/all_to_all | solution.py:352
  142.6 2.2 %copy-start.1 = (bf16[8,2048,128]{2,1,0:T(8,128)(2,1)S(1)}, bf16[8,2048,128]{2,1,0:T(8,128)(2,1)}, u32[]{:S(2)}) copy-start(bf16[8,2048,128]{2,1,0:T(8,128)(2,1)} %p3.1) | copy-start | bytes 12582916
  144.8 7.9 %copy-start.7 = (bf16[128,128]{1,0:T(8,128)(2,1)S(1)}, bf16[128,128]{1,0:T(8,128)(2,1)}, u32[]{:S(2)}) copy-start(bf16[128,128]{1,0:T(8,128)(2,1)} %w_ref.3) | copy-start | bytes 98308
  144.8 7.9 %copy-start.10 = (f32[128]{0:T(128)S(1)}, f32[128]{0:T(128)}, u32[]{:S(2)}) copy-start(f32[128]{0:T(128)} %param.17) | copy-start | bytes 1540
  144.8 7.9 %copy-start.11 = (f32[128]{0:T(128)S(1)}, f32[128]{0:T(128)}, u32[]{:S(2)}) copy-start(f32[128]{0:T(128)} %param.18) | copy-start | bytes 1540
